TPU v7x, 512 devices: a whole 4x4x16 slice. The times are simulated.
512 devices in a mesh: ctx: 32 (over x_lo, z), exp: 16 (over y, x_hi, core).
Axes of the slice: x: 4 (x_hi: 2, x_lo: 2; x = x_hi * 2 + x_lo), y: 4, z: 16, core: 2. Of those that a mesh axis runs over, the one named last changes fastest.
Arguments:
- queries: bfloat16 [32, 2048, 2048], P('exp', 'ctx'), may hold values from -128 to 128
- key_vectors: bfloat16 [32, 2048, 256], P('exp', 'ctx'), may hold values from -8 to 8
- value_vectors: bfloat16 [32, 2048, 256], P('exp', 'ctx'), may hold values from -4 to 4
- output_grad: bfloat16 [32, 2048, 2048], P('exp', 'ctx'), may hold values from -6 to 6
- doc_lengths: int32 [32, 8], P('exp'), may hold values from 1 to 1024, 2048 in all within a row
- expert_input: bfloat16 [65536, 2048], P(('ctx', 'exp')), may hold values from -6 to 6
- expert_grad: bfloat16 [65536, 2048], P(('ctx', 'exp')), may hold values from -6 to 6
- expert_pick: int32 [65536], P(('ctx', 'exp')), may hold values from 0 to 15, as said below
- gate_weight: float32 [65536], P(('ctx', 'exp')), may hold values from 0.1 to 1
- gate_matrix: bfloat16 [16, 2048, 384], P('exp', 'ctx'), may hold values from -0.125 to 0.125
- up_matrix: bfloat16 [16, 2048, 384], P('exp', 'ctx'), may hold values from -0.125 to 0.125
- down_matrix: bfloat16 [16, 384, 2048], P('exp', None, 'ctx'), may hold values from -0.3125 to 0.3125
Outputs:
- query_grad: bfloat16 [32, 2048, 2048], P('exp', 'ctx')
- key_grad: bfloat16 [32, 2048, 256], P('exp', 'ctx')
- value_grad: bfloat16 [32, 2048, 256], P('exp', 'ctx')
- input_grad: bfloat16 [65536, 2048], P(('ctx', 'exp'))
Inputs may be any that keep to these rules, and one draw needn't show every extreme that they name: `expert_pick`: one expert of this round lives on each index of exp. Among the rows of one device one expert, the same on every device and drawn from the seed, is picked by exactly 16 rows, and the other experts share the remaining rows evenly, within one row.
All inputs are finite; a program needn't handle non-finite values.
Results may differ from a plain program's by a relative error of at most 0.0057.
Values may be sent and summed in bfloat16 or wider, within the bound.
No kernel may reach another device: no remote copies, remote signals or barrier semaphores. Data moves between devices by JAX's collectives and lax.ppermute only.
A program may use at most 64 MiB of HBM per device.

v0:
```python
import math

import jax
import jax.numpy as jnp
from jax import lax
from jax.sharding import PartitionSpec as P

QUERY_HEADS = 16
KEY_VALUE_HEADS = 2
HEAD_WIDTH = 128


def document_ids(lengths, total_length):
    starts = jnp.cumsum(lengths) - lengths
    position = jnp.arange(total_length, dtype=jnp.int32)
    documents = jnp.sum((position[:, None] >= starts[None, :]).astype(jnp.int32), axis=1) - 1
    return (documents, starts)


def activation_grads(act_grad, gate_act, up_act):
    sigmoid_gate = jax.nn.sigmoid(gate_act)
    up_grad = (act_grad * gate_act * sigmoid_gate).astype(jnp.bfloat16)
    gate_grad = (act_grad * up_act * sigmoid_gate * (1.0 + gate_act * (1.0 - sigmoid_gate))).astype(
        jnp.bfloat16
    )
    return (gate_grad, up_grad)


def item_grads(query_item, key_item, value_item, grad_item, documents, block):
    total_length, head_size = query_item.shape
    count = total_length // block
    scale = 1.0 / math.sqrt(head_size)
    position = jnp.arange(block, dtype=jnp.int32)

    def tile_mask(query_start, key_start):
        query_docs = lax.dynamic_slice_in_dim(documents, query_start, block)
        key_docs = lax.dynamic_slice_in_dim(documents, key_start, block)
        causal = (key_start + position)[None, :] <= (query_start + position)[:, None]
        return causal & (key_docs[None, :] == query_docs[:, None])

    def tile_terms(query_tile, grad_tile, key_start, visible):
        key_tile = lax.dynamic_slice_in_dim(key_item, key_start, block)
        value_tile = lax.dynamic_slice_in_dim(value_item, key_start, block)
        scores = (
            jnp.einsum("qd,kd->qk", query_tile, key_tile, preferred_element_type=jnp.float32)
            * scale
        )
        scores = jnp.where(visible, scores, -1e30)
        dprobs = jnp.einsum("qd,kd->qk", grad_tile, value_tile, preferred_element_type=jnp.float32)
        return (scores, dprobs, key_tile)

    def query_step(query_block, carry):
        query_grads, key_grads, value_grads = carry
        query_start = query_block * block
        query_tile = lax.dynamic_slice_in_dim(query_item, query_start, block)
        grad_tile = lax.dynamic_slice_in_dim(grad_item, query_start, block)
        lowest = 0

        def stats_step(key_block, stats):
            highest, total, weighted = stats
            key_start = key_block * block
            visible = tile_mask(query_start, key_start)
            scores, dprobs, key_tile = tile_terms(query_tile, grad_tile, key_start, visible)
            new_high = jnp.maximum(highest, jnp.max(scores, axis=1))
            shrink = jnp.exp(highest - new_high)
            weights = jnp.where(visible, jnp.exp(scores - new_high[:, None]), 0.0)
            total = total * shrink + jnp.sum(weights, axis=1)
            weighted = weighted * shrink + jnp.sum(weights * dprobs, axis=1)
            return (new_high, total, weighted)

        zero_rows = jnp.zeros((block,), jnp.float32)
        start_stats = (jnp.full((block,), -1e30, jnp.float32), zero_rows, zero_rows)
        highest, total, weighted = lax.fori_loop(lowest, query_block + 1, stats_step, start_stats)
        delta = weighted / total
        log_total = highest + jnp.log(total)

        def grad_step(key_block, inner):
            query_acc, key_acc, value_acc = inner
            key_start = key_block * block
            visible = tile_mask(query_start, key_start)
            scores, dprobs, key_tile = tile_terms(query_tile, grad_tile, key_start, visible)
            probs = jnp.where(visible, jnp.exp(scores - log_total[:, None]), 0.0)
            dscores = (probs * (dprobs - delta[:, None])).astype(jnp.bfloat16)
            probs_low = probs.astype(jnp.bfloat16)
            query_acc = (
                query_acc + jnp.dot(dscores, key_tile, preferred_element_type=jnp.float32) * scale
            )
            key_piece = lax.dynamic_slice_in_dim(key_acc, key_start, block)
            key_piece = (
                key_piece
                + jnp.einsum("qk,qd->kd", dscores, query_tile, preferred_element_type=jnp.float32)
                * scale
            )
            value_piece = lax.dynamic_slice_in_dim(value_acc, key_start, block)
            value_piece = value_piece + jnp.einsum(
                "qk,qd->kd", probs_low, grad_tile, preferred_element_type=jnp.float32
            )
            key_acc = lax.dynamic_update_slice_in_dim(key_acc, key_piece, key_start, 0)
            value_acc = lax.dynamic_update_slice_in_dim(value_acc, value_piece, key_start, 0)
            return (query_acc, key_acc, value_acc)

        start_inner = (jnp.zeros((block, head_size), jnp.float32), key_grads, value_grads)
        query_acc, key_grads, value_grads = lax.fori_loop(
            lowest, query_block + 1, grad_step, start_inner
        )
        query_grads = lax.dynamic_update_slice_in_dim(
            query_grads, query_acc.astype(jnp.bfloat16), query_start, 0
        )
        return (query_grads, key_grads, value_grads)

    start_carry = (
        jnp.zeros((total_length, head_size), jnp.bfloat16),
        jnp.zeros((total_length, head_size), jnp.float32),
        jnp.zeros((total_length, head_size), jnp.float32),
    )
    return lax.fori_loop(0, count, query_step, start_carry)


def local(
    queries,
    key_vectors,
    value_vectors,
    output_grad,
    doc_lengths,
    expert_input,
    expert_grad,
    expert_pick,
    gate_weight,
    gate_matrix,
    up_matrix,
    down_matrix,
):
    groups, local_length, width = queries.shape
    heads = QUERY_HEADS
    head_size = HEAD_WIDTH
    key_head_rows = KEY_VALUE_HEADS
    group_share = heads // key_head_rows

    def to_items(array, count):
        return (
            array.reshape(groups, local_length, count, -1)
            .transpose(0, 2, 1, 3)
            .reshape(groups * count, local_length, -1)
        )

    query_items = to_items(queries, heads)
    grad_items = to_items(output_grad, heads)
    key_four = jnp.repeat(
        key_vectors.reshape(groups, local_length, key_head_rows, head_size), group_share, axis=2
    )
    value_four = jnp.repeat(
        value_vectors.reshape(groups, local_length, key_head_rows, head_size), group_share, axis=2
    )
    pair_items = (
        jnp.concatenate([key_four, value_four], axis=3)
        .transpose(0, 2, 1, 3)
        .reshape(groups * heads, local_length, 2 * head_size)
    )
    query_full, grad_full, pair_full = (
        lax.all_to_all(query_items, "ctx", split_axis=0, concat_axis=1, tiled=True),
        lax.all_to_all(grad_items, "ctx", split_axis=0, concat_axis=1, tiled=True),
        lax.all_to_all(pair_items, "ctx", split_axis=0, concat_axis=1, tiled=True),
    )
    per_device = query_full.shape[0]
    total_length = query_full.shape[1]
    block = min(512, total_length)
    first_item = lax.axis_index("ctx") * per_device

    def one_item(offset):
        sequence = (first_item + offset) // heads
        lengths = lax.dynamic_index_in_dim(doc_lengths, sequence, 0, keepdims=False)
        documents, starts = document_ids(lengths, total_length)
        query_item = lax.dynamic_index_in_dim(query_full, offset, 0, keepdims=False)
        grad_item = lax.dynamic_index_in_dim(grad_full, offset, 0, keepdims=False)
        pair_item = lax.dynamic_index_in_dim(pair_full, offset, 0, keepdims=False)
        return item_grads(
            query_item,
            pair_item[:, :head_size],
            pair_item[:, head_size:],
            grad_item,
            documents,
            block,
        )

    query_parts, key_portions, value_portions = lax.map(
        one_item, jnp.arange(per_device, dtype=jnp.int32)
    )
    pair_grads = jnp.concatenate([key_portions, value_portions], axis=2)
    query_back = lax.all_to_all(query_parts, "ctx", split_axis=1, concat_axis=0, tiled=True)
    pair_back = lax.all_to_all(pair_grads, "ctx", split_axis=1, concat_axis=0, tiled=True)
    query_grad = (
        query_back.reshape(groups, heads, local_length, head_size)
        .transpose(0, 2, 1, 3)
        .reshape(groups, local_length, heads * head_size)
    )
    summed = jnp.sum(
        pair_back.reshape(groups, key_head_rows, group_share, local_length, 2 * head_size), axis=2
    )
    key_grad = (
        summed[..., :head_size]
        .astype(jnp.bfloat16)
        .transpose(0, 2, 1, 3)
        .reshape(groups, local_length, key_head_rows * head_size)
    )
    value_grad = (
        summed[..., head_size:]
        .astype(jnp.bfloat16)
        .transpose(0, 2, 1, 3)
        .reshape(groups, local_length, key_head_rows * head_size)
    )
    tokens, model_width = expert_input.shape
    rounds = lax.axis_size("exp")
    capacity = 2 * tokens // rounds
    choose = (expert_pick[:, None] == jnp.arange(rounds, dtype=jnp.int32)[None, :]).astype(
        jnp.int32
    )
    before = jnp.cumsum(choose, axis=0) - choose
    rank = jnp.sum(before * choose, axis=1)
    slot = expert_pick * capacity + rank
    source = (
        jnp.zeros((rounds * capacity,), jnp.int32).at[slot].set(jnp.arange(tokens, dtype=jnp.int32))
    )
    filled = jnp.zeros((rounds * capacity,), jnp.bool_).at[slot].set(True)
    scaled_grad = (gate_weight[:, None] * expert_grad.astype(jnp.float32)).astype(jnp.bfloat16)
    nothing = jnp.zeros((), jnp.bfloat16)
    send_rows = jnp.where(filled[:, None], expert_input[source], nothing).reshape(
        rounds, capacity, model_width
    )
    send_grads = jnp.where(filled[:, None], scaled_grad[source], nothing).reshape(
        rounds, capacity, model_width
    )
    gate_whole, up_whole, down_whole = (
        lax.all_gather(gate_matrix, "ctx", axis=1, tiled=True),
        lax.all_gather(up_matrix, "ctx", axis=1, tiled=True),
        lax.all_gather(down_matrix, "ctx", axis=2, tiled=True),
    )
    gate_whole = gate_whole[0]
    up_whole = up_whole[0]
    down_whole = down_whole[0]
    rows = lax.all_to_all(send_rows, "exp", split_axis=0, concat_axis=0, tiled=True)
    grads = lax.all_to_all(send_grads, "exp", split_axis=0, concat_axis=0, tiled=True)
    flat_rows = rows.reshape(-1, model_width)
    flat_grads = grads.reshape(-1, model_width)
    gate_act = jnp.dot(flat_rows, gate_whole, preferred_element_type=jnp.float32)
    up_act = jnp.dot(flat_rows, up_whole, preferred_element_type=jnp.float32)
    act_grad = jnp.einsum("rd,fd->rf", flat_grads, down_whole, preferred_element_type=jnp.float32)
    gate_grad, up_grad = activation_grads(act_grad, gate_act, up_act)
    result = jnp.einsum("rf,df->rd", gate_grad, gate_whole, preferred_element_type=jnp.float32)
    result = result + jnp.einsum("rf,df->rd", up_grad, up_whole, preferred_element_type=jnp.float32)
    result = result.astype(jnp.bfloat16).reshape(rows.shape)
    returned = lax.all_to_all(result, "exp", split_axis=0, concat_axis=0, tiled=True)
    input_grad = returned.reshape(rounds * capacity, model_width)[slot]
    return (query_grad, key_grad, value_grad, input_grad)


def solution(mesh):
    placed = (
        P("exp", "ctx", None),
        P("exp", "ctx", None),
        P("exp", "ctx", None),
        P("exp", "ctx", None),
        P("exp", None),
        P(("ctx", "exp"), None),
        P(("ctx", "exp"), None),
        P(("ctx", "exp")),
        P(("ctx", "exp")),
        P("exp", "ctx", None),
        P("exp", "ctx", None),
        P("exp", None, "ctx"),
    )
    return jax.shard_map(
        local,
        mesh=mesh,
        in_specs=placed,
        out_specs=(
            P("exp", "ctx", None),
            P("exp", "ctx", None),
            P("exp", "ctx", None),
            P(("ctx", "exp"), None),
        ),
        check_vma=False,
    )
```

profile of v0, /device:TPU:24, one launch (start us, length us, event | category | flops | bytes accessed | tf_op | source)
XLA Modules:
  0.0 697.0 jit_solution(9761493406098044015)
XLA Ops:
  17.6 24.8 %all_to_all.60 = bf16[16,16,2048]{2,1,0:T(8,128)(2,1)S(1)} all-to-all(bf16[16,16,2048]{2,1,0:T(8,128)(2,1)S(1)} %get-tuple-element.774), channel_id=1, replica_groups=mesh['ctx'=32,'exp'=16] {'exp'}, dimensions={0} | all-to-all | bytes 2097152 | tf_op jit(solution)/shard_map/all_to_all | solution.py:240
  42.4 6.1 all-to-all-start.5
  49.6 16.7 %all-to-all-done.5 = bf16[16,16,2048]{2,1,0:T(8,128)(2,1)S(1)} async-done(((bf16[16,16,2048]{2,1,0:T(8,128)(2,1)}), bf16[16,16,2048]{2,1,0:T(8,128)(2,1)S(1)}, u32[]{:S(2)}, u32[]{:S(2)}) %all-to-all-start.5) | async-done | bytes 1048608 | tf_op jit(solution)/shard_map/all_to_all | solution.py:241
  66.3 11.3 %all-to-all-start = ((bf16[32,64,128]{2,1,0:T(8,128)(2,1)}), bf16[32,64,128]{2,1,0:T(8,128)(2,1)}, u32[]{:S(2)}, u32[]{:S(2)}) async-start(bf16[32,64,128]{2,1,0:T(8,128)(2,1)} %bitcast.1), calls=%async_computation | async-start | bytes 1048576 | tf_op jit(solution)/shard_map/all_to_all | solution.py:160
  79.8 31.3 %all-to-all-done = bf16[32,64,128]{2,1,0:T(8,128)(2,1)} async-done(((bf16[32,64,128]{2,1,0:T(8,128)(2,1)}), bf16[32,64,128]{2,1,0:T(8,128)(2,1)}, u32[]{:S(2)}, u32[]{:S(2)}) %all-to-all-start) | async-done | bytes 524320 | tf_op jit(solution)/shard_map/all_to_all | solution.py:160
  111.1 5.7 all-to-all-start.2
  119.0 51.2 %all-to-all-done.2 = bf16[32,64,256]{2,1,0:T(8,128)(2,1)S(1)} async-done(((bf16[32,64,256]{2,1,0:T(8,128)(2,1)}), bf16[32,64,256]{2,1,0:T(8,128)(2,1)S(1)}, u32[]{:S(2)}, u32[]{:S(2)}) %all-to-all-start.2) | async-done | bytes 1048608 | tf_op jit(solution)/shard_map/all_to_all | solution.py:162
  170.2 9.0 %all-to-all-start.1 = ((bf16[32,64,128]{2,1,0:T(8,128)(2,1)}), bf16[32,64,128]{2,1,0:T(8,128)(2,1)}, u32[]{:S(2)}, u32[]{:S(2)}) async-start(bf16[32,64,128]{2,1,0:T(8,128)(2,1)} %bitcast.4), calls=%async_computation.1 | async-start | bytes 1048576 | tf_op jit(solution)/shard_map/all_to_all | solution.py:161
  179.3 2.1 fusion.33
  181.4 123.2 %all-gather.4.cloned.1.call-done = bf16[1,384,2048]{1,2,0:T(8,128)(2,1)} async-done(((bf16[1,384,64]{1,2,0:T(8,128)(2,1)}), bf16[1,384,2048]{1,2,0:T(8,128)(2,1)}) %all-gather.4.cloned.1.call-update) | async-done | bytes 1572880 | tf_op jit(solution)/shard_map/all_gather | solution.py:235
  304.7 3.2 fusion.38
  307.8 124.6 %all-gather.6.cloned.1.call-done = bf16[1,2048,384]{2,1,0:T(8,128)(2,1)} async-done(((bf16[1,64,384]{2,1,0:T(8,128)(2,1)}), bf16[1,2048,384]{2,1,0:T(8,128)(2,1)}) %all-gather.6.cloned.1.call-update) | async-done | bytes 1572880 | tf_op jit(solution)/shard_map/all_gather | solution.py:234
  432.4 4.2 fusion.31
  436.7 4.0 fusion.30
  441.7 6.9 all-to-all-start.7
  449.7 84.1 %while.106 = (s32[]{:T(128)}, bf16[2048,128]{1,0:T(8,128)(2,1)}, f32[2048,128]{1,0:T(8,128)S(1)}, f32[2048,128]{1,0:T(8,128)S(1)}, bf16[2048,128]{1,0:T(8,128)(2...) while((s32[]{:T(128)}, bf16[2048,128]{1,0:T(8,128)(2,1)}, ...), condition=%wide.region_10.11_spmd.clone.clone, body=%wide.region_2.10_spmd.clone.clone.sunk | while | flops 478024192 | bytes 12176417 | solution.py:116
  450.7 3.1 while.107
  453.9 4.6 while.108
  460.2 6.2 while.107
  466.5 9.2 %while.108 = (s32[]{:T(128)}, f32[512,128]{1,0:T(8,128)S(1)}, f32[2048,128]{1,0:T(8,128)S(1)}, f32[2048,128]{1,0:T(8,128)S(1)}, s32[]{:T(128)}, /*index=5*/s32[5...) while((s32[]{:T(128)}, f32[512,128]{1,0:T(8,128)S(1)}, ...), condition=%wide.region_9.9_spmd.clone, body=%wide.region_8.8_spmd.clone.sunk | while | flops 338756608 | bytes 7231739 | solution.py:103
  477.4 9.3 %while.107 = (s32[]{:T(128)}, f32[512]{0:T(512)S(1)}, f32[512]{0:T(512)S(1)}, f32[512]{0:T(512)S(1)}, s32[]{:T(128)}, /*index=5*/s32[512]{0:T(512)S(1)}, s32[]{:...) while((s32[]{:T(128)}, f32[512]{0:T(512)S(1)}, ...), condition=%wide.region_7.7_spmd.clone, body=%wide.region_3.6_spmd.clone.sunk | while | flops 139201024 | bytes 3741919 | solution.py:73
  486.8 13.7 %while.108 = (s32[]{:T(128)}, f32[512,128]{1,0:T(8,128)S(1)}, f32[2048,128]{1,0:T(8,128)S(1)}, f32[2048,128]{1,0:T(8,128)S(1)}, s32[]{:T(128)}, /*index=5*/s32[5...) while((s32[]{:T(128)}, f32[512,128]{1,0:T(8,128)S(1)}, ...), condition=%wide.region_9.9_spmd.clone, body=%wide.region_8.8_spmd.clone.sunk | while | flops 338756608 | bytes 7231739 | solution.py:103
  502.3 12.4 %while.107 = (s32[]{:T(128)}, f32[512]{0:T(512)S(1)}, f32[512]{0:T(512)S(1)}, f32[512]{0:T(512)S(1)}, s32[]{:T(128)}, /*index=5*/s32[512]{0:T(512)S(1)}, s32[]{:...) while((s32[]{:T(128)}, f32[512]{0:T(512)S(1)}, ...), condition=%wide.region_7.7_spmd.clone, body=%wide.region_3.6_spmd.clone.sunk | while | flops 139201024 | bytes 3741919 | solution.py:73
  514.8 18.3 %while.108 = (s32[]{:T(128)}, f32[512,128]{1,0:T(8,128)S(1)}, f32[2048,128]{1,0:T(8,128)S(1)}, f32[2048,128]{1,0:T(8,128)S(1)}, s32[]{:T(128)}, /*index=5*/s32[5...) while((s32[]{:T(128)}, f32[512,128]{1,0:T(8,128)S(1)}, ...), condition=%wide.region_9.9_spmd.clone, body=%wide.region_8.8_spmd.clone.sunk | while | flops 338756608 | bytes 7231739 | solution.py:103
  533.8 2.6 copy.65
  536.9 12.6 %reduce = bf16[2048,128]{1,0:T(8,128)(2,1)S(1)} reduce(bf16[2048,1,128]{2,1,0:T(2,128)(2,1)} %bitcast.162, bf16[]{:T(256)} %broadcast.162), dimensions={1}, to_apply=%bitcast.126.reduce_sub_computation | reduce | bytes 1048578
  550.3 4.5 all-to-all-start.3
  554.8 3.0 pad_maximum_fusion
  557.9 28.2 %all-to-all-done.3 = bf16[32,2,4096]{2,1,0:T(2,128)(2,1)S(1)} async-done(((bf16[32,2,4096]{2,1,0:T(2,128)(2,1)}), bf16[32,2,4096]{2,1,0:T(2,128)(2,1)S(1)}, u32[]{:S(2)}, u32[]{:S(2)}) %all-to-all-start.3) | async-done | bytes 524320 | tf_op jit(solution)/shard_map/all_to_all | solution.py:189
  586.1 5.5 all-to-all-start.4
  591.6 3.6 gather_fusion.2
  599.2 87.4 %all-to-all-done.4 = f32[1,2048,256]{2,0,1:T(1,128)S(1)} async-done(((f32[1,2048,256]{2,0,1:T(1,128)}), f32[1,2048,256]{2,0,1:T(1,128)S(1)}, u32[]{:S(2)}, u32[]{:S(2)}) %all-to-all-start.4) | async-done | bytes 2097184 | tf_op jit(solution)/shard_map/all_to_all | solution.py:190
  (260 shorter events, 109.9 us)
Async XLA Ops:
  7.2 6.8 copy-start
  7.2 172.1 %all-gather.8.cloned.1.call-start = ((), (), s32[]{:S(2)}) async-start(), calls=%async_computation.10 | async-start | bytes 1622016 | tf_op jit(solution)/shard_map/all_gather | solution.py:233
  42.4 6.1 copy-start.5
  42.4 23.9 %all-to-all-start.5 = ((bf16[16,16,2048]{2,1,0:T(8,128)(2,1)}), bf16[16,16,2048]{2,1,0:T(8,128)(2,1)S(1)}, u32[]{:S(2)}, u32[]{:S(2)}) async-start(bf16[16,16,2048]{2,1,0:T(8,128)(2,1)} %get-tuple-element.775), calls=%async_computation.5 | async-start | bytes 2097152 | tf_op jit(solution)/shard_map/all_to_all | solution.py:241
  48.6 29.8 %copy-start.7 = (bf16[2,64,256]{2,1,0:T(8,128)(2,1)S(1)}, bf16[2,64,256]{2,1,0:T(8,128)(2,1)}, u32[]{:S(2)}) copy-start(bf16[2,64,256]{2,1,0:T(8,128)(2,1)} %param.19) | copy-start | bytes 196612
  48.6 29.8 %copy-start.8 = (bf16[2,64,256]{2,1,0:T(8,128)(2,1)S(1)}, bf16[2,64,256]{2,1,0:T(8,128)(2,1)}, u32[]{:S(2)}) copy-start(bf16[2,64,256]{2,1,0:T(8,128)(2,1)} %param.20) | copy-start | bytes 196612
  66.3 13.5 %copy-start.2 = (bf16[16,16,2048]{2,1,0:T(8,128)(2,1)}, bf16[16,16,2048]{2,1,0:T(8,128)(2,1)S(1)}, u32[]{:S(2)}) copy-start(bf16[16,16,2048]{2,1,0:T(8,128)(2,1)S(1)} %all-to-all-done.5) | copy-start | bytes 3145732
  66.3 44.8 %all-to-all-start = ((bf16[32,64,128]{2,1,0:T(8,128)(2,1)}), bf16[32,64,128]{2,1,0:T(8,128)(2,1)}, u32[]{:S(2)}, u32[]{:S(2)}) async-start(bf16[32,64,128]{2,1,0:T(8,128)(2,1)} %bitcast.1), calls=%async_computation | async-start | bytes 1048576 | tf_op jit(solution)/shard_map/all_to_all | solution.py:160
  77.7 227.0 %all-gather.4.cloned.1.call-start = ((), (), s32[]{:S(2)}) async-start(), calls=%async_computation.8 | async-start | bytes 1622016 | tf_op jit(solution)/shard_map/all_gather | solution.py:235
  79.8 37.8 %copy-start.9 = (s32[2,8]{1,0:T(2,128)S(1)}, s32[2,8]{1,0:T(2,128)}, u32[]{:S(2)}) copy-start(s32[2,8]{1,0:T(2,128)} %param.22) | copy-start | bytes 196
  79.8 38.0 %copy-start.6 = (bf16[2,64,2048]{2,1,0:T(8,128)(2,1)S(1)}, bf16[2,64,2048]{2,1,0:T(8,128)(2,1)}, u32[]{:S(2)}) copy-start(bf16[2,64,2048]{2,1,0:T(8,128)(2,1)} %param.21) | copy-start | bytes 1572868
  111.1 59.1 %all-to-all-start.2 = ((bf16[32,64,256]{2,1,0:T(8,128)(2,1)}), bf16[32,64,256]{2,1,0:T(8,128)(2,1)S(1)}, u32[]{:S(2)}, u32[]{:S(2)}) async-start(bf16[32,64,256]{2,1,0:T(8,128)(2,1)} %bitcast.159), calls=%async_computation.2 | async-start | bytes 2097152 | tf_op jit(solution)/shard_map/all_to_all | solution.py:162
  116.8 315.6 %all-gather.6.cloned.1.call-start = ((), (), s32[]{:S(2)}) async-start(), calls=%async_computation.9 | async-start | bytes 1622016 | tf_op jit(solution)/shard_map/all_gather | solution.py:234
  170.2 9.1 %copy-start.3 = (bf16[32,64,256]{2,1,0:T(8,128)(2,1)}, bf16[32,64,256]{2,1,0:T(8,128)(2,1)S(1)}, u32[]{:S(2)}) copy-start(bf16[32,64,256]{2,1,0:T(8,128)(2,1)S(1)} %all-to-all-done.2) | copy-start | bytes 3145732
  170.2 271.5 %all-to-all-start.1 = ((bf16[32,64,128]{2,1,0:T(8,128)(2,1)}), bf16[32,64,128]{2,1,0:T(8,128)(2,1)}, u32[]{:S(2)}, u32[]{:S(2)}) async-start(bf16[32,64,128]{2,1,0:T(8,128)(2,1)} %bitcast.4), calls=%async_computation.1 | async-start | bytes 1048576 | tf_op jit(solution)/shard_map/all_to_all | solution.py:161
  181.4 251.0 %copy-start.1 = (bf16[1,2048,384]{2,1,0:T(8,128)(2,1)S(1)}, bf16[1,2048,384]{2,1,0:T(8,128)(2,1)}, u32[]{:S(2)}) copy-start(bf16[1,2048,384]{2,1,0:T(8,128)(2,1)} %all-gather.8.cloned.1.call-done) | copy-start | bytes 4718596
  436.6 4.0 copy-start.4
  441.7 108.6 %all-to-all-start.7 = ((bf16[16,16,2048]{2,1,0:T(8,128)(2,1)}), bf16[16,16,2048]{2,1,0:T(8,128)(2,1)}, u32[]{:S(2)}, u32[]{:S(2)}) async-start(bf16[16,16,2048]{2,1,0:T(8,128)(2,1)} %bitcast.25), calls=%async_computation.7 | async-start | bytes 2097152 | tf_op jit(solution)/shard_map/all_to_all | solution.py:251
  550.3 35.7 %all-to-all-start.3 = ((bf16[32,2,4096]{2,1,0:T(2,128)(2,1)}), bf16[32,2,4096]{2,1,0:T(2,128)(2,1)S(1)}, u32[]{:S(2)}, u32[]{:S(2)}) async-start(bf16[32,2,4096]{2,1,0:T(2,128)(2,1)} %reshape.194), calls=%async_computation.3 | async-start | bytes 1048576 | tf_op jit(solution)/shard_map/all_to_all | solution.py:189
  586.1 100.5 %all-to-all-start.4 = ((f32[1,2048,256]{2,0,1:T(1,128)}), f32[1,2048,256]{2,0,1:T(1,128)S(1)}, u32[]{:S(2)}, u32[]{:S(2)}) async-start(f32[1,2048,256]{2,0,1:T(1,128)} %pad_maximum_fusion), calls=%async_computation.4 | async-start | bytes 4194304 | tf_op jit(solution)/shard_map/all_to_all | solution.py:190
Sparse Core Ops, SparseCore 0:
  10.1 155.4 all-gather.7
  167.7 136.9 all-gather.3
  306.7 125.6 all-gather.5
where the time goes:
time: 704 us; the launch traced here: 697 us
  waiting for transfers between devices  465 us (66%)
  matrix products  84.3 us (12%)
  starting transfers between devices  49.1 us (7%)
  other arithmetic  29.7 us (4%)
  local copies, waits for them, and re-layouts  29 us (4%)
  blocking collectives  24.8 us (4%)
  between operations  14.1 us (2%)
    all_gather x1, waiting for transfers between devices, local(): lax.all_gather(up_matrix, 'ctx', axis=1, tiled=True)  125 us
    all_gather x1, waiting for transfers between devices, local(): lax.all_gather(down_matrix, 'ctx', axis=2, tiled=True)  123 us
    all_to_all x1, waiting for transfers between devices, local(): lax.all_to_all(pair_grads, 'ctx', split_axis=1, concat_axis=0, tiled=True)  87.4 us
    all_to_all x1, waiting for transfers between devices, local(): lax.all_to_all(pair_items, 'ctx', split_axis=0, concat_axis=1, tiled=True)  51.2 us
    all_to_all x1, waiting for transfers between devices, local(): lax.all_to_all(query_items, 'ctx', split_axis=0, concat_axis=1, tiled=True)  31.3 us
    all_to_all x1, waiting for transfers between devices, local(): lax.all_to_all(query_parts, 'ctx', split_axis=1, concat_axis=0, tiled=True)  28.2 us
    dot_general x20, matrix products, tile_terms(): jnp.einsum('qd,kd->qk', query_tile, key_tile, preferred_element_type=jnp....  26.4 us
    dot_general x20, matrix products, tile_terms(): jnp.einsum('qd,kd->qk', grad_tile, value_tile, preferred_element_type=jnp...  25.5 us
  transfers between devices with their start and end apart: 10, of which 7 were waited for; matrix products, arithmetic and copies ran while one was open for 20% of the time, Pallas kernels for 0%

commit v1 on v0

v1 whole, which is shorter than its diff:
```python
import functools
import math

import jax
import jax.numpy as jnp
from jax import lax
from jax.experimental import pallas as pl
from jax.experimental.pallas import tpu as pltpu
from jax.sharding import PartitionSpec as P

HEADS = 16
KV_HEADS = 2
WIDTH = 128
SHARE = HEADS // KV_HEADS
BLOCK = 128
RING = 8
LANES = SHARE * BLOCK
MOST = 9
SCALE = 1.0 / math.sqrt(WIDTH)

X_PAIRS = [[z, 16 + z] for z in range(16)]
Z_LINES = [[x * 16 + z for z in range(16)] for x in range(2)]
QUADS = [[2 * j, 2 * j + 1, 16 + 2 * j, 16 + 2 * j + 1] for j in range(8)]
RINGS = [[x * 16 + 2 * j + p for j in range(8)] for x in range(2) for p in range(2)]


def z_shift(step):
    return [(x * 16 + z, x * 16 + (z + step) % 16) for x in range(2) for z in range(16)]


NT = (((1,), (1,)), ((), ()))
TN = (((0,), (0,)), ((), ()))


def attention_kernel(
    lengths_ref, place_ref, qg_ref, kv_ref, dq_ref, dkv_ref, q_rows, g_rows, prob, dprob, acc
):
    ring = place_ref[0]
    sequence = place_ref[1]
    starts = [jnp.int32(0)]
    for d in range(7):
        starts.append(starts[-1] + lengths_ref[sequence, d])
    acc[...] = jnp.zeros_like(acc)
    for half in range(2):
        query_block = ring + RING * half
        first = query_block * BLOCK
        rows = pl.ds(half * BLOCK, BLOCK)
        for h in range(SHARE):
            q_rows[h * BLOCK : (h + 1) * BLOCK, :] = qg_ref[rows, h * WIDTH : (h + 1) * WIDTH]
            g_rows[h * BLOCK : (h + 1) * BLOCK, :] = qg_ref[
                rows, (SHARE + h) * WIDTH : (SHARE + h + 1) * WIDTH
            ]
        lane = lax.broadcasted_iota(jnp.int32, (1, LANES), 1)
        position = first + lane % BLOCK
        begin = jnp.zeros((1, LANES), jnp.int32)
        low = jnp.int32(0)
        for start in starts:
            begin = jnp.where(position >= start, start, begin)
            low = jnp.where(first >= start, start, low)
        low_block = low // BLOCK
        count = query_block - low_block + 1

        def tile(i):
            block = low_block + i
            return (ring - block) & (RING - 1), pl.multiple_of((block // RING) * BLOCK, BLOCK), block

        def score_step(i, highest):
            slot, offset, block = tile(i)
            keys = kv_ref[slot, pl.ds(offset, BLOCK), 0:WIDTH]
            values = kv_ref[slot, pl.ds(offset, BLOCK), WIDTH : 2 * WIDTH]
            scores = (
                lax.dot_general(keys, q_rows[...], NT, preferred_element_type=jnp.float32) * SCALE
            )
            at = block * BLOCK + lax.broadcasted_iota(jnp.int32, (BLOCK, LANES), 0)
            scores = jnp.where((at >= begin) & (at <= position), scores, -1e30)
            prob[i] = scores
            dprob[i] = lax.dot_general(
                values, g_rows[...], NT, preferred_element_type=jnp.float32
            )
            return jnp.maximum(highest, jnp.max(scores, axis=0, keepdims=True))

        highest = lax.fori_loop(0, count, score_step, jnp.full((1, LANES), -1e30, jnp.float32))

        def sum_step(i, carry):
            total, weighted = carry
            weights = jnp.exp(prob[i] - highest)
            prob[i] = weights
            return (
                total + jnp.sum(weights, axis=0, keepdims=True),
                weighted + jnp.sum(weights * dprob[i], axis=0, keepdims=True),
            )

        zero = jnp.zeros((1, LANES), jnp.float32)
        total, weighted = lax.fori_loop(0, count, sum_step, (zero, zero))
        inverse = 1.0 / total
        delta = weighted * inverse

        def grad_step(i, query_acc):
            slot, offset, block = tile(i)
            keys = kv_ref[slot, pl.ds(offset, BLOCK), 0:WIDTH]
            probs = prob[i] * inverse
            dscores = (probs * (dprob[i] - delta)).astype(jnp.bfloat16)
            home = block & (RING - 1)
            acc[home, pl.ds(offset, BLOCK), 0:WIDTH] += (
                jnp.dot(dscores, q_rows[...], preferred_element_type=jnp.float32) * SCALE
            )
            acc[home, pl.ds(offset, BLOCK), WIDTH : 2 * WIDTH] += jnp.dot(
                probs.astype(jnp.bfloat16), g_rows[...], preferred_element_type=jnp.float32
            )
            return query_acc + lax.dot_general(
                keys, dscores, TN, preferred_element_type=jnp.float32
            )

        query_acc = lax.fori_loop(0, count, grad_step, jnp.zeros((WIDTH, LANES), jnp.float32))
        query_acc = (query_acc * SCALE).T.astype(jnp.bfloat16)
        for h in range(SHARE):
            dq_ref[rows, h * WIDTH : (h + 1) * WIDTH] = query_acc[h * BLOCK : (h + 1) * BLOCK, :]
    dkv_ref[...] = acc[...].astype(jnp.bfloat16)


def attention(lengths, place, qg, kv):
    vmem = pl.BlockSpec(memory_space=pltpu.VMEM)
    smem = pl.BlockSpec(memory_space=pltpu.SMEM)
    return pl.pallas_call(
        attention_kernel,
        out_shape=(
            jax.ShapeDtypeStruct((2 * BLOCK, SHARE * WIDTH), jnp.bfloat16),
            jax.ShapeDtypeStruct((RING, 2 * BLOCK, 2 * WIDTH), jnp.bfloat16),
        ),
        in_specs=[smem, smem, vmem, vmem],
        out_specs=(vmem, vmem),
        scratch_shapes=[
            pltpu.VMEM((LANES, WIDTH), jnp.bfloat16),
            pltpu.VMEM((LANES, WIDTH), jnp.bfloat16),
            pltpu.VMEM((MOST, BLOCK, LANES), jnp.float32),
            pltpu.VMEM((MOST, BLOCK, LANES), jnp.float32),
            pltpu.VMEM((RING, 2 * BLOCK, 2 * WIDTH), jnp.float32),
        ],
        compiler_params=pltpu.CompilerParams(vmem_limit_bytes=40 * 1024 * 1024),
        cost_estimate=pl.CostEstimate(
            flops=2_000_000_000, bytes_accessed=4_000_000, transcendentals=2_000_000
        ),
    )(lengths, place, qg, kv)


def expert_kernel(units, x_ref, w_ref, out_ref):
    depth = w_ref.shape[0] * w_ref.shape[2]
    model = 2 * depth
    weights = [w_ref[:, x].reshape(depth, 3 * units) for x in range(2)]

    def through(first, column):
        total = None
        for x in range(2):
            part = jnp.dot(
                x_ref[:, first + x * depth : first + (x + 1) * depth],
                weights[x][:, column * units : (column + 1) * units],
                preferred_element_type=jnp.float32,
            )
            total = part if total is None else total + part
        return total

    gate_act = through(0, 0)
    up_act = through(0, 1)
    act_grad = through(model, 2)
    sigmoid = jax.nn.sigmoid(gate_act)
    up_grad = (act_grad * gate_act * sigmoid).astype(jnp.bfloat16)
    gate_grad = (act_grad * up_act * sigmoid * (1.0 + gate_act * (1.0 - sigmoid))).astype(
        jnp.bfloat16
    )
    both = jnp.concatenate([gate_grad, up_grad], axis=1)
    for x in range(2):
        out_ref[:, x * depth : (x + 1) * depth] = lax.dot_general(
            both, weights[x][:, : 2 * units], NT, preferred_element_type=jnp.float32
        ).astype(jnp.bfloat16)


def experts(rows, weights):
    count, width = rows.shape
    units = weights.shape[-1] // 3
    vmem = pl.BlockSpec(memory_space=pltpu.VMEM)
    return pl.pallas_call(
        functools.partial(expert_kernel, units),
        out_shape=jax.ShapeDtypeStruct((count, width // 2), jnp.bfloat16),
        in_specs=[vmem, vmem],
        out_specs=vmem,
        compiler_params=pltpu.CompilerParams(vmem_limit_bytes=40 * 1024 * 1024),
        cost_estimate=pl.CostEstimate(
            flops=2_000_000_000, bytes_accessed=8_000_000, transcendentals=100_000
        ),
    )(rows, weights)


def local(
    queries,
    key_vectors,
    value_vectors,
    output_grad,
    doc_lengths,
    expert_input,
    expert_grad,
    expert_pick,
    gate_weight,
    gate_matrix,
    up_matrix,
    down_matrix,
):
    groups, length, width = queries.shape
    ctx = lax.axis_index("ctx")
    ring = (ctx % 16) // 2
    sequence = ctx // 16
    place = jnp.stack([ring, sequence]).astype(jnp.int32)

    shard = jnp.concatenate([gate_matrix[0], up_matrix[0], down_matrix[0].T], axis=1)
    pair = lax.all_gather(shard, "ctx", axis_index_groups=X_PAIRS)
    weights = lax.all_gather(pair, "ctx", axis_index_groups=Z_LINES)

    def to_quads(array):
        split = array.reshape(groups, length, KV_HEADS, -1).transpose(0, 2, 1, 3)
        return split.reshape(groups * KV_HEADS, length, -1)

    kv_send = jnp.concatenate([to_quads(key_vectors), to_quads(value_vectors)], axis=2)
    kv_own = lax.all_to_all(
        kv_send, "ctx", 0, 0, tiled=True, axis_index_groups=QUADS
    ).reshape(2 * BLOCK, 2 * WIDTH)
    qg_send = jnp.concatenate([to_quads(queries), to_quads(output_grad)], axis=2)
    qg = lax.all_to_all(qg_send, "ctx", 0, 0, tiled=True, axis_index_groups=QUADS).reshape(
        2 * BLOCK, -1
    )
    kv = [None] * RING
    kv[0] = up = down = kv_own
    for step in range(1, 5):
        up = lax.ppermute(up, "ctx", z_shift(2))
        kv[step] = up
        if step < 4:
            down = lax.ppermute(down, "ctx", z_shift(-2))
            kv[RING - step] = down

    tokens, model_width = expert_input.shape
    rounds = lax.axis_size("exp")
    capacity = 2 * tokens // rounds
    choose = (expert_pick[:, None] == jnp.arange(rounds, dtype=jnp.int32)[None, :]).astype(
        jnp.int32
    )
    before = jnp.cumsum(choose, axis=0) - choose
    rank = jnp.sum(before * choose, axis=1)
    slot = expert_pick * capacity + rank
    scaled_grad = (gate_weight[:, None] * expert_grad.astype(jnp.float32)).astype(jnp.bfloat16)
    both = jnp.concatenate([expert_input, scaled_grad], axis=1)
    pick = (
        slot[None, :] == jnp.arange(rounds * capacity, dtype=jnp.int32)[:, None]
    ).astype(jnp.bfloat16)
    send = jnp.dot(pick, both, preferred_element_type=jnp.float32).astype(jnp.bfloat16)
    rows = lax.all_to_all(
        send.reshape(rounds, capacity, 2 * model_width), "exp", 0, 0, tiled=True
    )

    dq, dkv = attention(doc_lengths, place, qg, jnp.stack(kv))

    result = experts(rows.reshape(rounds * capacity, 2 * model_width), weights)
    returned = lax.all_to_all(
        result.reshape(rounds, capacity, model_width), "exp", 0, 0, tiled=True
    )
    input_grad = jnp.dot(
        pick.T, returned.reshape(rounds * capacity, model_width), preferred_element_type=jnp.float32
    ).astype(jnp.bfloat16)

    dq_back = lax.all_to_all(
        dq.reshape(4, length, -1), "ctx", 0, 0, tiled=True, axis_index_groups=QUADS
    )
    query_grad = (
        dq_back.reshape(groups, KV_HEADS, length, -1).transpose(0, 2, 1, 3).reshape(queries.shape)
    )
    dkv_own = lax.psum_scatter(
        dkv.reshape(RING * 2 * BLOCK, 2 * WIDTH),
        "ctx",
        scatter_dimension=0,
        tiled=True,
        axis_index_groups=RINGS,
    )
    dkv_back = lax.all_to_all(
        dkv_own.reshape(4, length, 2 * WIDTH), "ctx", 0, 0, tiled=True, axis_index_groups=QUADS
    ).reshape(groups, KV_HEADS, length, 2 * WIDTH)
    key_grad = dkv_back[..., :WIDTH].transpose(0, 2, 1, 3).reshape(key_vectors.shape)
    value_grad = dkv_back[..., WIDTH:].transpose(0, 2, 1, 3).reshape(value_vectors.shape)
    return (query_grad, key_grad, value_grad, input_grad)


def solution(mesh):
    placed = (
        P("exp", "ctx", None),
        P("exp", "ctx", None),
        P("exp", "ctx", None),
        P("exp", "ctx", None),
        P("exp", None),
        P(("ctx", "exp"), None),
        P(("ctx", "exp"), None),
        P(("ctx", "exp")),
        P(("ctx", "exp")),
        P("exp", "ctx", None),
        P("exp", "ctx", None),
        P("exp", None, "ctx"),
    )
    return jax.shard_map(
        local,
        mesh=mesh,
        in_specs=placed,
        out_specs=(
            P("exp", "ctx", None),
            P("exp", "ctx", None),
            P("exp", "ctx", None),
            P(("ctx", "exp"), None),
        ),
        check_vma=False,
    )
```

time: 704 us -> 233 us (0.33)
  waiting for transfers between devices: 465 us -> 79.7 us
  matrix products: 84.3 us -> 1.84 us
  blocking collectives: 24.8 us -> 58.3 us
  other arithmetic: 29.7 us -> 2.51 us
  local copies, waits for them, and re-layouts: 29 us -> 7.59 us
  Pallas kernels: 0 us -> 14.7 us
    all_gather x3 -> x1, waiting for transfers between devices: 248 us -> 27.9 us  [local(): weights = lax.all_gather(pair, 'ctx', axis_index_groups=Z_LINES)]
    all_to_all x7 -> x4, waiting for transfers between devices: 215 us -> 16 us  [the longest x1 13.3 us: local(): lax.all_to_all(result.reshape(rounds, capacity, model_width), 'exp', 0, 0...]
    dot_general x74 -> x2, matrix products: 84.3 us -> 1.84 us  [the longest x1 1.15 us: local(): jnp.dot(pick.T, returned.reshape(rounds * capacity, model_width), preferr...]
    ppermute x0 -> x7, starting transfers between devices: none -> 30.9 us  [the longest x3 20 us: local(): down = lax.ppermute(down, 'ctx', z_shift(-2))]
    all_to_all x7 -> x4, starting transfers between devices: 49 us -> 18.3 us  [the longest x1 7.31 us: local(): lax.all_to_all(result.reshape(rounds, capacity, model_width), 'exp', 0, 0...]
    all_to_all x1 -> x2, blocking collectives: 24.8 us -> 52.2 us  [the longest x1 32.5 us: local(): lax.all_to_all(send.reshape(rounds, capacity, 2 * model_width), 'exp', 0,...]
    ppermute x0 -> x7, waiting for transfers between devices: none -> 26.8 us  [the longest x4 26.8 us: local(): up = lax.ppermute(up, 'ctx', z_shift(2))]
    pallas_call x0 -> x2, Pallas kernels: none -> 14.7 us  [the longest x1 11 us: attention(): pl.pallas_call(attention_kernel, out_shape=(jax.ShapeDtypeStruct((2 * BLO...]
  transfers between devices with their start and end apart: 10 -> 13, of which waited for: 7 -> 8; matrix products, arithmetic and copies ran while one was open for 20% -> 3% of each run, Pallas kernels for 0% -> 2%
where the time goes in v1:
time: 233 us; the launch traced here: 230 us
  waiting for transfers between devices  79.7 us (34%)
  blocking collectives  58.3 us (25%)
  starting transfers between devices  49.2 us (21%)
  between operations  15.9 us (7%)
  Pallas kernels  14.7 us (6%)
  local copies, waits for them, and re-layouts  7.59 us (3%)
  other arithmetic  2.51 us (1%)
    all_to_all x1, blocking collectives, local(): lax.all_to_all(send.reshape(rounds, capacity, 2 * model_width), 'exp', 0,...  32.5 us
    all_gather x1, waiting for transfers between devices, local(): weights = lax.all_gather(pair, 'ctx', axis_index_groups=Z_LINES)  27.9 us
    ppermute x4, waiting for transfers between devices, local(): up = lax.ppermute(up, 'ctx', z_shift(2))  26.8 us
    ppermute x3, starting transfers between devices, local(): down = lax.ppermute(down, 'ctx', z_shift(-2))  20 us
    all_to_all x1, blocking collectives, local(): lax.all_to_all(dq.reshape(4, length, -1), 'ctx', 0, 0, tiled=True, axis_i...  19.7 us
    all_to_all x1, waiting for transfers between devices, local(): lax.all_to_all(result.reshape(rounds, capacity, model_width), 'exp', 0, 0...  13.3 us
    pallas_call x1, Pallas kernels, attention(): pl.pallas_call(attention_kernel, out_shape=(jax.ShapeDtypeStruct((2 * BLO...  11 us
    ppermute x4, starting transfers between devices, local(): up = lax.ppermute(up, 'ctx', z_shift(2))  10.9 us
  transfers between devices with their start and end apart: 13, of which 8 were waited for; matrix products, arithmetic and copies ran while one was open for 3% of the time, Pallas kernels for 2%

profile of v1, /device:TPU:24, one launch (start us, length us, event | category | flops | bytes accessed | tf_op | source)
XLA Modules:
  0.0 229.7 jit_solution(16366093564321455716)
XLA Ops:
  8.0 0.8 fusion.9
  8.8 0.8 fusion.10
  10.3 4.1 %all-to-all-start.1 = ((bf16[4,64,256]{2,1,0:T(8,128)(2,1)}), bf16[4,64,256]{2,1,0:T(8,128)(2,1)S(1)}, u32[]{:S(2)}, u32[]{:S(2)}) async-start(bf16[4,64,256]{2,1,0:T(8,128)(2,1)} %pad_maximum_fusion.4), calls=%async_computation.1 | async-start | bytes 262144 | tf_op jit(solution)/shard_map/all_to_all | solution.py:222
  14.4 1.1 fusion.7
  15.6 1.1 pad_maximum_fusion
  16.7 2.7 %all-to-all-done.1 = bf16[4,64,256]{2,1,0:T(8,128)(2,1)S(1)} async-done(((bf16[4,64,256]{2,1,0:T(8,128)(2,1)}), bf16[4,64,256]{2,1,0:T(8,128)(2,1)S(1)}, u32[]{:S(2)}, u32[]{:S(2)}) %all-to-all-start.1) | async-done | bytes 131104 | tf_op jit(solution)/shard_map/all_to_all | solution.py:222
  19.5 3.5 %all-to-all-start = ((bf16[4,64,2048]{2,1,0:T(8,128)(2,1)}), bf16[4,64,2048]{2,1,0:T(8,128)(2,1)S(1)}, u32[]{:S(2)}, u32[]{:S(2)}) async-start(bf16[4,64,2048]{2,1,0:T(8,128)(2,1)} %pad_maximum_fusion), calls=%async_computation | async-start | bytes 2097152 | tf_op jit(solution)/shard_map/all_to_all | solution.py:226
  23.1 5.2 %collective-permute-start = (bf16[256,256]{1,0:T(8,128)(2,1)S(1)}, bf16[256,256]{1,0:T(8,128)(2,1)S(1)}, u32[]{:S(2)}, u32[]{:S(2)}) collective-permute-start(bf16[256,256]{1,0:T(8,128)(2,1)S(1)} %bitcast.66), channel_id=1, source_target_pairs={{0,32},{16,48},{32,64},{48,80},{64,96},{80,112},{96,128},{112,144}... | collective-permute-start | bytes 393224 | tf_op jit(solution)/shard_map/ppermute | solution.py:232
  28.3 7.8 %collective-permute-start.4 = (bf16[256,256]{1,0:T(8,128)(2,1)S(1)}, bf16[256,256]{1,0:T(8,128)(2,1)S(1)}, u32[]{:S(2)}, u32[]{:S(2)}) collective-permute-start(bf16[256,256]{1,0:T(8,128)(2,1)S(1)} %bitcast.67), channel_id=1, source_target_pairs={{0,224},{16,240},{32,0},{48,16},{64,32},{80,48},{96,64},{112,80},{... | collective-permute-start | bytes 393224 | tf_op jit(solution)/shard_map/ppermute | solution.py:235
  36.1 15.4 %collective-permute-done = bf16[256,256]{1,0:T(8,128)(2,1)S(1)} collective-permute-done((bf16[256,256]{1,0:T(8,128)(2,1)S(1)}, bf16[256,256]{1,0:T(8,128)(2,1)S(1)}, u32[]{:S(2)}, u32[]{:S(2)}) %collective-permute-start) | collective-permute-done | bytes 131104 | tf_op jit(solution)/shard_map/ppermute | solution.py:232
  51.5 1.9 collective-permute-start.1
  53.4 6.0 %collective-permute-start.5 = (bf16[256,256]{1,0:T(8,128)(2,1)S(1)}, bf16[256,256]{1,0:T(8,128)(2,1)S(1)}, u32[]{:S(2)}, u32[]{:S(2)}) collective-permute-start(bf16[256,256]{1,0:T(8,128)(2,1)S(1)} %collective-permute-done.4), channel_id=1, source_target_pairs={{0,224},{16,240},{32,0},{48,16},{64,32},{80,48},{96,64},{112,80},{... | collective-permute-start | bytes 393224 | tf_op jit(solution)/shard_map/ppermute | solution.py:235
  59.5 2.2 collective-permute-done.1
  61.7 1.9 collective-permute-start.2
  63.6 6.2 %collective-permute-start.6 = (bf16[256,256]{1,0:T(8,128)(2,1)S(1)}, bf16[256,256]{1,0:T(8,128)(2,1)S(1)}, u32[]{:S(2)}, u32[]{:S(2)}) collective-permute-start(bf16[256,256]{1,0:T(8,128)(2,1)S(1)} %collective-permute-done.5), channel_id=1, source_target_pairs={{0,224},{16,240},{32,0},{48,16},{64,32},{80,48},{96,64},{112,80},{... | collective-permute-start | bytes 393224 | tf_op jit(solution)/shard_map/ppermute | solution.py:235
  69.8 2.2 collective-permute-done.2
  72.1 1.9 collective-permute-start.3
  74.0 7.0 %collective-permute-done.3 = bf16[256,256]{1,0:T(8,128)(2,1)S(1)} collective-permute-done((bf16[256,256]{1,0:T(8,128)(2,1)S(1)}, bf16[256,256]{1,0:T(8,128)(2,1)S(1)}, u32[]{:S(2)}, u32[]{:S(2)}) %collective-permute-start.3) | collective-permute-done | bytes 131104 | tf_op jit(solution)/shard_map/ppermute | solution.py:232
  81.2 11.0 %shard_map.147 = (bf16[256,1024]{1,0:T(8,128)(2,1)S(1)}, bf16[8,256,256]{2,1,0:T(8,128)(2,1)}) custom-call(s32[2,8]{1,0:T(2,128)S(1)} %copy-done.1, s32[2]{0:T(128)S(1)} %pad_add_fusion.place_ref, bf16[256,2048]{1,0:T(8,128)(2,1)S(1)} %bitcast.57, bf16[8,256,256]{2,1,0:T(8,128)(2,1)S(1)} %bitcast_dynamic-update-slice_fusion.kv_ref), custom_call_target="tpu_custom_call" | custom-call | flops 2000000000 | bytes 4000000 | tf_op jit(solution)/shard_map/pallas_call | solution.py:124
  92.3 6.1 %all-gather = bf16[128,1152]{1,0:T(8,128)(2,1)} all-gather(bf16[64,1152]{1,0:T(8,128)(2,1)S(1)} %pad_maximum_fusion.3), channel_id=2, replica_groups={{0,256},{16,272},{32,288},{48,304},{64,320},{80,336},{96,352},{112,368}..., dimensions={0}, use_global_device_ids=true | all-gather | bytes 442368 | tf_op jit(solution)/shard_map/all_gather | solution.py:214
  99.0 0.7 convolution_convert_fusion
  99.7 32.5 %all_to_all.30 = bf16[16,16,4096]{2,1,0:T(8,128)(2,1)S(1)} all-to-all(bf16[16,16,4096]{2,1,0:T(8,128)(2,1)S(1)} %bitcast.59), channel_id=1, replica_groups=mesh['ctx'=32,'exp'=16] {'exp'}, dimensions={0} | all-to-all | bytes 4194304 | tf_op jit(solution)/shard_map/all_to_all | solution.py:253
  132.3 19.7 %all_to_all.31 = bf16[4,64,1024]{2,1,0:T(8,128)(2,1)S(1)} all-to-all(bf16[4,64,1024]{2,1,0:T(8,128)(2,1)S(1)} %bitcast.58), channel_id=1, replica_groups={{0,16,256,272},{32,48,288,304},{64,80,320,336},{96,112,352,368},{128,14..., dimensions={0} | all-to-all | bytes 1048576 | tf_op jit(solution)/shard_map/all_to_all | solution.py:267
  151.9 8.8 %reduce-scatter.2.cloned.1.call-done = bf16[256,256]{1,0:T(8,128)(2,1)} async-done(((bf16[2048,256]{1,0:T(8,128)(2,1)}), bf16[256,256]{1,0:T(8,128)(2,1)}) %reduce-scatter.2.cloned.1.call-update) | async-done | bytes 131088 | tf_op jit(solution)/shard_map/reduce_scatter | solution.py:273
  160.8 3.3 %all-to-all-start.3 = ((bf16[4,64,256]{2,1,0:T(8,128)(2,1)}), bf16[4,64,256]{2,1,0:T(8,128)(2,1)S(1)}, u32[]{:S(2)}, u32[]{:S(2)}) async-start(bf16[4,64,256]{2,1,0:T(8,128)(2,1)} %bitcast.72), calls=%async_computation.4 | async-start | bytes 262144 | tf_op jit(solution)/shard_map/all_to_all | solution.py:280
  164.1 27.9 %all-gather.4.cloned.1.call-done = bf16[32,64,1152]{2,1,0:T(8,128)(2,1)} async-done(((bf16[2,64,1152]{2,1,0:T(8,128)(2,1)}), bf16[32,64,1152]{2,1,0:T(8,128)(2,1)}) %all-gather.4.cloned.1.call-update) | async-done | bytes 4718608 | tf_op jit(solution)/shard_map/all_gather | solution.py:215
  192.0 2.3 %copy-done = bf16[32,64,1152]{2,1,0:T(8,128)(2,1)S(1)} copy-done((bf16[32,64,1152]{2,1,0:T(8,128)(2,1)S(1)}, bf16[32,64,1152]{2,1,0:T(8,128)(2,1)}, u32[]{:S(2)}) %copy-start) | copy-done | bytes 4718616
  194.4 3.7 %shard_map.148 = bf16[256,2048]{1,0:T(8,128)(2,1)} custom-call(bf16[256,4096]{1,0:T(8,128)(2,1)S(1)} %bitcast.55, bf16[16,2,64,1152]{3,2,1,0:T(8,128)(2,1)S(1)} %bitcast.56), custom_call_target="tpu_custom_call" | custom-call | flops 2000000000 | bytes 8000000 | tf_op jit(solution)/shard_map/pallas_call | solution.py:181
  198.1 7.3 %all-to-all-start.5 = ((bf16[16,16,2048]{2,1,0:T(8,128)(2,1)}), bf16[16,16,2048]{2,1,0:T(8,128)(2,1)S(1)}, u32[]{:S(2)}, u32[]{:S(2)}) async-start(bf16[16,16,2048]{2,1,0:T(8,128)(2,1)} %bitcast.32), calls=%async_computation.6 | async-start | bytes 2097152 | tf_op jit(solution)/shard_map/all_to_all | solution.py:260
  206.0 1.2 reshape.77
  207.8 13.3 %all-to-all-done.5 = bf16[16,16,2048]{2,1,0:T(8,128)(2,1)S(1)} async-done(((bf16[16,16,2048]{2,1,0:T(8,128)(2,1)}), bf16[16,16,2048]{2,1,0:T(8,128)(2,1)S(1)}, u32[]{:S(2)}, u32[]{:S(2)}) %all-to-all-start.5) | async-done | bytes 1048608 | tf_op jit(solution)/shard_map/all_to_all | solution.py:260
  221.1 1.1 convolution_convert_fusion.1
  (52 shorter events, 3.0 us)
Async XLA Ops:
  8.0 7.5 %copy-start.2 = (bf16[2,64,2048]{2,1,0:T(8,128)(2,1)S(1)}, bf16[2,64,2048]{2,1,0:T(8,128)(2,1)}, u32[]{:S(2)}) copy-start(bf16[2,64,2048]{2,1,0:T(8,128)(2,1)} %param.15) | copy-start | bytes 1572868
  10.3 9.1 %all-to-all-start.1 = ((bf16[4,64,256]{2,1,0:T(8,128)(2,1)}), bf16[4,64,256]{2,1,0:T(8,128)(2,1)S(1)}, u32[]{:S(2)}, u32[]{:S(2)}) async-start(bf16[4,64,256]{2,1,0:T(8,128)(2,1)} %pad_maximum_fusion.4), calls=%async_computation.1 | async-start | bytes 262144 | tf_op jit(solution)/shard_map/all_to_all | solution.py:222
  16.7 64.4 %copy-start.1 = (s32[2,8]{1,0:T(2,128)S(1)}, s32[2,8]{1,0:T(2,128)}, u32[]{:S(2)}) copy-start(s32[2,8]{1,0:T(2,128)} %lengths_ref.1) | copy-start | bytes 196
  19.5 61.7 %all-to-all-start = ((bf16[4,64,2048]{2,1,0:T(8,128)(2,1)}), bf16[4,64,2048]{2,1,0:T(8,128)(2,1)S(1)}, u32[]{:S(2)}, u32[]{:S(2)}) async-start(bf16[4,64,2048]{2,1,0:T(8,128)(2,1)} %pad_maximum_fusion), calls=%async_computation | async-start | bytes 2097152 | tf_op jit(solution)/shard_map/all_to_all | solution.py:226
  23.0 137.8 %reduce-scatter.2.cloned.1.call-start = ((), (), s32[]{:S(2)}) async-start(), calls=%async_computation.7 | async-start | bytes 1179648 | tf_op jit(solution)/shard_map/reduce_scatter | solution.py:273
  23.1 28.4 %collective-permute-start = (bf16[256,256]{1,0:T(8,128)(2,1)S(1)}, bf16[256,256]{1,0:T(8,128)(2,1)S(1)}, u32[]{:S(2)}, u32[]{:S(2)}) collective-permute-start(bf16[256,256]{1,0:T(8,128)(2,1)S(1)} %bitcast.66), channel_id=1, source_target_pairs={{0,32},{16,48},{32,64},{48,80},{64,96},{80,112},{96,128},{112,144}... | collective-permute-start | bytes 393224 | tf_op jit(solution)/shard_map/ppermute | solution.py:232
  28.3 25.2 %collective-permute-start.4 = (bf16[256,256]{1,0:T(8,128)(2,1)S(1)}, bf16[256,256]{1,0:T(8,128)(2,1)S(1)}, u32[]{:S(2)}, u32[]{:S(2)}) collective-permute-start(bf16[256,256]{1,0:T(8,128)(2,1)S(1)} %bitcast.67), channel_id=1, source_target_pairs={{0,224},{16,240},{32,0},{48,16},{64,32},{80,48},{96,64},{112,80},{... | collective-permute-start | bytes 393224 | tf_op jit(solution)/shard_map/ppermute | solution.py:235
  51.5 10.2 %collective-permute-start.1 = (bf16[256,256]{1,0:T(8,128)(2,1)S(1)}, bf16[256,256]{1,0:T(8,128)(2,1)S(1)}, u32[]{:S(2)}, u32[]{:S(2)}) collective-permute-start(bf16[256,256]{1,0:T(8,128)(2,1)S(1)} %collective-permute-done), channel_id=1, source_target_pairs={{0,32},{16,48},{32,64},{48,80},{64,96},{80,112},{96,128},{112,144}... | collective-permute-start | bytes 393224 | tf_op jit(solution)/shard_map/ppermute | solution.py:232
  53.4 10.2 %collective-permute-start.5 = (bf16[256,256]{1,0:T(8,128)(2,1)S(1)}, bf16[256,256]{1,0:T(8,128)(2,1)S(1)}, u32[]{:S(2)}, u32[]{:S(2)}) collective-permute-start(bf16[256,256]{1,0:T(8,128)(2,1)S(1)} %collective-permute-done.4), channel_id=1, source_target_pairs={{0,224},{16,240},{32,0},{48,16},{64,32},{80,48},{96,64},{112,80},{... | collective-permute-start | bytes 393224 | tf_op jit(solution)/shard_map/ppermute | solution.py:235
  61.7 10.4 %collective-permute-start.2 = (bf16[256,256]{1,0:T(8,128)(2,1)S(1)}, bf16[256,256]{1,0:T(8,128)(2,1)S(1)}, u32[]{:S(2)}, u32[]{:S(2)}) collective-permute-start(bf16[256,256]{1,0:T(8,128)(2,1)S(1)} %collective-permute-done.1), channel_id=1, source_target_pairs={{0,32},{16,48},{32,64},{48,80},{64,96},{80,112},{96,128},{112,144}... | collective-permute-start | bytes 393224 | tf_op jit(solution)/shard_map/ppermute | solution.py:232
  63.6 17.4 %collective-permute-start.6 = (bf16[256,256]{1,0:T(8,128)(2,1)S(1)}, bf16[256,256]{1,0:T(8,128)(2,1)S(1)}, u32[]{:S(2)}, u32[]{:S(2)}) collective-permute-start(bf16[256,256]{1,0:T(8,128)(2,1)S(1)} %collective-permute-done.5), channel_id=1, source_target_pairs={{0,224},{16,240},{32,0},{48,16},{64,32},{80,48},{96,64},{112,80},{... | collective-permute-start | bytes 393224 | tf_op jit(solution)/shard_map/ppermute | solution.py:235
  72.1 9.0 %collective-permute-start.3 = (bf16[256,256]{1,0:T(8,128)(2,1)S(1)}, bf16[256,256]{1,0:T(8,128)(2,1)S(1)}, u32[]{:S(2)}, u32[]{:S(2)}) collective-permute-start(bf16[256,256]{1,0:T(8,128)(2,1)S(1)} %collective-permute-done.2), channel_id=1, source_target_pairs={{0,32},{16,48},{32,64},{48,80},{64,96},{80,112},{96,128},{112,144}... | collective-permute-start | bytes 393224 | tf_op jit(solution)/shard_map/ppermute | solution.py:232
  81.1 11.1 %copy-start.5 = (bf16[1,384,64]{1,2,0:T(8,128)(2,1)S(1)}, bf16[1,384,64]{1,2,0:T(8,128)(2,1)}, u32[]{:S(2)}) copy-start(bf16[1,384,64]{1,2,0:T(8,128)(2,1)} %param.23) | copy-start | bytes 147460
  81.1 11.1 %copy-start.6 = (bf16[1,64,384]{2,1,0:T(8,128)(2,1)S(1)}, bf16[1,64,384]{2,1,0:T(8,128)(2,1)}, u32[]{:S(2)}) copy-start(bf16[1,64,384]{2,1,0:T(8,128)(2,1)} %param.22) | copy-start | bytes 147460
  81.2 11.1 %copy-start.7 = (bf16[1,64,384]{2,1,0:T(8,128)(2,1)S(1)}, bf16[1,64,384]{2,1,0:T(8,128)(2,1)}, u32[]{:S(2)}) copy-start(bf16[1,64,384]{2,1,0:T(8,128)(2,1)} %param.21) | copy-start | bytes 147460
  92.2 6.2 %copy-start.8 = (s32[128]{0:T(128)S(1)}, s32[128]{0:T(128)}, u32[]{:S(2)}) copy-start(s32[128]{0:T(128)} %param.19) | copy-start | bytes 1540
  92.2 6.7 %copy-start.3 = (bf16[128,2048]{1,0:T(8,128)(2,1)S(1)}, bf16[128,2048]{1,0:T(8,128)(2,1)}, u32[]{:S(2)}) copy-start(bf16[128,2048]{1,0:T(8,128)(2,1)} %param.18) | copy-start | bytes 1572868
  92.2 6.7 %copy-start.9 = (f32[128]{0:T(128)S(1)}, f32[128]{0:T(128)}, u32[]{:S(2)}) copy-start(f32[128]{0:T(128)} %param.20) | copy-start | bytes 1540
  92.2 6.9 %copy-start.4 = (bf16[128,2048]{1,0:T(8,128)(2,1)S(1)}, bf16[128,2048]{1,0:T(8,128)(2,1)}, u32[]{:S(2)}) copy-start(bf16[128,2048]{1,0:T(8,128)(2,1)} %param.17) | copy-start | bytes 1572868
  92.2 99.9 %all-gather.4.cloned.1.call-start = ((), (), s32[]{:S(2)}) async-start(), calls=%async_computation.8 | async-start | bytes 5013504 | tf_op jit(solution)/shard_map/all_gather | solution.py:215
  160.8 37.3 %all-to-all-start.3 = ((bf16[4,64,256]{2,1,0:T(8,128)(2,1)}), bf16[4,64,256]{2,1,0:T(8,128)(2,1)S(1)}, u32[]{:S(2)}, u32[]{:S(2)}) async-start(bf16[4,64,256]{2,1,0:T(8,128)(2,1)} %bitcast.72), calls=%async_computation.4 | async-start | bytes 262144 | tf_op jit(solution)/shard_map/all_to_all | solution.py:280
  192.0 2.3 %copy-start = (bf16[32,64,1152]{2,1,0:T(8,128)(2,1)S(1)}, bf16[32,64,1152]{2,1,0:T(8,128)(2,1)}, u32[]{:S(2)}) copy-start(bf16[32,64,1152]{2,1,0:T(8,128)(2,1)} %all-gather.4.cloned.1.call-done) | copy-start | bytes 14155780
  198.1 23.0 %all-to-all-start.5 = ((bf16[16,16,2048]{2,1,0:T(8,128)(2,1)}), bf16[16,16,2048]{2,1,0:T(8,128)(2,1)S(1)}, u32[]{:S(2)}, u32[]{:S(2)}) async-start(bf16[16,16,2048]{2,1,0:T(8,128)(2,1)} %bitcast.32), calls=%async_computation.6 | async-start | bytes 2097152 | tf_op jit(solution)/shard_map/all_to_all | solution.py:260
Sparse Core Ops, SparseCore 0:
  92.3 68.4 reduce-scatter.1
Sparse Core Ops, SparseCore 1:
  98.5 93.5 all-gather.3

commit v2 on v1

--- a/solution.py
+++ b/solution.py
@@ -138,7 +138,7 @@
         ],
         compiler_params=pltpu.CompilerParams(vmem_limit_bytes=40 * 1024 * 1024),
         cost_estimate=pl.CostEstimate(
-            flops=2_000_000_000, bytes_accessed=4_000_000, transcendentals=2_000_000
+            flops=1_000_000, bytes_accessed=10_000, transcendentals=0
         ),
     )(lengths, place, qg, kv)
 
@@ -212,20 +212,20 @@
 
     shard = jnp.concatenate([gate_matrix[0], up_matrix[0], down_matrix[0].T], axis=1)
     pair = lax.all_gather(shard, "ctx", axis_index_groups=X_PAIRS)
-    weights = lax.all_gather(pair, "ctx", axis_index_groups=Z_LINES)
 
     def to_quads(array):
         split = array.reshape(groups, length, KV_HEADS, -1).transpose(0, 2, 1, 3)
         return split.reshape(groups * KV_HEADS, length, -1)
 
-    kv_send = jnp.concatenate([to_quads(key_vectors), to_quads(value_vectors)], axis=2)
-    kv_own = lax.all_to_all(
-        kv_send, "ctx", 0, 0, tiled=True, axis_index_groups=QUADS
-    ).reshape(2 * BLOCK, 2 * WIDTH)
-    qg_send = jnp.concatenate([to_quads(queries), to_quads(output_grad)], axis=2)
-    qg = lax.all_to_all(qg_send, "ctx", 0, 0, tiled=True, axis_index_groups=QUADS).reshape(
-        2 * BLOCK, -1
-    )
+    quad_send = jnp.concatenate(
+        [to_quads(a) for a in (key_vectors, value_vectors, queries, output_grad)], axis=2
+    )
+    pair, quad_send = lax.optimization_barrier((pair, quad_send))
+    weights = lax.all_gather(pair, "ctx", axis_index_groups=Z_LINES)
+    quad = lax.all_to_all(
+        quad_send, "ctx", 0, 0, tiled=True, axis_index_groups=QUADS
+    ).reshape(2 * BLOCK, -1)
+    kv_own, qg = quad[:, : 2 * WIDTH], quad[:, 2 * WIDTH :]
     kv = [None] * RING
     kv[0] = up = down = kv_own
     for step in range(1, 5):
@@ -254,8 +254,13 @@
         send.reshape(rounds, capacity, 2 * model_width), "exp", 0, 0, tiled=True
     )
 
+    *kv, rows = lax.optimization_barrier((*kv, rows))
     dq, dkv = attention(doc_lengths, place, qg, jnp.stack(kv))
 
+    dq_back = lax.all_to_all(
+        dq.reshape(4, length, -1), "ctx", 0, 0, tiled=True, axis_index_groups=QUADS
+    )
+    dq_back, rows = lax.optimization_barrier((dq_back, rows))
     result = experts(rows.reshape(rounds * capacity, 2 * model_width), weights)
     returned = lax.all_to_all(
         result.reshape(rounds, capacity, model_width), "exp", 0, 0, tiled=True
@@ -264,9 +269,6 @@
         pick.T, returned.reshape(rounds * capacity, model_width), preferred_element_type=jnp.float32
     ).astype(jnp.bfloat16)
 
-    dq_back = lax.all_to_all(
-        dq.reshape(4, length, -1), "ctx", 0, 0, tiled=True, axis_index_groups=QUADS
-    )
     query_grad = (
         dq_back.reshape(groups, KV_HEADS, length, -1).transpose(0, 2, 1, 3).reshape(queries.shape)
     )
@@ -277,6 +279,7 @@
         tiled=True,
         axis_index_groups=RINGS,
     )
+    dkv_own, input_grad = lax.optimization_barrier((dkv_own, input_grad))
     dkv_back = lax.all_to_all(
         dkv_own.reshape(4, length, 2 * WIDTH), "ctx", 0, 0, tiled=True, axis_index_groups=QUADS
     ).reshape(groups, KV_HEADS, length, 2 * WIDTH)

time: 233 us -> 200 us (0.86)
  blocking collectives: 58.3 us -> 28.5 us
  waiting for transfers between devices: 79.7 us -> 70.6 us
  local copies, waits for them, and re-layouts: 7.59 us -> 13.7 us
  starting transfers between devices: 49.2 us -> 52.3 us
  Pallas kernels: 14.7 us -> 11.8 us
    all_to_all x2 -> x1, blocking collectives: 52.2 us -> 22.1 us  [local(): lax.all_to_all(result.reshape(rounds, capacity, model_width), 'exp', 0, 0...]
    all_gather x1, waiting for transfers between devices: 27.9 us -> 0.01 us  [local(): weights = lax.all_gather(pair, 'ctx', axis_index_groups=Z_LINES)]
    reduce_scatter x1, waiting for transfers between devices: 8.84 us -> 19.4 us  [local(): lax.psum_scatter(dkv.reshape(RING * 2 * BLOCK, 2 * WIDTH), 'ctx', scatter...]
    unnamed x28 -> x34, local copies, waits for them, and re-layouts: 2.48 us -> 8.8 us
    all_to_all x1, waiting for transfers between devices: 0.01 us -> 3.26 us  [local(): lax.all_to_all(dkv_own.reshape(4, length, 2 * WIDTH), 'ctx', 0, 0, tiled=...]
    ppermute x3, starting transfers between devices: 20 us -> 23.2 us  [local(): down = lax.ppermute(down, 'ctx', z_shift(-2))]
    ppermute x4, waiting for transfers between devices: 26.8 us -> 30 us  [local(): up = lax.ppermute(up, 'ctx', z_shift(2))]
  transfers between devices with their start and end apart: 13 -> 13, of which waited for: 8 -> 8; matrix products, arithmetic and copies ran while one was open for 3% -> 6% of each run, Pallas kernels for 2% -> 6%
where the time goes in v2:
time: 200 us; the launch traced here: 199 us
  waiting for transfers between devices  70.6 us (35%)
  starting transfers between devices  52.3 us (26%)
  blocking collectives  28.5 us (14%)
  between operations  15.9 us (8%)
  local copies, waits for them, and re-layouts  13.7 us (7%)
  Pallas kernels  11.8 us (6%)
  matrix products  3.21 us (2%)
  other arithmetic  2.8 us (1%)
    ppermute x4, waiting for transfers between devices, local(): up = lax.ppermute(up, 'ctx', z_shift(2))  30 us
    ppermute x3, starting transfers between devices, local(): down = lax.ppermute(down, 'ctx', z_shift(-2))  23.2 us
    all_to_all x1, blocking collectives, local(): lax.all_to_all(result.reshape(rounds, capacity, model_width), 'exp', 0, 0...  22.1 us
    reduce_scatter x1, waiting for transfers between devices, local(): lax.psum_scatter(dkv.reshape(RING * 2 * BLOCK, 2 * WIDTH), 'ctx', scatter...  19.4 us
    all_to_all x1, waiting for transfers between devices, local(): lax.all_to_all(quad_send, 'ctx', 0, 0, tiled=True, axis_index_groups=QUADS)  11.5 us
    ppermute x4, starting transfers between devices, local(): up = lax.ppermute(up, 'ctx', z_shift(2))  10.9 us
    pallas_call x1, Pallas kernels, attention(): pl.pallas_call(attention_kernel, out_shape=(jax.ShapeDtypeStruct((2 * BLO...  9.11 us
    unnamed x34, local copies, waits for them, and re-layouts  8.8 us
  transfers between devices with their start and end apart: 13, of which 8 were waited for; matrix products, arithmetic and copies ran while one was open for 6% of the time, Pallas kernels for 6%

profile of v2, /device:TPU:24, one launch (start us, length us, event | category | flops | bytes accessed | tf_op | source)
XLA Modules:
  0.0 198.8 jit_solution(17024326320937060357)
XLA Ops:
  9.0 6.4 %all-gather = bf16[128,1152]{1,0:T(8,128)(2,1)} all-gather(bf16[64,1152]{1,0:T(8,128)(2,1)S(1)} %pad_maximum_fusion.3), channel_id=2, replica_groups={{0,256},{16,272},{32,288},{48,304},{64,320},{80,336},{96,352},{112,368}..., dimensions={0}, use_global_device_ids=true | all-gather | bytes 442368 | tf_op jit(solution)/shard_map/all_gather | solution.py:214
  15.4 1.1 fusion.8
  16.7 1.1 pad_maximum_fusion
  17.9 4.3 %all-to-all-start = ((bf16[4,64,2304]{2,1,0:T(8,128)(2,1)}), bf16[4,64,2304]{2,1,0:T(8,128)(2,1)S(1)}, u32[]{:S(2)}, u32[]{:S(2)}) async-start(bf16[4,64,2304]{2,1,0:T(8,128)(2,1)} %pad_maximum_fusion), calls=%async_computation | async-start | bytes 2359296 | tf_op jit(solution)/shard_map/all_to_all | solution.py:225
  22.8 2.1 %convolution_convert_fusion = bf16[256,4096]{1,0:T(8,128)(2,1)} fusion(bf16[128,2048]{1,0:T(8,128)(2,1)S(1)} %multiply_convert_fusion, bf16[128,2048]{1,0:T(8,128)(2,1)S(1)} %copy-done.7, s32[128]{0:T(128)S(1)} %multiply_add_fusion), kind=kOutput, calls=%fused_computation | convolution fusion | flops 271613952 | bytes 3146240 | tf_op jit(solution)/shard_map/dot_general | solution.py:252
  24.8 11.5 %all-to-all-done = bf16[4,64,2304]{2,1,0:T(8,128)(2,1)S(1)} async-done(((bf16[4,64,2304]{2,1,0:T(8,128)(2,1)}), bf16[4,64,2304]{2,1,0:T(8,128)(2,1)S(1)}, u32[]{:S(2)}, u32[]{:S(2)}) %all-to-all-start) | async-done | bytes 1179680 | tf_op jit(solution)/shard_map/all_to_all | solution.py:225
  36.3 7.0 %all-to-all-start.1 = ((bf16[16,16,4096]{2,1,0:T(8,128)(2,1)}), bf16[16,16,4096]{2,1,0:T(8,128)(2,1)S(1)}, u32[]{:S(2)}, u32[]{:S(2)}) async-start(bf16[16,16,4096]{2,1,0:T(8,128)(2,1)} %bitcast.58), calls=%async_computation.1 | async-start | bytes 4194304 | tf_op jit(solution)/shard_map/all_to_all | solution.py:253
  43.3 5.2 %collective-permute-start = (bf16[256,256]{1,0:T(8,128)(2,1)S(1)}, bf16[256,256]{1,0:T(8,128)(2,1)S(1)}, u32[]{:S(2)}, u32[]{:S(2)}) collective-permute-start(bf16[256,256]{1,0:T(8,128)(2,1)S(1)} %slice.49), channel_id=1, source_target_pairs={{0,32},{16,48},{32,64},{48,80},{64,96},{80,112},{96,128},{112,144}... | collective-permute-start | bytes 393224 | tf_op jit(solution)/shard_map/ppermute | solution.py:232
  48.5 11.2 %collective-permute-start.4 = (bf16[256,256]{1,0:T(8,128)(2,1)S(1)}, bf16[256,256]{1,0:T(8,128)(2,1)S(1)}, u32[]{:S(2)}, u32[]{:S(2)}) collective-permute-start(bf16[256,256]{1,0:T(8,128)(2,1)S(1)} %slice.49), channel_id=1, source_target_pairs={{0,224},{16,240},{32,0},{48,16},{64,32},{80,48},{96,64},{112,80},{... | collective-permute-start | bytes 393224 | tf_op jit(solution)/shard_map/ppermute | solution.py:235
  59.7 7.2 %collective-permute-done = bf16[256,256]{1,0:T(8,128)(2,1)S(1)} collective-permute-done((bf16[256,256]{1,0:T(8,128)(2,1)S(1)}, bf16[256,256]{1,0:T(8,128)(2,1)S(1)}, u32[]{:S(2)}, u32[]{:S(2)}) %collective-permute-start) | collective-permute-done | bytes 131104 | tf_op jit(solution)/shard_map/ppermute | solution.py:232
  66.9 1.9 collective-permute-start.1
  68.9 6.0 %collective-permute-start.5 = (bf16[256,256]{1,0:T(8,128)(2,1)S(1)}, bf16[256,256]{1,0:T(8,128)(2,1)}, u32[]{:S(2)}, u32[]{:S(2)}) collective-permute-start(bf16[256,256]{1,0:T(8,128)(2,1)S(1)} %collective-permute-done.4), channel_id=1, source_target_pairs={{0,224},{16,240},{32,0},{48,16},{64,32},{80,48},{96,64},{112,80},{... | collective-permute-start | bytes 393224 | tf_op jit(solution)/shard_map/ppermute | solution.py:235
  74.9 6.8 %collective-permute-done.1 = bf16[256,256]{1,0:T(8,128)(2,1)S(1)} collective-permute-done((bf16[256,256]{1,0:T(8,128)(2,1)S(1)}, bf16[256,256]{1,0:T(8,128)(2,1)S(1)}, u32[]{:S(2)}, u32[]{:S(2)}) %collective-permute-start.1) | collective-permute-done | bytes 131104 | tf_op jit(solution)/shard_map/ppermute | solution.py:232
  81.7 1.9 collective-permute-start.2
  83.6 6.0 %collective-permute-start.6 = (bf16[256,256]{1,0:T(8,128)(2,1)}, bf16[256,256]{1,0:T(8,128)(2,1)}, u32[]{:S(2)}, u32[]{:S(2)}) collective-permute-start(bf16[256,256]{1,0:T(8,128)(2,1)} %collective-permute-done.5), channel_id=1, source_target_pairs={{0,224},{16,240},{32,0},{48,16},{64,32},{80,48},{96,64},{112,80},{... | collective-permute-start | bytes 393224 | tf_op jit(solution)/shard_map/ppermute | solution.py:235
  89.7 5.8 %collective-permute-done.2 = bf16[256,256]{1,0:T(8,128)(2,1)} collective-permute-done((bf16[256,256]{1,0:T(8,128)(2,1)S(1)}, bf16[256,256]{1,0:T(8,128)(2,1)}, u32[]{:S(2)}, u32[]{:S(2)}) %collective-permute-start.2) | collective-permute-done | bytes 131104 | tf_op jit(solution)/shard_map/ppermute | solution.py:232
  95.4 1.9 collective-permute-start.3
  97.5 1.3 slice.48.qg_ref
  98.8 10.2 %collective-permute-done.3 = bf16[256,256]{1,0:T(8,128)(2,1)} collective-permute-done((bf16[256,256]{1,0:T(8,128)(2,1)}, bf16[256,256]{1,0:T(8,128)(2,1)}, u32[]{:S(2)}, u32[]{:S(2)}) %collective-permute-start.3) | collective-permute-done | bytes 131104 | tf_op jit(solution)/shard_map/ppermute | solution.py:232
  109.1 0.9 bitcast_dynamic-update-slice_fusion.5
  113.7 9.1 %shard_map.147 = (bf16[256,1024]{1,0:T(8,128)(2,1)S(1)}, bf16[8,256,256]{2,1,0:T(8,128)(2,1)S(1)}) custom-call(s32[2,8]{1,0:T(2,128)S(1)} %copy-done.3, s32[2]{0:T(128)S(1)} %pad_add_fusion.place_ref, bf16[256,2048]{1,0:T(8,128)(2,1)S(1)} %slice.48.qg_ref, bf16[8,256,256]{2,1,0:T(8,128)(2,1)S(1)} %bitcast_dynamic-update-slice_fusion.kv_ref), custom_call_target="tpu_custom_call" | custom-call | flops 1000000 | bytes 10000 | tf_op jit(solution)/shard_map/pallas_call | solution.py:124
  122.8 1.0 copy-done.1
  124.6 3.5 %all-to-all-start.2 = ((bf16[4,64,1024]{2,1,0:T(8,128)(2,1)}), bf16[4,64,1024]{2,1,0:T(8,128)(2,1)S(1)}, u32[]{:S(2)}, u32[]{:S(2)}) async-start(bf16[4,64,1024]{2,1,0:T(8,128)(2,1)} %bitcast.57), calls=%async_computation.2 | async-start | bytes 1048576 | tf_op jit(solution)/shard_map/all_to_all | solution.py:260
  128.7 6.0 %all-to-all-done.2 = bf16[4,64,1024]{2,1,0:T(8,128)(2,1)S(1)} async-done(((bf16[4,64,1024]{2,1,0:T(8,128)(2,1)}), bf16[4,64,1024]{2,1,0:T(8,128)(2,1)S(1)}, u32[]{:S(2)}, u32[]{:S(2)}) %all-to-all-start.2) | async-done | bytes 524320 | tf_op jit(solution)/shard_map/all_to_all | solution.py:260
  134.7 2.3 %copy-done = bf16[32,64,1152]{2,1,0:T(8,128)(2,1)S(1)} copy-done((bf16[32,64,1152]{2,1,0:T(8,128)(2,1)S(1)}, bf16[32,64,1152]{2,1,0:T(8,128)(2,1)}, u32[]{:S(2)}) %copy-start) | copy-done | bytes 4718616
  137.0 2.7 %shard_map.148 = bf16[256,2048]{1,0:T(8,128)(2,1)S(1)} custom-call(bf16[256,4096]{1,0:T(8,128)(2,1)S(1)} %bitcast.53, bf16[16,2,64,1152]{3,2,1,0:T(8,128)(2,1)S(1)} %bitcast.54), custom_call_target="tpu_custom_call" | custom-call | flops 2000000000 | bytes 8000000 | tf_op jit(solution)/shard_map/pallas_call | solution.py:181
  139.7 22.1 %all_to_all.25 = bf16[16,16,2048]{2,1,0:T(8,128)(2,1)S(1)} all-to-all(bf16[16,16,2048]{2,1,0:T(8,128)(2,1)S(1)} %bitcast.55), channel_id=1, replica_groups=mesh['ctx'=32,'exp'=16] {'exp'}, dimensions={0} | all-to-all | bytes 2097152 | tf_op jit(solution)/shard_map/all_to_all | solution.py:265
  161.8 1.1 convolution_convert_fusion.1
  163.0 19.4 %reduce-scatter.2.cloned.1.call-done = bf16[256,256]{1,0:T(8,128)(2,1)} async-done(((bf16[2048,256]{1,0:T(8,128)(2,1)}), bf16[256,256]{1,0:T(8,128)(2,1)}) %reduce-scatter.2.cloned.1.call-update) | async-done | bytes 131088 | tf_op jit(solution)/shard_map/reduce_scatter | solution.py:275
  182.3 3.3 %all-to-all-start.4 = ((bf16[4,64,256]{2,1,0:T(8,128)(2,1)}), bf16[4,64,256]{2,1,0:T(8,128)(2,1)S(1)}, u32[]{:S(2)}, u32[]{:S(2)}) async-start(bf16[4,64,256]{2,1,0:T(8,128)(2,1)} %bitcast.70), calls=%async_computation.5 | async-start | bytes 262144 | tf_op jit(solution)/shard_map/all_to_all | solution.py:283
  186.2 1.2 reshape.74
  187.4 3.3 %all-to-all-done.4 = bf16[4,64,256]{2,1,0:T(8,128)(2,1)S(1)} async-done(((bf16[4,64,256]{2,1,0:T(8,128)(2,1)}), bf16[4,64,256]{2,1,0:T(8,128)(2,1)S(1)}, u32[]{:S(2)}, u32[]{:S(2)}) %all-to-all-start.4) | async-done | bytes 131104 | tf_op jit(solution)/shard_map/all_to_all | solution.py:283
  (58 shorter events, 8.1 us)
Async XLA Ops:
  8.0 8.4 %copy-start.5 = (bf16[2,64,2048]{2,1,0:T(8,128)(2,1)S(1)}, bf16[2,64,2048]{2,1,0:T(8,128)(2,1)}, u32[]{:S(2)}) copy-start(bf16[2,64,2048]{2,1,0:T(8,128)(2,1)} %param.12) | copy-start | bytes 1572868
  8.0 8.5 %copy-start.9 = (bf16[2,64,256]{2,1,0:T(8,128)(2,1)S(1)}, bf16[2,64,256]{2,1,0:T(8,128)(2,1)}, u32[]{:S(2)}) copy-start(bf16[2,64,256]{2,1,0:T(8,128)(2,1)} %param.14) | copy-start | bytes 196612
  8.0 8.5 %copy-start.10 = (bf16[2,64,256]{2,1,0:T(8,128)(2,1)S(1)}, bf16[2,64,256]{2,1,0:T(8,128)(2,1)}, u32[]{:S(2)}) copy-start(bf16[2,64,256]{2,1,0:T(8,128)(2,1)} %param.13) | copy-start | bytes 196612
  8.0 126.6 %all-gather.4.cloned.1.call-start = ((), (), s32[]{:S(2)}) async-start(), calls=%async_computation.7 | async-start | bytes 5013504 | tf_op jit(solution)/shard_map/all_gather | solution.py:224
  16.7 5.5 %copy-start.11 = (s32[128]{0:T(128)S(1)}, s32[128]{0:T(128)}, u32[]{:S(2)}) copy-start(s32[128]{0:T(128)} %param.19) | copy-start | bytes 1540
  16.7 5.9 %copy-start.6 = (bf16[128,2048]{1,0:T(8,128)(2,1)S(1)}, bf16[128,2048]{1,0:T(8,128)(2,1)}, u32[]{:S(2)}) copy-start(bf16[128,2048]{1,0:T(8,128)(2,1)} %param.18) | copy-start | bytes 1572868
  16.7 5.9 %copy-start.12 = (f32[128]{0:T(128)S(1)}, f32[128]{0:T(128)}, u32[]{:S(2)}) copy-start(f32[128]{0:T(128)} %param.20) | copy-start | bytes 1540
  17.8 4.9 %copy-start.7 = (bf16[128,2048]{1,0:T(8,128)(2,1)S(1)}, bf16[128,2048]{1,0:T(8,128)(2,1)}, u32[]{:S(2)}) copy-start(bf16[128,2048]{1,0:T(8,128)(2,1)} %param.17) | copy-start | bytes 1572868
  17.9 18.4 %all-to-all-start = ((bf16[4,64,2304]{2,1,0:T(8,128)(2,1)}), bf16[4,64,2304]{2,1,0:T(8,128)(2,1)S(1)}, u32[]{:S(2)}, u32[]{:S(2)}) async-start(bf16[4,64,2304]{2,1,0:T(8,128)(2,1)} %pad_maximum_fusion), calls=%async_computation | async-start | bytes 2359296 | tf_op jit(solution)/shard_map/all_to_all | solution.py:225
  36.3 7.0 %copy-start.4 = (bf16[4,64,2304]{2,1,0:T(8,128)(2,1)}, bf16[4,64,2304]{2,1,0:T(8,128)(2,1)S(1)}, u32[]{:S(2)}) copy-start(bf16[4,64,2304]{2,1,0:T(8,128)(2,1)S(1)} %all-to-all-done) | copy-start | bytes 3538948
  36.3 62.5 %all-to-all-start.1 = ((bf16[16,16,4096]{2,1,0:T(8,128)(2,1)}), bf16[16,16,4096]{2,1,0:T(8,128)(2,1)S(1)}, u32[]{:S(2)}, u32[]{:S(2)}) async-start(bf16[16,16,4096]{2,1,0:T(8,128)(2,1)} %bitcast.58), calls=%async_computation.1 | async-start | bytes 4194304 | tf_op jit(solution)/shard_map/all_to_all | solution.py:253
  43.3 23.6 %collective-permute-start = (bf16[256,256]{1,0:T(8,128)(2,1)S(1)}, bf16[256,256]{1,0:T(8,128)(2,1)S(1)}, u32[]{:S(2)}, u32[]{:S(2)}) collective-permute-start(bf16[256,256]{1,0:T(8,128)(2,1)S(1)} %slice.49), channel_id=1, source_target_pairs={{0,32},{16,48},{32,64},{48,80},{64,96},{80,112},{96,128},{112,144}... | collective-permute-start | bytes 393224 | tf_op jit(solution)/shard_map/ppermute | solution.py:232
  48.5 20.3 %collective-permute-start.4 = (bf16[256,256]{1,0:T(8,128)(2,1)S(1)}, bf16[256,256]{1,0:T(8,128)(2,1)S(1)}, u32[]{:S(2)}, u32[]{:S(2)}) collective-permute-start(bf16[256,256]{1,0:T(8,128)(2,1)S(1)} %slice.49), channel_id=1, source_target_pairs={{0,224},{16,240},{32,0},{48,16},{64,32},{80,48},{96,64},{112,80},{... | collective-permute-start | bytes 393224 | tf_op jit(solution)/shard_map/ppermute | solution.py:235
  66.9 14.8 %collective-permute-start.1 = (bf16[256,256]{1,0:T(8,128)(2,1)S(1)}, bf16[256,256]{1,0:T(8,128)(2,1)S(1)}, u32[]{:S(2)}, u32[]{:S(2)}) collective-permute-start(bf16[256,256]{1,0:T(8,128)(2,1)S(1)} %collective-permute-done), channel_id=1, source_target_pairs={{0,32},{16,48},{32,64},{48,80},{64,96},{80,112},{96,128},{112,144}... | collective-permute-start | bytes 393224 | tf_op jit(solution)/shard_map/ppermute | solution.py:232
  68.9 14.8 %collective-permute-start.5 = (bf16[256,256]{1,0:T(8,128)(2,1)S(1)}, bf16[256,256]{1,0:T(8,128)(2,1)}, u32[]{:S(2)}, u32[]{:S(2)}) collective-permute-start(bf16[256,256]{1,0:T(8,128)(2,1)S(1)} %collective-permute-done.4), channel_id=1, source_target_pairs={{0,224},{16,240},{32,0},{48,16},{64,32},{80,48},{96,64},{112,80},{... | collective-permute-start | bytes 393224 | tf_op jit(solution)/shard_map/ppermute | solution.py:235
  81.7 15.7 %copy-start.8 = (bf16[256,256]{1,0:T(8,128)(2,1)}, bf16[256,256]{1,0:T(8,128)(2,1)S(1)}, u32[]{:S(2)}) copy-start(bf16[256,256]{1,0:T(8,128)(2,1)S(1)} %collective-permute-done.1) | copy-start | bytes 393220
  81.7 13.7 %collective-permute-start.2 = (bf16[256,256]{1,0:T(8,128)(2,1)S(1)}, bf16[256,256]{1,0:T(8,128)(2,1)}, u32[]{:S(2)}, u32[]{:S(2)}) collective-permute-start(bf16[256,256]{1,0:T(8,128)(2,1)S(1)} %collective-permute-done.1), channel_id=1, source_target_pairs={{0,32},{16,48},{32,64},{48,80},{64,96},{80,112},{96,128},{112,144}... | collective-permute-start | bytes 393224 | tf_op jit(solution)/shard_map/ppermute | solution.py:232
  83.6 15.2 %collective-permute-start.6 = (bf16[256,256]{1,0:T(8,128)(2,1)}, bf16[256,256]{1,0:T(8,128)(2,1)}, u32[]{:S(2)}, u32[]{:S(2)}) collective-permute-start(bf16[256,256]{1,0:T(8,128)(2,1)} %collective-permute-done.5), channel_id=1, source_target_pairs={{0,224},{16,240},{32,0},{48,16},{64,32},{80,48},{96,64},{112,80},{... | collective-permute-start | bytes 393224 | tf_op jit(solution)/shard_map/ppermute | solution.py:235
  95.4 13.6 %collective-permute-start.3 = (bf16[256,256]{1,0:T(8,128)(2,1)}, bf16[256,256]{1,0:T(8,128)(2,1)}, u32[]{:S(2)}, u32[]{:S(2)}) collective-permute-start(bf16[256,256]{1,0:T(8,128)(2,1)} %collective-permute-done.2), channel_id=1, source_target_pairs={{0,32},{16,48},{32,64},{48,80},{64,96},{80,112},{96,128},{112,144}... | collective-permute-start | bytes 393224 | tf_op jit(solution)/shard_map/ppermute | solution.py:232
  97.5 16.2 %copy-start.3 = (s32[2,8]{1,0:T(2,128)S(1)}, s32[2,8]{1,0:T(2,128)}, u32[]{:S(2)}) copy-start(s32[2,8]{1,0:T(2,128)} %lengths_ref.1) | copy-start | bytes 196
  122.8 1.0 copy-start.1
  123.8 0.8 copy-start.2
  124.6 10.0 %all-to-all-start.2 = ((bf16[4,64,1024]{2,1,0:T(8,128)(2,1)}), bf16[4,64,1024]{2,1,0:T(8,128)(2,1)S(1)}, u32[]{:S(2)}, u32[]{:S(2)}) async-start(bf16[4,64,1024]{2,1,0:T(8,128)(2,1)} %bitcast.57), calls=%async_computation.2 | async-start | bytes 1048576 | tf_op jit(solution)/shard_map/all_to_all | solution.py:260
  128.1 54.2 %reduce-scatter.2.cloned.1.call-start = ((), (), s32[]{:S(2)}) async-start(), calls=%async_computation.6 | async-start | bytes 1179648 | tf_op jit(solution)/shard_map/reduce_scatter | solution.py:275
  134.7 2.3 %copy-start = (bf16[32,64,1152]{2,1,0:T(8,128)(2,1)S(1)}, bf16[32,64,1152]{2,1,0:T(8,128)(2,1)}, u32[]{:S(2)}) copy-start(bf16[32,64,1152]{2,1,0:T(8,128)(2,1)} %all-gather.4.cloned.1.call-done) | copy-start | bytes 14155780
  182.3 8.3 %all-to-all-start.4 = ((bf16[4,64,256]{2,1,0:T(8,128)(2,1)}), bf16[4,64,256]{2,1,0:T(8,128)(2,1)S(1)}, u32[]{:S(2)}, u32[]{:S(2)}) async-start(bf16[4,64,256]{2,1,0:T(8,128)(2,1)} %bitcast.70), calls=%async_computation.5 | async-start | bytes 262144 | tf_op jit(solution)/shard_map/all_to_all | solution.py:283
Sparse Core Ops, SparseCore 0:
  18.0 102.6 all-gather.3
Sparse Core Ops, SparseCore 1:
  131.4 50.9 reduce-scatter.1

commit v3 on v2

--- a/solution.py
+++ b/solution.py
@@ -16,11 +16,13 @@
 RING = 8
 LANES = SHARE * BLOCK
 MOST = 9
+PIECE = 64
 SCALE = 1.0 / math.sqrt(WIDTH)
 
 X_PAIRS = [[z, 16 + z] for z in range(16)]
 Z_LINES = [[x * 16 + z for z in range(16)] for x in range(2)]
 QUADS = [[2 * j, 2 * j + 1, 16 + 2 * j, 16 + 2 * j + 1] for j in range(8)]
+PLANES = [[(x * 16 + z) * 16 + e for x in range(2) for e in range(16)] for z in range(16)]
 RINGS = [[x * 16 + 2 * j + p for j in range(8)] for x in range(2) for p in range(2)]
 
 
@@ -28,15 +30,28 @@
     return [(x * 16 + z, x * 16 + (z + step) % 16) for x in range(2) for z in range(16)]
 
 
+def member_swap(step):
+    return [
+        (x * 16 + z, (x ^ (step // 2)) * 16 + (z ^ (step % 2))) for x in range(2) for z in range(16)
+    ]
+
+
 NT = (((1,), (1,)), ((), ()))
 TN = (((0,), (0,)), ((), ()))
 
 
 def attention_kernel(
-    lengths_ref, place_ref, qg_ref, kv_ref, dq_ref, dkv_ref, q_rows, g_rows, prob, dprob, acc
+    lengths_ref, place_ref, qg_ref, *refs
 ):
+    kv_refs = refs[: RING - 1]
+    dq_refs = refs[RING - 1 : RING + 3]
+    dkv_ref, kv_ref, q_rows, g_rows, prob, dprob, acc, dq_all = refs[RING + 3 :]
+    kv_ref[0] = qg_ref[:, : 2 * WIDTH]
+    for slot in range(1, RING):
+        kv_ref[slot] = kv_refs[slot - 1][...]
     ring = place_ref[0]
     sequence = place_ref[1]
+    member = place_ref[2]
     starts = [jnp.int32(0)]
     for d in range(7):
         starts.append(starts[-1] + lengths_ref[sequence, d])
@@ -46,9 +61,11 @@
         first = query_block * BLOCK
         rows = pl.ds(half * BLOCK, BLOCK)
         for h in range(SHARE):
-            q_rows[h * BLOCK : (h + 1) * BLOCK, :] = qg_ref[rows, h * WIDTH : (h + 1) * WIDTH]
+            q_rows[h * BLOCK : (h + 1) * BLOCK, :] = qg_ref[
+                rows, (2 + h) * WIDTH : (3 + h) * WIDTH
+            ]
             g_rows[h * BLOCK : (h + 1) * BLOCK, :] = qg_ref[
-                rows, (SHARE + h) * WIDTH : (SHARE + h + 1) * WIDTH
+                rows, (2 + SHARE + h) * WIDTH : (3 + SHARE + h) * WIDTH
             ]
         lane = lax.broadcasted_iota(jnp.int32, (1, LANES), 1)
         position = first + lane % BLOCK
@@ -114,7 +131,13 @@
         query_acc = lax.fori_loop(0, count, grad_step, jnp.zeros((WIDTH, LANES), jnp.float32))
         query_acc = (query_acc * SCALE).T.astype(jnp.bfloat16)
         for h in range(SHARE):
-            dq_ref[rows, h * WIDTH : (h + 1) * WIDTH] = query_acc[h * BLOCK : (h + 1) * BLOCK, :]
+            for part in range(2):
+                first_row = h * BLOCK + part * PIECE
+                dq_all[2 * half + part, :, h * WIDTH : (h + 1) * WIDTH] = query_acc[
+                    first_row : first_row + PIECE, :
+                ]
+    for step in range(4):
+        dq_refs[step][...] = dq_all[member ^ step]
     dkv_ref[...] = acc[...].astype(jnp.bfloat16)
 
 
@@ -124,35 +147,75 @@
     return pl.pallas_call(
         attention_kernel,
         out_shape=(
-            jax.ShapeDtypeStruct((2 * BLOCK, SHARE * WIDTH), jnp.bfloat16),
+            *[jax.ShapeDtypeStruct((PIECE, SHARE * WIDTH), jnp.bfloat16)] * 4,
             jax.ShapeDtypeStruct((RING, 2 * BLOCK, 2 * WIDTH), jnp.bfloat16),
         ),
-        in_specs=[smem, smem, vmem, vmem],
-        out_specs=(vmem, vmem),
+        in_specs=[smem, smem, vmem] + [vmem] * (RING - 1),
+        out_specs=(vmem,) * 5,
         scratch_shapes=[
+            pltpu.VMEM((RING, 2 * BLOCK, 2 * WIDTH), jnp.bfloat16),
             pltpu.VMEM((LANES, WIDTH), jnp.bfloat16),
             pltpu.VMEM((LANES, WIDTH), jnp.bfloat16),
             pltpu.VMEM((MOST, BLOCK, LANES), jnp.float32),
             pltpu.VMEM((MOST, BLOCK, LANES), jnp.float32),
             pltpu.VMEM((RING, 2 * BLOCK, 2 * WIDTH), jnp.float32),
+            pltpu.VMEM((4, PIECE, SHARE * WIDTH), jnp.bfloat16),
         ],
-        compiler_params=pltpu.CompilerParams(vmem_limit_bytes=40 * 1024 * 1024),
+        compiler_params=pltpu.CompilerParams(vmem_limit_bytes=56 * 1024 * 1024),
         cost_estimate=pl.CostEstimate(
             flops=1_000_000, bytes_accessed=10_000, transcendentals=0
         ),
-    )(lengths, place, qg, kv)
-
-
-def expert_kernel(units, x_ref, w_ref, out_ref):
+    )(lengths, place, qg, *kv)
+
+
+def unpack_kernel(widths, place_ref, *refs):
+    pieces, outs, stack = refs[:4], refs[4:-1], refs[-1]
+    member = place_ref[2]
+    for step in range(4):
+        stack[step] = pieces[step][...]
+    for s in range(2):
+        for g in range(KV_HEADS):
+            piece = stack[member ^ (2 * s + g)]
+            column = 0
+            for out, width in zip(outs, widths):
+                out[s, :, g * width : (g + 1) * width] = piece[:, column : column + width]
+                column += width
+
+
+def unpack(place, pieces, widths):
+    vmem = pl.BlockSpec(memory_space=pltpu.VMEM)
+    return pl.pallas_call(
+        functools.partial(unpack_kernel, widths),
+        out_shape=tuple(
+            jax.ShapeDtypeStruct((2, PIECE, KV_HEADS * width), jnp.bfloat16) for width in widths
+        ),
+        in_specs=[pl.BlockSpec(memory_space=pltpu.SMEM)] + [vmem] * 4,
+        out_specs=(vmem,) * len(widths),
+        scratch_shapes=[pltpu.VMEM((4, PIECE, sum(widths)), jnp.bfloat16)],
+        compiler_params=pltpu.CompilerParams(vmem_limit_bytes=16 * 1024 * 1024),
+        cost_estimate=pl.CostEstimate(flops=0, bytes_accessed=1_000_000, transcendentals=0),
+    )(place, *pieces)
+
+
+def swap(pieces):
+    return [pieces[0]] + [
+        lax.ppermute(pieces[step], "ctx", member_swap(step)) for step in range(1, 4)
+    ]
+
+
+def expert_kernel(units, place_ref, x_ref, w_ref, out_ref):
     depth = w_ref.shape[0] * w_ref.shape[2]
     model = 2 * depth
     weights = [w_ref[:, x].reshape(depth, 3 * units) for x in range(2)]
+
+    def half(first, x):
+        return pl.ds(pl.multiple_of(first + (place_ref[1] ^ x) * depth, depth), depth)
 
     def through(first, column):
         total = None
         for x in range(2):
             part = jnp.dot(
-                x_ref[:, first + x * depth : first + (x + 1) * depth],
+                x_ref[:, half(first, x)],
                 weights[x][:, column * units : (column + 1) * units],
                 preferred_element_type=jnp.float32,
             )
@@ -169,25 +232,25 @@
     )
     both = jnp.concatenate([gate_grad, up_grad], axis=1)
     for x in range(2):
-        out_ref[:, x * depth : (x + 1) * depth] = lax.dot_general(
+        out_ref[:, half(0, x)] = lax.dot_general(
             both, weights[x][:, : 2 * units], NT, preferred_element_type=jnp.float32
         ).astype(jnp.bfloat16)
 
 
-def experts(rows, weights):
+def experts(place, rows, weights):
     count, width = rows.shape
     units = weights.shape[-1] // 3
     vmem = pl.BlockSpec(memory_space=pltpu.VMEM)
     return pl.pallas_call(
         functools.partial(expert_kernel, units),
         out_shape=jax.ShapeDtypeStruct((count, width // 2), jnp.bfloat16),
-        in_specs=[vmem, vmem],
+        in_specs=[pl.BlockSpec(memory_space=pltpu.SMEM), vmem, vmem],
         out_specs=vmem,
         compiler_params=pltpu.CompilerParams(vmem_limit_bytes=40 * 1024 * 1024),
         cost_estimate=pl.CostEstimate(
             flops=2_000_000_000, bytes_accessed=8_000_000, transcendentals=100_000
         ),
-    )(rows, weights)
+    )(place, rows, weights)
 
 
 def local(
@@ -208,11 +271,11 @@
     ctx = lax.axis_index("ctx")
     ring = (ctx % 16) // 2
     sequence = ctx // 16
-    place = jnp.stack([ring, sequence]).astype(jnp.int32)
+    place = jnp.stack([ring, sequence, 2 * sequence + ctx % 2]).astype(jnp.int32)
 
     shard = jnp.concatenate([gate_matrix[0], up_matrix[0], down_matrix[0].T], axis=1)
-    pair = lax.all_gather(shard, "ctx", axis_index_groups=X_PAIRS)
-
+    other = lax.ppermute(shard, "ctx", member_swap(2))
+    pair = jnp.stack([shard, other])
     def to_quads(array):
         split = array.reshape(groups, length, KV_HEADS, -1).transpose(0, 2, 1, 3)
         return split.reshape(groups * KV_HEADS, length, -1)
@@ -225,53 +288,43 @@
     quad = lax.all_to_all(
         quad_send, "ctx", 0, 0, tiled=True, axis_index_groups=QUADS
     ).reshape(2 * BLOCK, -1)
-    kv_own, qg = quad[:, : 2 * WIDTH], quad[:, 2 * WIDTH :]
+    tokens, model_width = expert_input.shape
+    rounds = lax.axis_size("exp")
+    half = tokens // rounds
+    choose = (expert_pick[:, None] == jnp.arange(rounds, dtype=jnp.int32)[None, :]).astype(
+        jnp.int32
+    )
+    before = jnp.cumsum(choose, axis=0) - choose
+    rank = jnp.sum(before * choose, axis=1)
+    slot = (rank // half * rounds + expert_pick) * half + rank % half
+    scaled_grad = (gate_weight[:, None] * expert_grad.astype(jnp.float32)).astype(jnp.bfloat16)
+    both = jnp.concatenate([expert_input, scaled_grad], axis=1)
+    pick = (slot[None, :] == jnp.arange(2 * tokens, dtype=jnp.int32)[:, None]).astype(
+        jnp.bfloat16
+    )
+    send = jnp.dot(pick, both, preferred_element_type=jnp.float32).astype(jnp.bfloat16)
+
+    def over_plane(array):
+        return lax.all_to_all(
+            array.reshape(2 * rounds, half, -1),
+            ("ctx", "exp"),
+            0,
+            0,
+            tiled=True,
+            axis_index_groups=PLANES,
+        ).reshape(2 * tokens, -1)
+
+    kv_own = quad[:, : 2 * WIDTH]
+    send, kv_own = lax.optimization_barrier((send, kv_own))
+    rows = over_plane(send)
     kv = [None] * RING
     kv[0] = up = down = kv_own
     for step in range(1, 5):
-        up = lax.ppermute(up, "ctx", z_shift(2))
-        kv[step] = up
+        up = kv[step] = lax.ppermute(up, "ctx", z_shift(2))
         if step < 4:
-            down = lax.ppermute(down, "ctx", z_shift(-2))
-            kv[RING - step] = down
-
-    tokens, model_width = expert_input.shape
-    rounds = lax.axis_size("exp")
-    capacity = 2 * tokens // rounds
-    choose = (expert_pick[:, None] == jnp.arange(rounds, dtype=jnp.int32)[None, :]).astype(
-        jnp.int32
-    )
-    before = jnp.cumsum(choose, axis=0) - choose
-    rank = jnp.sum(before * choose, axis=1)
-    slot = expert_pick * capacity + rank
-    scaled_grad = (gate_weight[:, None] * expert_grad.astype(jnp.float32)).astype(jnp.bfloat16)
-    both = jnp.concatenate([expert_input, scaled_grad], axis=1)
-    pick = (
-        slot[None, :] == jnp.arange(rounds * capacity, dtype=jnp.int32)[:, None]
-    ).astype(jnp.bfloat16)
-    send = jnp.dot(pick, both, preferred_element_type=jnp.float32).astype(jnp.bfloat16)
-    rows = lax.all_to_all(
-        send.reshape(rounds, capacity, 2 * model_width), "exp", 0, 0, tiled=True
-    )
-
+            down = kv[RING - step] = lax.ppermute(down, "ctx", z_shift(-2))
     *kv, rows = lax.optimization_barrier((*kv, rows))
-    dq, dkv = attention(doc_lengths, place, qg, jnp.stack(kv))
-
-    dq_back = lax.all_to_all(
-        dq.reshape(4, length, -1), "ctx", 0, 0, tiled=True, axis_index_groups=QUADS
-    )
-    dq_back, rows = lax.optimization_barrier((dq_back, rows))
-    result = experts(rows.reshape(rounds * capacity, 2 * model_width), weights)
-    returned = lax.all_to_all(
-        result.reshape(rounds, capacity, model_width), "exp", 0, 0, tiled=True
-    )
-    input_grad = jnp.dot(
-        pick.T, returned.reshape(rounds * capacity, model_width), preferred_element_type=jnp.float32
-    ).astype(jnp.bfloat16)
-
-    query_grad = (
-        dq_back.reshape(groups, KV_HEADS, length, -1).transpose(0, 2, 1, 3).reshape(queries.shape)
-    )
+    *dq, dkv = attention(doc_lengths, place, quad, kv[1:])
     dkv_own = lax.psum_scatter(
         dkv.reshape(RING * 2 * BLOCK, 2 * WIDTH),
         "ctx",
@@ -279,12 +332,18 @@
         tiled=True,
         axis_index_groups=RINGS,
     )
-    dkv_own, input_grad = lax.optimization_barrier((dkv_own, input_grad))
+    *dq, weights = lax.optimization_barrier((*dq, weights))
+    query_grad, = unpack(place, swap(dq), (SHARE * WIDTH,))
+
+    result = experts(place, rows, weights)
+    returned = over_plane(result)
+    dkv_own, query_grad, returned = lax.optimization_barrier((dkv_own, query_grad, returned))
     dkv_back = lax.all_to_all(
         dkv_own.reshape(4, length, 2 * WIDTH), "ctx", 0, 0, tiled=True, axis_index_groups=QUADS
     ).reshape(groups, KV_HEADS, length, 2 * WIDTH)
     key_grad = dkv_back[..., :WIDTH].transpose(0, 2, 1, 3).reshape(key_vectors.shape)
     value_grad = dkv_back[..., WIDTH:].transpose(0, 2, 1, 3).reshape(value_vectors.shape)
+    input_grad = jnp.dot(pick.T, returned, preferred_element_type=jnp.float32).astype(jnp.bfloat16)
     return (query_grad, key_grad, value_grad, input_grad)
 
 

time: 200 us -> 192 us (0.960)
  blocking collectives: 28.5 us -> 0 us
  starting transfers between devices: 52.3 us -> 71.2 us
  local copies, waits for them, and re-layouts: 13.7 us -> 6.93 us
  waiting for transfers between devices: 70.6 us -> 76.6 us
    all_to_all x1 -> x0, blocking collectives: 22.1 us -> none  [local(): lax.all_to_all(result.reshape(rounds, capacity, model_width), 'exp', 0, 0...]
    ppermute x7 -> x11, starting transfers between devices: 34.1 us -> 47.3 us  [the longest x3 23.8 us: local(): down = kv[RING - step] = lax.ppermute(down, 'ctx', z_shift(-2))]
    ppermute x7 -> x11, waiting for transfers between devices: 30 us -> 41 us  [the longest x4 30.2 us: local(): up = kv[step] = lax.ppermute(up, 'ctx', z_shift(2))]
    all_gather x1 -> x0, blocking collectives: 6.37 us -> none  [local(): pair = lax.all_gather(shard, 'ctx', axis_index_groups=X_PAIRS)]
    all_to_all x2, waiting for transfers between devices: 5.97 us -> 0.01 us  [over_plane(): lax.all_to_all(array.reshape(2 * rounds, half, -1), ('ctx', 'exp'), 0, 0,...]
    all_to_all x2, starting transfers between devices: 10.5 us -> 16 us  [over_plane(): lax.all_to_all(array.reshape(2 * rounds, half, -1), ('ctx', 'exp'), 0, 0,...]
    unnamed x34 -> x41, local copies, waits for them, and re-layouts: 8.8 us -> 4.09 us
    all_gather x1, waiting for transfers between devices: 0.01 us -> 3.01 us  [local(): weights = lax.all_gather(pair, 'ctx', axis_index_groups=Z_LINES)]
  transfers between devices with their start and end apart: 13 -> 17, of which waited for: 8 -> 10; matrix products, arithmetic and copies ran while one was open for 6% -> 4% of each run, Pallas kernels for 6% -> 6%
where the time goes in v3:
time: 192 us; the launch traced here: 190 us
  waiting for transfers between devices  76.6 us (40%)
  starting transfers between devices  71.2 us (37%)
  between operations  15.9 us (8%)
  Pallas kernels  11.9 us (6%)
  local copies, waits for them, and re-layouts  6.93 us (4%)
  other arithmetic  4.07 us (2%)
  matrix products  3.21 us (2%)
    ppermute x4, waiting for transfers between devices, local(): up = kv[step] = lax.ppermute(up, 'ctx', z_shift(2))  30.2 us
    ppermute x3, starting transfers between devices, local(): down = kv[RING - step] = lax.ppermute(down, 'ctx', z_shift(-2))  23.8 us
    reduce_scatter x1, waiting for transfers between devices, local(): lax.psum_scatter(dkv.reshape(RING * 2 * BLOCK, 2 * WIDTH), 'ctx', scatter...  17.3 us
    all_to_all x2, starting transfers between devices, over_plane(): lax.all_to_all(array.reshape(2 * rounds, half, -1), ('ctx', 'exp'), 0, 0,...  16 us
    all_to_all x1, waiting for transfers between devices, local(): lax.all_to_all(quad_send, 'ctx', 0, 0, tiled=True, axis_index_groups=QUADS)  11.5 us
    ppermute x4, starting transfers between devices, local(): up = kv[step] = lax.ppermute(up, 'ctx', z_shift(2))  10.9 us
    ppermute x3, waiting for transfers between devices, swap(): lax.ppermute(pieces[step], 'ctx', member_swap(step))  10.2 us
    ppermute x3, starting transfers between devices, swap(): lax.ppermute(pieces[step], 'ctx', member_swap(step))  9.21 us
  transfers between devices with their start and end apart: 17, of which 10 were waited for; matrix products, arithmetic and copies ran while one was open for 4% of the time, Pallas kernels for 6%

profile of v3, /device:TPU:24, one launch (start us, length us, event | category | flops | bytes accessed | tf_op | source)
XLA Modules:
  0.0 189.9 jit_solution(17005332137180482101)
XLA Ops:
  8.9 3.4 %collective-permute-start = (bf16[64,1152]{1,0:T(8,128)(2,1)S(1)}, bf16[64,1152]{1,0:T(8,128)(2,1)S(1)}, u32[]{:S(2)}, u32[]{:S(2)}) collective-permute-start(bf16[64,1152]{1,0:T(8,128)(2,1)S(1)} %get-tuple-element.59), channel_id=1, source_target_pairs={{0,256},{16,272},{32,288},{48,304},{64,320},{80,336},{96,352},{112... | collective-permute-start | bytes 442376 | tf_op jit(solution)/shard_map/ppermute | solution.py:277
  12.3 1.1 fusion.10
  14.7 1.2 pad_maximum_fusion
  17.2 4.3 %all-to-all-start = ((bf16[4,64,2304]{2,1,0:T(8,128)(2,1)}), bf16[4,64,2304]{2,1,0:T(8,128)(2,1)S(1)}, u32[]{:S(2)}, u32[]{:S(2)}) async-start(bf16[4,64,2304]{2,1,0:T(8,128)(2,1)} %pad_maximum_fusion), calls=%async_computation | async-start | bytes 2359296 | tf_op jit(solution)/shard_map/all_to_all | solution.py:288
  22.1 2.1 %convolution_convert_fusion = bf16[256,4096]{1,0:T(8,128)(2,1)} fusion(bf16[128,2048]{1,0:T(8,128)(2,1)S(1)} %multiply_convert_fusion, bf16[128,2048]{1,0:T(8,128)(2,1)S(1)} %copy-done.5, s32[128]{0:T(128)S(1)} %fusion.6), kind=kOutput, calls=%fused_computation | convolution fusion | flops 271613952 | bytes 3146240 | tf_op jit(solution)/shard_map/dot_general | solution.py:305
  24.2 11.5 %all-to-all-done = bf16[4,64,2304]{2,1,0:T(8,128)(2,1)S(1)} async-done(((bf16[4,64,2304]{2,1,0:T(8,128)(2,1)}), bf16[4,64,2304]{2,1,0:T(8,128)(2,1)S(1)}, u32[]{:S(2)}, u32[]{:S(2)}) %all-to-all-start) | async-done | bytes 1179680 | tf_op jit(solution)/shard_map/all_to_all | solution.py:288
  36.7 7.2 %all-to-all-start.1 = ((bf16[32,8,4096]{2,1,0:T(8,128)(2,1)}), bf16[32,8,4096]{2,1,0:T(8,128)(2,1)S(1)}, u32[]{:S(2)}, u32[]{:S(2)}) async-start(bf16[32,8,4096]{2,1,0:T(8,128)(2,1)} %bitcast.37), calls=%async_computation.1 | async-start | bytes 4194304 | tf_op jit(solution)/shard_map/all_to_all | solution.py:308
  43.9 5.2 %collective-permute-start.1 = (bf16[256,256]{1,0:T(8,128)(2,1)S(1)}, bf16[256,256]{1,0:T(8,128)(2,1)S(1)}, u32[]{:S(2)}, u32[]{:S(2)}) collective-permute-start(bf16[256,256]{1,0:T(8,128)(2,1)S(1)} %slice.44), channel_id=1, source_target_pairs={{0,32},{16,48},{32,64},{48,80},{64,96},{80,112},{96,128},{112,144}... | collective-permute-start | bytes 393224 | tf_op jit(solution)/shard_map/ppermute | solution.py:323
  49.1 11.8 %collective-permute-start.5 = (bf16[256,256]{1,0:T(8,128)(2,1)S(1)}, bf16[256,256]{1,0:T(8,128)(2,1)S(1)}, u32[]{:S(2)}, u32[]{:S(2)}) collective-permute-start(bf16[256,256]{1,0:T(8,128)(2,1)S(1)} %slice.44), channel_id=1, source_target_pairs={{0,224},{16,240},{32,0},{48,16},{64,32},{80,48},{96,64},{112,80},{... | collective-permute-start | bytes 393224 | tf_op jit(solution)/shard_map/ppermute | solution.py:325
  60.9 7.4 %collective-permute-done.1.refs_0_ = bf16[256,256]{1,0:T(8,128)(2,1)S(1)} collective-permute-done((bf16[256,256]{1,0:T(8,128)(2,1)S(1)}, bf16[256,256]{1,0:T(8,128)(2,1)S(1)}, u32[]{:S(2)}, u32[]{:S(2)}) %collective-permute-start.1) | collective-permute-done | bytes 131104 | tf_op jit(solution)/shard_map/ppermute | solution.py:323
  68.2 1.9 %collective-permute-start.2 = (bf16[256,256]{1,0:T(8,128)(2,1)S(1)}, bf16[256,256]{1,0:T(8,128)(2,1)S(1)}, u32[]{:S(2)}, u32[]{:S(2)}) collective-permute-start(bf16[256,256]{1,0:T(8,128)(2,1)S(1)} %collective-permute-done.1.refs_0_), channel_id=1, source_target_pairs={{0,32},{16,48},{32,64},{48,80},{64,96},{80,112},{96,128},{112,144}... | collective-permute-start | bytes 393224 | tf_op jit(solution)/shard_map/ppermute | solution.py:323
  70.2 6.0 %collective-permute-start.6 = (bf16[256,256]{1,0:T(8,128)(2,1)S(1)}, bf16[256,256]{1,0:T(8,128)(2,1)S(1)}, u32[]{:S(2)}, u32[]{:S(2)}) collective-permute-start(bf16[256,256]{1,0:T(8,128)(2,1)S(1)} %collective-permute-done.5.refs_6_), channel_id=1, source_target_pairs={{0,224},{16,240},{32,0},{48,16},{64,32},{80,48},{96,64},{112,80},{... | collective-permute-start | bytes 393224 | tf_op jit(solution)/shard_map/ppermute | solution.py:325
  76.2 6.4 %collective-permute-done.2.refs_1_ = bf16[256,256]{1,0:T(8,128)(2,1)S(1)} collective-permute-done((bf16[256,256]{1,0:T(8,128)(2,1)S(1)}, bf16[256,256]{1,0:T(8,128)(2,1)S(1)}, u32[]{:S(2)}, u32[]{:S(2)}) %collective-permute-start.2) | collective-permute-done | bytes 131104 | tf_op jit(solution)/shard_map/ppermute | solution.py:323
  82.6 1.9 %collective-permute-start.3 = (bf16[256,256]{1,0:T(8,128)(2,1)S(1)}, bf16[256,256]{1,0:T(8,128)(2,1)S(1)}, u32[]{:S(2)}, u32[]{:S(2)}) collective-permute-start(bf16[256,256]{1,0:T(8,128)(2,1)S(1)} %collective-permute-done.2.refs_1_), channel_id=1, source_target_pairs={{0,32},{16,48},{32,64},{48,80},{64,96},{80,112},{96,128},{112,144}... | collective-permute-start | bytes 393224 | tf_op jit(solution)/shard_map/ppermute | solution.py:323
  84.5 6.0 %collective-permute-start.7 = (bf16[256,256]{1,0:T(8,128)(2,1)S(1)}, bf16[256,256]{1,0:T(8,128)(2,1)S(1)}, u32[]{:S(2)}, u32[]{:S(2)}) collective-permute-start(bf16[256,256]{1,0:T(8,128)(2,1)S(1)} %collective-permute-done.6.refs_5_), channel_id=1, source_target_pairs={{0,224},{16,240},{32,0},{48,16},{64,32},{80,48},{96,64},{112,80},{... | collective-permute-start | bytes 393224 | tf_op jit(solution)/shard_map/ppermute | solution.py:325
  90.6 6.1 %collective-permute-done.3.refs_2_ = bf16[256,256]{1,0:T(8,128)(2,1)S(1)} collective-permute-done((bf16[256,256]{1,0:T(8,128)(2,1)S(1)}, bf16[256,256]{1,0:T(8,128)(2,1)S(1)}, u32[]{:S(2)}, u32[]{:S(2)}) %collective-permute-start.3) | collective-permute-done | bytes 131104 | tf_op jit(solution)/shard_map/ppermute | solution.py:323
  96.7 1.9 %collective-permute-start.4 = (bf16[256,256]{1,0:T(8,128)(2,1)S(1)}, bf16[256,256]{1,0:T(8,128)(2,1)S(1)}, u32[]{:S(2)}, u32[]{:S(2)}) collective-permute-start(bf16[256,256]{1,0:T(8,128)(2,1)S(1)} %collective-permute-done.3.refs_2_), channel_id=1, source_target_pairs={{0,32},{16,48},{32,64},{48,80},{64,96},{80,112},{96,128},{112,144}... | collective-permute-start | bytes 393224 | tf_op jit(solution)/shard_map/ppermute | solution.py:323
  99.3 10.3 %collective-permute-done.4.refs_3_ = bf16[256,256]{1,0:T(8,128)(2,1)S(1)} collective-permute-done((bf16[256,256]{1,0:T(8,128)(2,1)S(1)}, bf16[256,256]{1,0:T(8,128)(2,1)S(1)}, u32[]{:S(2)}, u32[]{:S(2)}) %collective-permute-start.4) | collective-permute-done | bytes 131104 | tf_op jit(solution)/shard_map/ppermute | solution.py:323
  110.3 6.2 %shard_map.147 = (bf16[64,1024]{1,0:T(8,128)(2,1)}, bf16[64,1024]{1,0:T(8,128)(2,1)}, bf16[64,1024]{1,0:T(8,128)(2,1)}, bf16[64,1024]{1,0:T(8,128)(2,1)}, bf16[8,256,256]{2,1,0:T(8,128)(2,1)}) custom-call(s32[2,8]{1,0:T(2,128)} %lengths_ref.1, s32[3]{0:T(128)} %pad_add_fusion.place_ref, bf16[256,2304]{1,0:T(8,128)(2,1)} %bitcast.39, ...), custom_call_target="tpu_custom_call" | custom-call | flops 1000000 | bytes 10000 | tf_op jit(solution)/shard_map/pallas_call | solution.py:147
  116.5 3.0 %all-gather.3.cloned.1.call-done = bf16[32,64,1152]{2,1,0:T(8,128)(2,1)} async-done(((bf16[2,64,1152]{2,1,0:T(8,128)(2,1)}), bf16[32,64,1152]{2,1,0:T(8,128)(2,1)}) %all-gather.3.cloned.1.call-update) | async-done | bytes 4718608 | tf_op jit(solution)/shard_map/all_gather | solution.py:287
  119.5 2.3 %copy-done = bf16[32,64,1152]{2,1,0:T(8,128)(2,1)S(1)} copy-done((bf16[32,64,1152]{2,1,0:T(8,128)(2,1)S(1)}, bf16[32,64,1152]{2,1,0:T(8,128)(2,1)}, u32[]{:S(2)}) %copy-start) | copy-done | bytes 4718616
  121.9 4.3 %shard_map.149 = bf16[256,2048]{1,0:T(8,128)(2,1)} custom-call(s32[3]{0:T(128)S(1)} %copy-done.2, bf16[256,4096]{1,0:T(8,128)(2,1)S(1)} %bitcast.35, bf16[16,2,64,1152]{3,2,1,0:T(8,128)(2,1)S(1)} %bitcast.36), custom_call_target="tpu_custom_call" | custom-call | flops 2000000000 | bytes 8000000 | tf_op jit(solution)/shard_map/pallas_call | solution.py:244
  126.2 8.8 %all-to-all-start.2 = ((bf16[32,8,2048]{2,1,0:T(8,128)(2,1)}), bf16[32,8,2048]{2,1,0:T(8,128)(2,1)S(1)}, u32[]{:S(2)}, u32[]{:S(2)}) async-start(bf16[32,8,2048]{2,1,0:T(8,128)(2,1)} %bitcast.18), calls=%async_computation.3 | async-start | bytes 2097152 | tf_op jit(solution)/shard_map/all_to_all | solution.py:308
  135.0 1.9 %collective-permute-start.8 = (bf16[64,1024]{1,0:T(8,128)(2,1)S(1)}, bf16[64,1024]{1,0:T(8,128)(2,1)S(1)}, u32[]{:S(2)}, u32[]{:S(2)}) collective-permute-start(bf16[64,1024]{1,0:T(8,128)(2,1)S(1)} %copy-done.19), channel_id=1, source_target_pairs={{0,16},{16,0},{32,48},{48,32},{64,80},{80,64},{96,112},{112,96},{1... | collective-permute-start | bytes 393224 | tf_op jit(solution)/shard_map/ppermute | solution.py:202
  136.9 3.4 %collective-permute-start.9 = (bf16[64,1024]{1,0:T(8,128)(2,1)S(1)}, bf16[64,1024]{1,0:T(8,128)(2,1)S(1)}, u32[]{:S(2)}, u32[]{:S(2)}) collective-permute-start(bf16[64,1024]{1,0:T(8,128)(2,1)S(1)} %copy-done.18), channel_id=1, source_target_pairs={{0,256},{16,272},{32,288},{48,304},{64,320},{80,336},{96,352},{112... | collective-permute-start | bytes 393224 | tf_op jit(solution)/shard_map/ppermute | solution.py:202
  140.4 3.9 %collective-permute-start.10 = (bf16[64,1024]{1,0:T(8,128)(2,1)S(1)}, bf16[64,1024]{1,0:T(8,128)(2,1)S(1)}, u32[]{:S(2)}, u32[]{:S(2)}) collective-permute-start(bf16[64,1024]{1,0:T(8,128)(2,1)S(1)} %copy-done.17), channel_id=1, source_target_pairs={{0,272},{16,256},{32,304},{48,288},{64,336},{80,320},{96,368},{112... | collective-permute-start | bytes 393224 | tf_op jit(solution)/shard_map/ppermute | solution.py:202
  144.3 10.2 %collective-permute-done.9.refs_2_ = bf16[64,1024]{1,0:T(8,128)(2,1)S(1)} collective-permute-done((bf16[64,1024]{1,0:T(8,128)(2,1)S(1)}, bf16[64,1024]{1,0:T(8,128)(2,1)S(1)}, u32[]{:S(2)}, u32[]{:S(2)}) %collective-permute-start.9) | collective-permute-done | bytes 131104 | tf_op jit(solution)/shard_map/ppermute | solution.py:202
  154.5 1.4 shard_map.148
  155.9 17.3 %reduce-scatter.2.cloned.1.call-done = bf16[256,256]{1,0:T(8,128)(2,1)} async-done(((bf16[2048,256]{1,0:T(8,128)(2,1)}), bf16[256,256]{1,0:T(8,128)(2,1)}) %reduce-scatter.2.cloned.1.call-update) | async-done | bytes 131088 | tf_op jit(solution)/shard_map/reduce_scatter | solution.py:328
  173.2 3.5 %all-to-all-start.3 = ((bf16[4,64,256]{2,1,0:T(8,128)(2,1)}), bf16[4,64,256]{2,1,0:T(8,128)(2,1)S(1)}, u32[]{:S(2)}, u32[]{:S(2)}) async-start(bf16[4,64,256]{2,1,0:T(8,128)(2,1)} %bitcast.48), calls=%async_computation.4 | async-start | bytes 262144 | tf_op jit(solution)/shard_map/all_to_all | solution.py:341
  176.7 1.1 convolution_convert_fusion.1
  177.9 3.9 %all-to-all-done.3 = bf16[4,64,256]{2,1,0:T(8,128)(2,1)S(1)} async-done(((bf16[4,64,256]{2,1,0:T(8,128)(2,1)}), bf16[4,64,256]{2,1,0:T(8,128)(2,1)S(1)}, u32[]{:S(2)}, u32[]{:S(2)}) %all-to-all-start.3) | async-done | bytes 131104 | tf_op jit(solution)/shard_map/all_to_all | solution.py:341
  (69 shorter events, 7.1 us)
Async XLA Ops:
  8.0 6.5 %copy-start.13 = (bf16[2,64,256]{2,1,0:T(8,128)(2,1)S(1)}, bf16[2,64,256]{2,1,0:T(8,128)(2,1)}, u32[]{:S(2)}) copy-start(bf16[2,64,256]{2,1,0:T(8,128)(2,1)} %param.14) | copy-start | bytes 196612
  8.0 6.5 %copy-start.14 = (bf16[2,64,256]{2,1,0:T(8,128)(2,1)S(1)}, bf16[2,64,256]{2,1,0:T(8,128)(2,1)}, u32[]{:S(2)}) copy-start(bf16[2,64,256]{2,1,0:T(8,128)(2,1)} %param.13) | copy-start | bytes 196612
  8.0 111.5 %all-gather.3.cloned.1.call-start = ((), (), s32[]{:S(2)}) async-start(), calls=%async_computation.6 | async-start | bytes 5013504 | tf_op jit(solution)/shard_map/all_gather | solution.py:287
  8.9 7.5 %collective-permute-start = (bf16[64,1152]{1,0:T(8,128)(2,1)S(1)}, bf16[64,1152]{1,0:T(8,128)(2,1)S(1)}, u32[]{:S(2)}, u32[]{:S(2)}) collective-permute-start(bf16[64,1152]{1,0:T(8,128)(2,1)S(1)} %get-tuple-element.59), channel_id=1, source_target_pairs={{0,256},{16,272},{32,288},{48,304},{64,320},{80,336},{96,352},{112... | collective-permute-start | bytes 442376 | tf_op jit(solution)/shard_map/ppermute | solution.py:277
  15.8 6.1 %copy-start.4 = (bf16[128,2048]{1,0:T(8,128)(2,1)S(1)}, bf16[128,2048]{1,0:T(8,128)(2,1)}, u32[]{:S(2)}) copy-start(bf16[128,2048]{1,0:T(8,128)(2,1)} %param.18) | copy-start | bytes 1572868
  15.8 6.1 %copy-start.16 = (f32[128]{0:T(128)S(1)}, f32[128]{0:T(128)}, u32[]{:S(2)}) copy-start(f32[128]{0:T(128)} %param.20) | copy-start | bytes 1540
  17.2 18.4 %all-to-all-start = ((bf16[4,64,2304]{2,1,0:T(8,128)(2,1)}), bf16[4,64,2304]{2,1,0:T(8,128)(2,1)S(1)}, u32[]{:S(2)}, u32[]{:S(2)}) async-start(bf16[4,64,2304]{2,1,0:T(8,128)(2,1)} %pad_maximum_fusion), calls=%async_computation | async-start | bytes 2359296 | tf_op jit(solution)/shard_map/all_to_all | solution.py:288
  36.7 72.9 %all-to-all-start.1 = ((bf16[32,8,4096]{2,1,0:T(8,128)(2,1)}), bf16[32,8,4096]{2,1,0:T(8,128)(2,1)S(1)}, u32[]{:S(2)}, u32[]{:S(2)}) async-start(bf16[32,8,4096]{2,1,0:T(8,128)(2,1)} %bitcast.37), calls=%async_computation.1 | async-start | bytes 4194304 | tf_op jit(solution)/shard_map/all_to_all | solution.py:308
  43.9 129.3 %reduce-scatter.2.cloned.1.call-start = ((), (), s32[]{:S(2)}) async-start(), calls=%async_computation.5 | async-start | bytes 1179648 | tf_op jit(solution)/shard_map/reduce_scatter | solution.py:328
  43.9 24.3 %collective-permute-start.1 = (bf16[256,256]{1,0:T(8,128)(2,1)S(1)}, bf16[256,256]{1,0:T(8,128)(2,1)S(1)}, u32[]{:S(2)}, u32[]{:S(2)}) collective-permute-start(bf16[256,256]{1,0:T(8,128)(2,1)S(1)} %slice.44), channel_id=1, source_target_pairs={{0,32},{16,48},{32,64},{48,80},{64,96},{80,112},{96,128},{112,144}... | collective-permute-start | bytes 393224 | tf_op jit(solution)/shard_map/ppermute | solution.py:323
  49.1 21.1 %collective-permute-start.5 = (bf16[256,256]{1,0:T(8,128)(2,1)S(1)}, bf16[256,256]{1,0:T(8,128)(2,1)S(1)}, u32[]{:S(2)}, u32[]{:S(2)}) collective-permute-start(bf16[256,256]{1,0:T(8,128)(2,1)S(1)} %slice.44), channel_id=1, source_target_pairs={{0,224},{16,240},{32,0},{48,16},{64,32},{80,48},{96,64},{112,80},{... | collective-permute-start | bytes 393224 | tf_op jit(solution)/shard_map/ppermute | solution.py:325
  68.2 41.4 %copy-start.6 = (bf16[256,256]{1,0:T(8,128)(2,1)}, bf16[256,256]{1,0:T(8,128)(2,1)S(1)}, u32[]{:S(2)}) copy-start(bf16[256,256]{1,0:T(8,128)(2,1)S(1)} %collective-permute-done.1.refs_0_) | copy-start | bytes 393220
  68.2 14.4 %collective-permute-start.2 = (bf16[256,256]{1,0:T(8,128)(2,1)S(1)}, bf16[256,256]{1,0:T(8,128)(2,1)S(1)}, u32[]{:S(2)}, u32[]{:S(2)}) collective-permute-start(bf16[256,256]{1,0:T(8,128)(2,1)S(1)} %collective-permute-done.1.refs_0_), channel_id=1, source_target_pairs={{0,32},{16,48},{32,64},{48,80},{64,96},{80,112},{96,128},{112,144}... | collective-permute-start | bytes 393224 | tf_op jit(solution)/shard_map/ppermute | solution.py:323
  70.2 39.4 %copy-start.7 = (bf16[256,256]{1,0:T(8,128)(2,1)}, bf16[256,256]{1,0:T(8,128)(2,1)S(1)}, u32[]{:S(2)}) copy-start(bf16[256,256]{1,0:T(8,128)(2,1)S(1)} %collective-permute-done.5.refs_6_) | copy-start | bytes 393220
  70.2 14.3 %collective-permute-start.6 = (bf16[256,256]{1,0:T(8,128)(2,1)S(1)}, bf16[256,256]{1,0:T(8,128)(2,1)S(1)}, u32[]{:S(2)}, u32[]{:S(2)}) collective-permute-start(bf16[256,256]{1,0:T(8,128)(2,1)S(1)} %collective-permute-done.5.refs_6_), channel_id=1, source_target_pairs={{0,224},{16,240},{32,0},{48,16},{64,32},{80,48},{96,64},{112,80},{... | collective-permute-start | bytes 393224 | tf_op jit(solution)/shard_map/ppermute | solution.py:325
  82.6 27.0 %copy-start.8 = (bf16[256,256]{1,0:T(8,128)(2,1)}, bf16[256,256]{1,0:T(8,128)(2,1)S(1)}, u32[]{:S(2)}) copy-start(bf16[256,256]{1,0:T(8,128)(2,1)S(1)} %collective-permute-done.2.refs_1_) | copy-start | bytes 393220
  82.6 14.1 %collective-permute-start.3 = (bf16[256,256]{1,0:T(8,128)(2,1)S(1)}, bf16[256,256]{1,0:T(8,128)(2,1)S(1)}, u32[]{:S(2)}, u32[]{:S(2)}) collective-permute-start(bf16[256,256]{1,0:T(8,128)(2,1)S(1)} %collective-permute-done.2.refs_1_), channel_id=1, source_target_pairs={{0,32},{16,48},{32,64},{48,80},{64,96},{80,112},{96,128},{112,144}... | collective-permute-start | bytes 393224 | tf_op jit(solution)/shard_map/ppermute | solution.py:323
  84.5 25.1 %copy-start.9 = (bf16[256,256]{1,0:T(8,128)(2,1)}, bf16[256,256]{1,0:T(8,128)(2,1)S(1)}, u32[]{:S(2)}) copy-start(bf16[256,256]{1,0:T(8,128)(2,1)S(1)} %collective-permute-done.6.refs_5_) | copy-start | bytes 393220
  84.5 14.7 %collective-permute-start.7 = (bf16[256,256]{1,0:T(8,128)(2,1)S(1)}, bf16[256,256]{1,0:T(8,128)(2,1)S(1)}, u32[]{:S(2)}, u32[]{:S(2)}) collective-permute-start(bf16[256,256]{1,0:T(8,128)(2,1)S(1)} %collective-permute-done.6.refs_5_), channel_id=1, source_target_pairs={{0,224},{16,240},{32,0},{48,16},{64,32},{80,48},{96,64},{112,80},{... | collective-permute-start | bytes 393224 | tf_op jit(solution)/shard_map/ppermute | solution.py:325
  96.7 13.0 %copy-start.10 = (bf16[256,256]{1,0:T(8,128)(2,1)}, bf16[256,256]{1,0:T(8,128)(2,1)S(1)}, u32[]{:S(2)}) copy-start(bf16[256,256]{1,0:T(8,128)(2,1)S(1)} %collective-permute-done.3.refs_2_) | copy-start | bytes 393220
  96.7 12.9 %collective-permute-start.4 = (bf16[256,256]{1,0:T(8,128)(2,1)S(1)}, bf16[256,256]{1,0:T(8,128)(2,1)S(1)}, u32[]{:S(2)}, u32[]{:S(2)}) collective-permute-start(bf16[256,256]{1,0:T(8,128)(2,1)S(1)} %collective-permute-done.3.refs_2_), channel_id=1, source_target_pairs={{0,32},{16,48},{32,64},{48,80},{64,96},{80,112},{96,128},{112,144}... | collective-permute-start | bytes 393224 | tf_op jit(solution)/shard_map/ppermute | solution.py:323
  99.3 20.3 %copy-start.2 = (s32[3]{0:T(128)S(1)}, s32[3]{0:T(128)}, u32[]{:S(2)}) copy-start(s32[3]{0:T(128)} %pad_add_fusion.place_ref) | copy-start | bytes 40
  99.3 10.4 %copy-start.11 = (bf16[256,256]{1,0:T(8,128)(2,1)}, bf16[256,256]{1,0:T(8,128)(2,1)S(1)}, u32[]{:S(2)}) copy-start(bf16[256,256]{1,0:T(8,128)(2,1)S(1)} %collective-permute-done.7.refs_4_) | copy-start | bytes 393220
  126.1 8.8 %copy-start.19 = (bf16[64,1024]{1,0:T(8,128)(2,1)S(1)}, bf16[64,1024]{1,0:T(8,128)(2,1)}, u32[]{:S(2)}) copy-start(bf16[64,1024]{1,0:T(8,128)(2,1)} %get-tuple-element.46) | copy-start | bytes 393220
  126.1 10.8 %copy-start.18 = (bf16[64,1024]{1,0:T(8,128)(2,1)S(1)}, bf16[64,1024]{1,0:T(8,128)(2,1)}, u32[]{:S(2)}) copy-start(bf16[64,1024]{1,0:T(8,128)(2,1)} %get-tuple-element.47) | copy-start | bytes 393220
  126.1 14.2 %copy-start.17 = (bf16[64,1024]{1,0:T(8,128)(2,1)S(1)}, bf16[64,1024]{1,0:T(8,128)(2,1)}, u32[]{:S(2)}) copy-start(bf16[64,1024]{1,0:T(8,128)(2,1)} %get-tuple-element.48) | copy-start | bytes 393220
  126.2 28.3 %copy-start.1 = (bf16[64,1024]{1,0:T(8,128)(2,1)S(1)}, bf16[64,1024]{1,0:T(8,128)(2,1)}, u32[]{:S(2)}) copy-start(bf16[64,1024]{1,0:T(8,128)(2,1)} %get-tuple-element.45.refs_0_) | copy-start | bytes 393220
  126.2 47.0 %all-to-all-start.2 = ((bf16[32,8,2048]{2,1,0:T(8,128)(2,1)}), bf16[32,8,2048]{2,1,0:T(8,128)(2,1)S(1)}, u32[]{:S(2)}, u32[]{:S(2)}) async-start(bf16[32,8,2048]{2,1,0:T(8,128)(2,1)} %bitcast.18), calls=%async_computation.3 | async-start | bytes 2097152 | tf_op jit(solution)/shard_map/all_to_all | solution.py:308
  135.0 9.3 %collective-permute-start.8 = (bf16[64,1024]{1,0:T(8,128)(2,1)S(1)}, bf16[64,1024]{1,0:T(8,128)(2,1)S(1)}, u32[]{:S(2)}, u32[]{:S(2)}) collective-permute-start(bf16[64,1024]{1,0:T(8,128)(2,1)S(1)} %copy-done.19), channel_id=1, source_target_pairs={{0,16},{16,0},{32,48},{48,32},{64,80},{80,64},{96,112},{112,96},{1... | collective-permute-start | bytes 393224 | tf_op jit(solution)/shard_map/ppermute | solution.py:202
  136.9 17.5 %collective-permute-start.9 = (bf16[64,1024]{1,0:T(8,128)(2,1)S(1)}, bf16[64,1024]{1,0:T(8,128)(2,1)S(1)}, u32[]{:S(2)}, u32[]{:S(2)}) collective-permute-start(bf16[64,1024]{1,0:T(8,128)(2,1)S(1)} %copy-done.18), channel_id=1, source_target_pairs={{0,256},{16,272},{32,288},{48,304},{64,320},{80,336},{96,352},{112... | collective-permute-start | bytes 393224 | tf_op jit(solution)/shard_map/ppermute | solution.py:202
  140.4 14.1 %collective-permute-start.10 = (bf16[64,1024]{1,0:T(8,128)(2,1)S(1)}, bf16[64,1024]{1,0:T(8,128)(2,1)S(1)}, u32[]{:S(2)}, u32[]{:S(2)}) collective-permute-start(bf16[64,1024]{1,0:T(8,128)(2,1)S(1)} %copy-done.17), channel_id=1, source_target_pairs={{0,272},{16,256},{32,304},{48,288},{64,336},{80,320},{96,368},{112... | collective-permute-start | bytes 393224 | tf_op jit(solution)/shard_map/ppermute | solution.py:202
  173.2 8.6 %all-to-all-start.3 = ((bf16[4,64,256]{2,1,0:T(8,128)(2,1)}), bf16[4,64,256]{2,1,0:T(8,128)(2,1)S(1)}, u32[]{:S(2)}, u32[]{:S(2)}) async-start(bf16[4,64,256]{2,1,0:T(8,128)(2,1)} %bitcast.48), calls=%async_computation.4 | async-start | bytes 262144 | tf_op jit(solution)/shard_map/all_to_all | solution.py:341
  (5 other events, 14.6 us)
Sparse Core Ops, SparseCore 0:
  17.3 102.1 all-gather.2
Sparse Core Ops, SparseCore 1:
  116.6 56.5 reduce-scatter.1

commit v4 on v3

--- a/solution.py
+++ b/solution.py
@@ -18,6 +18,7 @@
 MOST = 9
 PIECE = 64
 SCALE = 1.0 / math.sqrt(WIDTH)
+LOG2_E = 1.0 / math.log(2.0)
 
 X_PAIRS = [[z, 16 + z] for z in range(16)]
 Z_LINES = [[x * 16 + z for z in range(16)] for x in range(2)]
@@ -85,9 +86,7 @@
             slot, offset, block = tile(i)
             keys = kv_ref[slot, pl.ds(offset, BLOCK), 0:WIDTH]
             values = kv_ref[slot, pl.ds(offset, BLOCK), WIDTH : 2 * WIDTH]
-            scores = (
-                lax.dot_general(keys, q_rows[...], NT, preferred_element_type=jnp.float32) * SCALE
-            )
+            scores = lax.dot_general(keys, q_rows[...], NT, preferred_element_type=jnp.float32)
             at = block * BLOCK + lax.broadcasted_iota(jnp.int32, (BLOCK, LANES), 0)
             scores = jnp.where((at >= begin) & (at <= position), scores, -1e30)
             prob[i] = scores
@@ -100,7 +99,7 @@
 
         def sum_step(i, carry):
             total, weighted = carry
-            weights = jnp.exp(prob[i] - highest)
+            weights = jnp.exp2((prob[i] - highest) * (SCALE * LOG2_E))
             prob[i] = weights
             return (
                 total + jnp.sum(weights, axis=0, keepdims=True),
@@ -275,7 +274,6 @@
 
     shard = jnp.concatenate([gate_matrix[0], up_matrix[0], down_matrix[0].T], axis=1)
     other = lax.ppermute(shard, "ctx", member_swap(2))
-    pair = jnp.stack([shard, other])
     def to_quads(array):
         split = array.reshape(groups, length, KV_HEADS, -1).transpose(0, 2, 1, 3)
         return split.reshape(groups * KV_HEADS, length, -1)
@@ -283,8 +281,6 @@
     quad_send = jnp.concatenate(
         [to_quads(a) for a in (key_vectors, value_vectors, queries, output_grad)], axis=2
     )
-    pair, quad_send = lax.optimization_barrier((pair, quad_send))
-    weights = lax.all_gather(pair, "ctx", axis_index_groups=Z_LINES)
     quad = lax.all_to_all(
         quad_send, "ctx", 0, 0, tiled=True, axis_index_groups=QUADS
     ).reshape(2 * BLOCK, -1)
@@ -314,8 +310,10 @@
             axis_index_groups=PLANES,
         ).reshape(2 * tokens, -1)
 
+    other, send = lax.optimization_barrier((other, send))
+    pair, quad, send = lax.optimization_barrier((jnp.stack([shard, other]), quad, send))
+    weights = lax.all_gather(pair, "ctx", axis_index_groups=Z_LINES)
     kv_own = quad[:, : 2 * WIDTH]
-    send, kv_own = lax.optimization_barrier((send, kv_own))
     rows = over_plane(send)
     kv = [None] * RING
     kv[0] = up = down = kv_own

time: 192 us -> 187 us (0.974); the launches traced: 190 us -> 187 us
  starting transfers between devices: 71.2 us -> 68.9 us
    ppermute x4, waiting for transfers between devices: 30.2 us -> 8.6 us  [local(): up = kv[step] = lax.ppermute(up, 'ctx', z_shift(2))]
    all_gather x1, waiting for transfers between devices: 3.01 us -> 24.5 us  [local(): weights = lax.all_gather(pair, 'ctx', axis_index_groups=Z_LINES)]
    reduce_scatter x1, waiting for transfers between devices: 17.3 us -> 2.4 us  [local(): lax.psum_scatter(dkv.reshape(RING * 2 * BLOCK, 2 * WIDTH), 'ctx', scatter...]
    ppermute x3, waiting for transfers between devices: 0.01 us -> 14.6 us  [local(): down = kv[RING - step] = lax.ppermute(down, 'ctx', z_shift(-2))]
    all_to_all x1, waiting for transfers between devices: 11.5 us -> 0.01 us  [local(): lax.all_to_all(quad_send, 'ctx', 0, 0, tiled=True, axis_index_groups=QUADS)]
    ppermute x1, waiting for transfers between devices: 0.57 us -> 11.4 us  [local(): other = lax.ppermute(shard, 'ctx', member_swap(2))]
    unnamed x41 -> x47, local copies, waits for them, and re-layouts: 4.09 us -> 3.06 us
  transfers between devices with their start and end apart: 17 -> 17, of which waited for: 10 -> 12; matrix products, arithmetic and copies ran while one was open for 4% -> 3% of each run, Pallas kernels for 6% -> 7%
where the time goes in v4:
time: 187 us
  waiting for transfers between devices  76.2 us (41%)
  starting transfers between devices  68.9 us (37%)
  between operations  16 us (9%)
  Pallas kernels  13.6 us (7%)
  local copies, waits for them, and re-layouts  5.93 us (3%)
  other arithmetic  3.26 us (2%)
  matrix products  3.2 us (2%)
    all_gather x1, waiting for transfers between devices, local(): weights = lax.all_gather(pair, 'ctx', axis_index_groups=Z_LINES)  24.5 us
    ppermute x3, starting transfers between devices, local(): down = kv[RING - step] = lax.ppermute(down, 'ctx', z_shift(-2))  22.2 us
    all_to_all x2, starting transfers between devices, over_plane(): lax.all_to_all(array.reshape(2 * rounds, half, -1), ('ctx', 'exp'), 0, 0,...  14.8 us
    ppermute x3, waiting for transfers between devices, local(): down = kv[RING - step] = lax.ppermute(down, 'ctx', z_shift(-2))  14.6 us
    ppermute x1, waiting for transfers between devices, local(): other = lax.ppermute(shard, 'ctx', member_swap(2))  11.4 us
    ppermute x4, starting transfers between devices, local(): up = kv[step] = lax.ppermute(up, 'ctx', z_shift(2))  10.9 us
    ppermute x3, waiting for transfers between devices, swap(): lax.ppermute(pieces[step], 'ctx', member_swap(step))  10.7 us
    ppermute x3, starting transfers between devices, swap(): lax.ppermute(pieces[step], 'ctx', member_swap(step))  9.21 us
  transfers between devices with their start and end apart: 17, of which 12 were waited for; matrix products, arithmetic and copies ran while one was open for 3% of the time, Pallas kernels for 7%

profile of v4, /device:TPU:24, one launch (start us, length us, event | category | flops | bytes accessed | tf_op | source)
XLA Modules:
  0.0 187.0 jit_solution(2065369347537172724)
XLA Ops:
  11.6 4.2 %all-to-all-start = ((bf16[4,64,2304]{2,1,0:T(8,128)(2,1)}), bf16[4,64,2304]{2,1,0:T(8,128)(2,1)S(1)}, u32[]{:S(2)}, u32[]{:S(2)}) async-start(bf16[4,64,2304]{2,1,0:T(8,128)(2,1)} %pad_maximum_fusion), calls=%async_computation | async-start | bytes 2359296 | tf_op jit(solution)/shard_map/all_to_all | solution.py:284
  15.9 3.9 %collective-permute-start = (bf16[64,1152]{1,0:T(8,128)(2,1)S(1)}, bf16[64,1152]{1,0:T(8,128)(2,1)S(1)}, u32[]{:S(2)}, u32[]{:S(2)}) collective-permute-start(bf16[64,1152]{1,0:T(8,128)(2,1)S(1)} %get-tuple-element.61), channel_id=1, source_target_pairs={{0,256},{16,272},{32,288},{48,304},{64,320},{80,336},{96,352},{112... | collective-permute-start | bytes 442376 | tf_op jit(solution)/shard_map/ppermute | solution.py:276
  20.5 2.1 %convolution_convert_fusion = bf16[256,4096]{1,0:T(8,128)(2,1)} fusion(bf16[128,2048]{1,0:T(8,128)(2,1)S(1)} %multiply_convert_fusion, bf16[128,2048]{1,0:T(8,128)(2,1)S(1)} %copy-done.5, s32[128]{0:T(128)S(1)} %fusion.6), kind=kOutput, calls=%fused_computation | convolution fusion | flops 271613952 | bytes 3146240 | tf_op jit(solution)/shard_map/dot_general | solution.py:301
  22.5 11.4 %collective-permute-done = bf16[64,1152]{1,0:T(8,128)(2,1)S(1)} collective-permute-done((bf16[64,1152]{1,0:T(8,128)(2,1)S(1)}, bf16[64,1152]{1,0:T(8,128)(2,1)S(1)}, u32[]{:S(2)}, u32[]{:S(2)}) %collective-permute-start) | collective-permute-done | bytes 147488 | tf_op jit(solution)/shard_map/ppermute | solution.py:276
  34.7 7.0 %all-to-all-start.1 = ((bf16[32,8,4096]{2,1,0:T(8,128)(2,1)}), bf16[32,8,4096]{2,1,0:T(8,128)(2,1)S(1)}, u32[]{:S(2)}, u32[]{:S(2)}) async-start(bf16[32,8,4096]{2,1,0:T(8,128)(2,1)} %bitcast.37), calls=%async_computation.1 | async-start | bytes 4194304 | tf_op jit(solution)/shard_map/all_to_all | solution.py:304
  41.9 5.2 %collective-permute-start.1 = (bf16[256,256]{1,0:T(8,128)(2,1)S(1)}, bf16[256,256]{1,0:T(8,128)(2,1)S(1)}, u32[]{:S(2)}, u32[]{:S(2)}) collective-permute-start(bf16[256,256]{1,0:T(8,128)(2,1)S(1)} %slice.41), channel_id=1, source_target_pairs={{0,32},{16,48},{32,64},{48,80},{64,96},{80,112},{96,128},{112,144}... | collective-permute-start | bytes 393224 | tf_op jit(solution)/shard_map/ppermute | solution.py:321
  47.0 8.5 %collective-permute-start.5 = (bf16[256,256]{1,0:T(8,128)(2,1)S(1)}, bf16[256,256]{1,0:T(8,128)(2,1)S(1)}, u32[]{:S(2)}, u32[]{:S(2)}) collective-permute-start(bf16[256,256]{1,0:T(8,128)(2,1)S(1)} %slice.41), channel_id=1, source_target_pairs={{0,224},{16,240},{32,0},{48,16},{64,32},{80,48},{96,64},{112,80},{... | collective-permute-start | bytes 393224 | tf_op jit(solution)/shard_map/ppermute | solution.py:323
  55.6 2.0 %collective-permute-done.1.refs_0_ = bf16[256,256]{1,0:T(8,128)(2,1)S(1)} collective-permute-done((bf16[256,256]{1,0:T(8,128)(2,1)S(1)}, bf16[256,256]{1,0:T(8,128)(2,1)S(1)}, u32[]{:S(2)}, u32[]{:S(2)}) %collective-permute-start.1) | collective-permute-done | bytes 131104 | tf_op jit(solution)/shard_map/ppermute | solution.py:321
  57.6 1.9 %collective-permute-start.2 = (bf16[256,256]{1,0:T(8,128)(2,1)S(1)}, bf16[256,256]{1,0:T(8,128)(2,1)S(1)}, u32[]{:S(2)}, u32[]{:S(2)}) collective-permute-start(bf16[256,256]{1,0:T(8,128)(2,1)S(1)} %collective-permute-done.1.refs_0_), channel_id=1, source_target_pairs={{0,32},{16,48},{32,64},{48,80},{64,96},{80,112},{96,128},{112,144}... | collective-permute-start | bytes 393224 | tf_op jit(solution)/shard_map/ppermute | solution.py:321
  59.5 4.7 %collective-permute-done.5.refs_6_ = bf16[256,256]{1,0:T(8,128)(2,1)S(1)} collective-permute-done((bf16[256,256]{1,0:T(8,128)(2,1)S(1)}, bf16[256,256]{1,0:T(8,128)(2,1)S(1)}, u32[]{:S(2)}, u32[]{:S(2)}) %collective-permute-start.5) | collective-permute-done | bytes 131104 | tf_op jit(solution)/shard_map/ppermute | solution.py:323
  64.2 6.8 %collective-permute-start.6 = (bf16[256,256]{1,0:T(8,128)(2,1)S(1)}, bf16[256,256]{1,0:T(8,128)(2,1)S(1)}, u32[]{:S(2)}, u32[]{:S(2)}) collective-permute-start(bf16[256,256]{1,0:T(8,128)(2,1)S(1)} %collective-permute-done.5.refs_6_), channel_id=1, source_target_pairs={{0,224},{16,240},{32,0},{48,16},{64,32},{80,48},{96,64},{112,80},{... | collective-permute-start | bytes 393224 | tf_op jit(solution)/shard_map/ppermute | solution.py:323
  71.1 1.9 %collective-permute-start.3 = (bf16[256,256]{1,0:T(8,128)(2,1)S(1)}, bf16[256,256]{1,0:T(8,128)(2,1)S(1)}, u32[]{:S(2)}, u32[]{:S(2)}) collective-permute-start(bf16[256,256]{1,0:T(8,128)(2,1)S(1)} %collective-permute-done.2.refs_1_), channel_id=1, source_target_pairs={{0,32},{16,48},{32,64},{48,80},{64,96},{80,112},{96,128},{112,144}... | collective-permute-start | bytes 393224 | tf_op jit(solution)/shard_map/ppermute | solution.py:321
  73.0 5.8 %collective-permute-done.6.refs_5_ = bf16[256,256]{1,0:T(8,128)(2,1)S(1)} collective-permute-done((bf16[256,256]{1,0:T(8,128)(2,1)S(1)}, bf16[256,256]{1,0:T(8,128)(2,1)S(1)}, u32[]{:S(2)}, u32[]{:S(2)}) %collective-permute-start.6) | collective-permute-done | bytes 131104 | tf_op jit(solution)/shard_map/ppermute | solution.py:323
  78.8 6.8 %collective-permute-start.7 = (bf16[256,256]{1,0:T(8,128)(2,1)S(1)}, bf16[256,256]{1,0:T(8,128)(2,1)S(1)}, u32[]{:S(2)}, u32[]{:S(2)}) collective-permute-start(bf16[256,256]{1,0:T(8,128)(2,1)S(1)} %collective-permute-done.6.refs_5_), channel_id=1, source_target_pairs={{0,224},{16,240},{32,0},{48,16},{64,32},{80,48},{96,64},{112,80},{... | collective-permute-start | bytes 393224 | tf_op jit(solution)/shard_map/ppermute | solution.py:323
  85.6 1.9 %collective-permute-start.4 = (bf16[256,256]{1,0:T(8,128)(2,1)S(1)}, bf16[256,256]{1,0:T(8,128)(2,1)S(1)}, u32[]{:S(2)}, u32[]{:S(2)}) collective-permute-start(bf16[256,256]{1,0:T(8,128)(2,1)S(1)} %collective-permute-done.3.refs_2_), channel_id=1, source_target_pairs={{0,32},{16,48},{32,64},{48,80},{64,96},{80,112},{96,128},{112,144}... | collective-permute-start | bytes 393224 | tf_op jit(solution)/shard_map/ppermute | solution.py:321
  88.3 4.1 %collective-permute-done.7.refs_4_ = bf16[256,256]{1,0:T(8,128)(2,1)S(1)} collective-permute-done((bf16[256,256]{1,0:T(8,128)(2,1)S(1)}, bf16[256,256]{1,0:T(8,128)(2,1)S(1)}, u32[]{:S(2)}, u32[]{:S(2)}) %collective-permute-start.7) | collective-permute-done | bytes 131104 | tf_op jit(solution)/shard_map/ppermute | solution.py:323
  92.3 6.6 %collective-permute-done.4.refs_3_ = bf16[256,256]{1,0:T(8,128)(2,1)S(1)} collective-permute-done((bf16[256,256]{1,0:T(8,128)(2,1)S(1)}, bf16[256,256]{1,0:T(8,128)(2,1)S(1)}, u32[]{:S(2)}, u32[]{:S(2)}) %collective-permute-start.4) | collective-permute-done | bytes 131104 | tf_op jit(solution)/shard_map/ppermute | solution.py:321
  99.6 7.9 %shard_map.147 = (bf16[64,1024]{1,0:T(8,128)(2,1)}, bf16[64,1024]{1,0:T(8,128)(2,1)}, bf16[64,1024]{1,0:T(8,128)(2,1)}, bf16[64,1024]{1,0:T(8,128)(2,1)}, bf16[8,256,256]{2,1,0:T(8,128)(2,1)}) custom-call(s32[2,8]{1,0:T(2,128)} %lengths_ref.1, s32[3]{0:T(128)} %pad_add_fusion.place_ref, bf16[256,2304]{1,0:T(8,128)(2,1)} %bitcast.39, ...), custom_call_target="tpu_custom_call" | custom-call | flops 1000000 | bytes 10000 | tf_op jit(solution)/shard_map/pallas_call | solution.py:146
  107.5 24.5 %all-gather.3.cloned.1.call-done = bf16[32,64,1152]{2,1,0:T(8,128)(2,1)} async-done(((bf16[2,64,1152]{2,1,0:T(8,128)(2,1)}), bf16[32,64,1152]{2,1,0:T(8,128)(2,1)}) %all-gather.3.cloned.1.call-update) | async-done | bytes 4718608 | tf_op jit(solution)/shard_map/all_gather | solution.py:315
  132.1 2.3 %copy-done = bf16[32,64,1152]{2,1,0:T(8,128)(2,1)S(1)} copy-done((bf16[32,64,1152]{2,1,0:T(8,128)(2,1)S(1)}, bf16[32,64,1152]{2,1,0:T(8,128)(2,1)}, u32[]{:S(2)}) %copy-start) | copy-done | bytes 4718616
  134.4 4.3 %shard_map.149 = bf16[256,2048]{1,0:T(8,128)(2,1)} custom-call(s32[3]{0:T(128)S(1)} %copy-done.2, bf16[256,4096]{1,0:T(8,128)(2,1)S(1)} %bitcast.35, bf16[16,2,64,1152]{3,2,1,0:T(8,128)(2,1)S(1)} %bitcast.36), custom_call_target="tpu_custom_call" | custom-call | flops 2000000000 | bytes 8000000 | tf_op jit(solution)/shard_map/pallas_call | solution.py:243
  138.7 7.8 %all-to-all-start.2 = ((bf16[32,8,2048]{2,1,0:T(8,128)(2,1)}), bf16[32,8,2048]{2,1,0:T(8,128)(2,1)S(1)}, u32[]{:S(2)}, u32[]{:S(2)}) async-start(bf16[32,8,2048]{2,1,0:T(8,128)(2,1)} %bitcast.18), calls=%async_computation.3 | async-start | bytes 2097152 | tf_op jit(solution)/shard_map/all_to_all | solution.py:304
  146.6 3.1 %collective-permute-start.8 = (bf16[64,1024]{1,0:T(8,128)(2,1)S(1)}, bf16[64,1024]{1,0:T(8,128)(2,1)S(1)}, u32[]{:S(2)}, u32[]{:S(2)}) collective-permute-start(bf16[64,1024]{1,0:T(8,128)(2,1)S(1)} %copy-done.22), channel_id=1, source_target_pairs={{0,16},{16,0},{32,48},{48,32},{64,80},{80,64},{96,112},{112,96},{1... | collective-permute-start | bytes 393224 | tf_op jit(solution)/shard_map/ppermute | solution.py:201
  149.7 3.4 %collective-permute-start.9 = (bf16[64,1024]{1,0:T(8,128)(2,1)S(1)}, bf16[64,1024]{1,0:T(8,128)(2,1)S(1)}, u32[]{:S(2)}, u32[]{:S(2)}) collective-permute-start(bf16[64,1024]{1,0:T(8,128)(2,1)S(1)} %copy-done.21), channel_id=1, source_target_pairs={{0,256},{16,272},{32,288},{48,304},{64,320},{80,336},{96,352},{112... | collective-permute-start | bytes 393224 | tf_op jit(solution)/shard_map/ppermute | solution.py:201
  153.1 2.7 %collective-permute-start.10 = (bf16[64,1024]{1,0:T(8,128)(2,1)S(1)}, bf16[64,1024]{1,0:T(8,128)(2,1)S(1)}, u32[]{:S(2)}, u32[]{:S(2)}) collective-permute-start(bf16[64,1024]{1,0:T(8,128)(2,1)S(1)} %copy-done.20), channel_id=1, source_target_pairs={{0,272},{16,256},{32,304},{48,288},{64,336},{80,320},{96,368},{112... | collective-permute-start | bytes 393224 | tf_op jit(solution)/shard_map/ppermute | solution.py:201
  155.8 4.2 %collective-permute-done.8.refs_1_ = bf16[64,1024]{1,0:T(8,128)(2,1)S(1)} collective-permute-done((bf16[64,1024]{1,0:T(8,128)(2,1)S(1)}, bf16[64,1024]{1,0:T(8,128)(2,1)S(1)}, u32[]{:S(2)}, u32[]{:S(2)}) %collective-permute-start.8) | collective-permute-done | bytes 131104 | tf_op jit(solution)/shard_map/ppermute | solution.py:201
  160.1 5.4 %collective-permute-done.9.refs_2_ = bf16[64,1024]{1,0:T(8,128)(2,1)S(1)} collective-permute-done((bf16[64,1024]{1,0:T(8,128)(2,1)S(1)}, bf16[64,1024]{1,0:T(8,128)(2,1)S(1)}, u32[]{:S(2)}, u32[]{:S(2)}) %collective-permute-start.9) | collective-permute-done | bytes 131104 | tf_op jit(solution)/shard_map/ppermute | solution.py:201
  166.6 1.4 shard_map.148
  168.0 2.4 %reduce-scatter.2.cloned.1.call-done = bf16[256,256]{1,0:T(8,128)(2,1)} async-done(((bf16[2048,256]{1,0:T(8,128)(2,1)}), bf16[256,256]{1,0:T(8,128)(2,1)}) %reduce-scatter.2.cloned.1.call-update) | async-done | bytes 131088 | tf_op jit(solution)/shard_map/reduce_scatter | solution.py:326
  170.4 3.5 %all-to-all-start.3 = ((bf16[4,64,256]{2,1,0:T(8,128)(2,1)}), bf16[4,64,256]{2,1,0:T(8,128)(2,1)S(1)}, u32[]{:S(2)}, u32[]{:S(2)}) async-start(bf16[4,64,256]{2,1,0:T(8,128)(2,1)} %bitcast.48), calls=%async_computation.4 | async-start | bytes 262144 | tf_op jit(solution)/shard_map/all_to_all | solution.py:339
  173.9 1.1 convolution_convert_fusion.1
  175.0 3.9 %all-to-all-done.3 = bf16[4,64,256]{2,1,0:T(8,128)(2,1)S(1)} async-done(((bf16[4,64,256]{2,1,0:T(8,128)(2,1)}), bf16[4,64,256]{2,1,0:T(8,128)(2,1)S(1)}, u32[]{:S(2)}, u32[]{:S(2)}) %all-to-all-start.3) | async-done | bytes 131104 | tf_op jit(solution)/shard_map/all_to_all | solution.py:339
  (75 shorter events, 8.1 us)
Async XLA Ops:
  10.4 9.4 %copy-start.18 = (s32[128]{0:T(128)S(1)}, s32[128]{0:T(128)}, u32[]{:S(2)}) copy-start(s32[128]{0:T(128)} %param.19) | copy-start | bytes 1540
  11.6 8.7 %copy-start.4 = (bf16[128,2048]{1,0:T(8,128)(2,1)S(1)}, bf16[128,2048]{1,0:T(8,128)(2,1)}, u32[]{:S(2)}) copy-start(bf16[128,2048]{1,0:T(8,128)(2,1)} %param.18) | copy-start | bytes 1572868
  11.6 8.7 %copy-start.19 = (f32[128]{0:T(128)S(1)}, f32[128]{0:T(128)}, u32[]{:S(2)}) copy-start(f32[128]{0:T(128)} %param.20) | copy-start | bytes 1540
  11.6 8.9 %copy-start.5 = (bf16[128,2048]{1,0:T(8,128)(2,1)S(1)}, bf16[128,2048]{1,0:T(8,128)(2,1)}, u32[]{:S(2)}) copy-start(bf16[128,2048]{1,0:T(8,128)(2,1)} %param.17) | copy-start | bytes 1572868
  11.6 23.2 %all-to-all-start = ((bf16[4,64,2304]{2,1,0:T(8,128)(2,1)}), bf16[4,64,2304]{2,1,0:T(8,128)(2,1)S(1)}, u32[]{:S(2)}, u32[]{:S(2)}) async-start(bf16[4,64,2304]{2,1,0:T(8,128)(2,1)} %pad_maximum_fusion), calls=%async_computation | async-start | bytes 2359296 | tf_op jit(solution)/shard_map/all_to_all | solution.py:284
  15.8 116.3 %all-gather.3.cloned.1.call-start = ((), (), s32[]{:S(2)}) async-start(), calls=%async_computation.6 | async-start | bytes 5013504 | tf_op jit(solution)/shard_map/all_gather | solution.py:315
  15.9 18.1 %collective-permute-start = (bf16[64,1152]{1,0:T(8,128)(2,1)S(1)}, bf16[64,1152]{1,0:T(8,128)(2,1)S(1)}, u32[]{:S(2)}, u32[]{:S(2)}) collective-permute-start(bf16[64,1152]{1,0:T(8,128)(2,1)S(1)} %get-tuple-element.61), channel_id=1, source_target_pairs={{0,256},{16,272},{32,288},{48,304},{64,320},{80,336},{96,352},{112... | collective-permute-start | bytes 442376 | tf_op jit(solution)/shard_map/ppermute | solution.py:276
  34.7 7.1 %copy-start.3 = (bf16[4,64,2304]{2,1,0:T(8,128)(2,1)}, bf16[4,64,2304]{2,1,0:T(8,128)(2,1)S(1)}, u32[]{:S(2)}) copy-start(bf16[4,64,2304]{2,1,0:T(8,128)(2,1)S(1)} %all-to-all-done) | copy-start | bytes 3538948
  34.7 64.2 %all-to-all-start.1 = ((bf16[32,8,4096]{2,1,0:T(8,128)(2,1)}), bf16[32,8,4096]{2,1,0:T(8,128)(2,1)S(1)}, u32[]{:S(2)}, u32[]{:S(2)}) async-start(bf16[32,8,4096]{2,1,0:T(8,128)(2,1)} %bitcast.37), calls=%async_computation.1 | async-start | bytes 4194304 | tf_op jit(solution)/shard_map/all_to_all | solution.py:304
  41.8 128.6 %reduce-scatter.2.cloned.1.call-start = ((), (), s32[]{:S(2)}) async-start(), calls=%async_computation.5 | async-start | bytes 1179648 | tf_op jit(solution)/shard_map/reduce_scatter | solution.py:326
  41.9 15.7 %collective-permute-start.1 = (bf16[256,256]{1,0:T(8,128)(2,1)S(1)}, bf16[256,256]{1,0:T(8,128)(2,1)S(1)}, u32[]{:S(2)}, u32[]{:S(2)}) collective-permute-start(bf16[256,256]{1,0:T(8,128)(2,1)S(1)} %slice.41), channel_id=1, source_target_pairs={{0,32},{16,48},{32,64},{48,80},{64,96},{80,112},{96,128},{112,144}... | collective-permute-start | bytes 393224 | tf_op jit(solution)/shard_map/ppermute | solution.py:321
  47.0 17.2 %collective-permute-start.5 = (bf16[256,256]{1,0:T(8,128)(2,1)S(1)}, bf16[256,256]{1,0:T(8,128)(2,1)S(1)}, u32[]{:S(2)}, u32[]{:S(2)}) collective-permute-start(bf16[256,256]{1,0:T(8,128)(2,1)S(1)} %slice.41), channel_id=1, source_target_pairs={{0,224},{16,240},{32,0},{48,16},{64,32},{80,48},{96,64},{112,80},{... | collective-permute-start | bytes 393224 | tf_op jit(solution)/shard_map/ppermute | solution.py:323
  57.6 41.3 %copy-start.6 = (bf16[256,256]{1,0:T(8,128)(2,1)}, bf16[256,256]{1,0:T(8,128)(2,1)S(1)}, u32[]{:S(2)}) copy-start(bf16[256,256]{1,0:T(8,128)(2,1)S(1)} %collective-permute-done.1.refs_0_) | copy-start | bytes 393220
  57.6 13.5 %collective-permute-start.2 = (bf16[256,256]{1,0:T(8,128)(2,1)S(1)}, bf16[256,256]{1,0:T(8,128)(2,1)S(1)}, u32[]{:S(2)}, u32[]{:S(2)}) collective-permute-start(bf16[256,256]{1,0:T(8,128)(2,1)S(1)} %collective-permute-done.1.refs_0_), channel_id=1, source_target_pairs={{0,32},{16,48},{32,64},{48,80},{64,96},{80,112},{96,128},{112,144}... | collective-permute-start | bytes 393224 | tf_op jit(solution)/shard_map/ppermute | solution.py:321
  64.2 34.7 %copy-start.7 = (bf16[256,256]{1,0:T(8,128)(2,1)}, bf16[256,256]{1,0:T(8,128)(2,1)S(1)}, u32[]{:S(2)}) copy-start(bf16[256,256]{1,0:T(8,128)(2,1)S(1)} %collective-permute-done.5.refs_6_) | copy-start | bytes 393220
  64.2 14.5 %collective-permute-start.6 = (bf16[256,256]{1,0:T(8,128)(2,1)S(1)}, bf16[256,256]{1,0:T(8,128)(2,1)S(1)}, u32[]{:S(2)}, u32[]{:S(2)}) collective-permute-start(bf16[256,256]{1,0:T(8,128)(2,1)S(1)} %collective-permute-done.5.refs_6_), channel_id=1, source_target_pairs={{0,224},{16,240},{32,0},{48,16},{64,32},{80,48},{96,64},{112,80},{... | collective-permute-start | bytes 393224 | tf_op jit(solution)/shard_map/ppermute | solution.py:323
  71.1 27.9 %copy-start.8 = (bf16[256,256]{1,0:T(8,128)(2,1)}, bf16[256,256]{1,0:T(8,128)(2,1)S(1)}, u32[]{:S(2)}) copy-start(bf16[256,256]{1,0:T(8,128)(2,1)S(1)} %collective-permute-done.2.refs_1_) | copy-start | bytes 393220
  71.1 14.5 %collective-permute-start.3 = (bf16[256,256]{1,0:T(8,128)(2,1)S(1)}, bf16[256,256]{1,0:T(8,128)(2,1)S(1)}, u32[]{:S(2)}, u32[]{:S(2)}) collective-permute-start(bf16[256,256]{1,0:T(8,128)(2,1)S(1)} %collective-permute-done.2.refs_1_), channel_id=1, source_target_pairs={{0,32},{16,48},{32,64},{48,80},{64,96},{80,112},{96,128},{112,144}... | collective-permute-start | bytes 393224 | tf_op jit(solution)/shard_map/ppermute | solution.py:321
  78.8 20.2 %copy-start.9 = (bf16[256,256]{1,0:T(8,128)(2,1)}, bf16[256,256]{1,0:T(8,128)(2,1)S(1)}, u32[]{:S(2)}) copy-start(bf16[256,256]{1,0:T(8,128)(2,1)S(1)} %collective-permute-done.6.refs_5_) | copy-start | bytes 393220
  78.8 13.6 %collective-permute-start.7 = (bf16[256,256]{1,0:T(8,128)(2,1)S(1)}, bf16[256,256]{1,0:T(8,128)(2,1)S(1)}, u32[]{:S(2)}, u32[]{:S(2)}) collective-permute-start(bf16[256,256]{1,0:T(8,128)(2,1)S(1)} %collective-permute-done.6.refs_5_), channel_id=1, source_target_pairs={{0,224},{16,240},{32,0},{48,16},{64,32},{80,48},{96,64},{112,80},{... | collective-permute-start | bytes 393224 | tf_op jit(solution)/shard_map/ppermute | solution.py:323
  85.6 13.4 %copy-start.10 = (bf16[256,256]{1,0:T(8,128)(2,1)}, bf16[256,256]{1,0:T(8,128)(2,1)S(1)}, u32[]{:S(2)}) copy-start(bf16[256,256]{1,0:T(8,128)(2,1)S(1)} %collective-permute-done.3.refs_2_) | copy-start | bytes 393220
  85.6 13.3 %collective-permute-start.4 = (bf16[256,256]{1,0:T(8,128)(2,1)S(1)}, bf16[256,256]{1,0:T(8,128)(2,1)S(1)}, u32[]{:S(2)}, u32[]{:S(2)}) collective-permute-start(bf16[256,256]{1,0:T(8,128)(2,1)S(1)} %collective-permute-done.3.refs_2_), channel_id=1, source_target_pairs={{0,32},{16,48},{32,64},{48,80},{64,96},{80,112},{96,128},{112,144}... | collective-permute-start | bytes 393224 | tf_op jit(solution)/shard_map/ppermute | solution.py:321
  88.2 43.8 %copy-start.2 = (s32[3]{0:T(128)S(1)}, s32[3]{0:T(128)}, u32[]{:S(2)}) copy-start(s32[3]{0:T(128)} %pad_add_fusion.place_ref) | copy-start | bytes 40
  138.7 7.8 %copy-start.22 = (bf16[64,1024]{1,0:T(8,128)(2,1)S(1)}, bf16[64,1024]{1,0:T(8,128)(2,1)}, u32[]{:S(2)}) copy-start(bf16[64,1024]{1,0:T(8,128)(2,1)} %get-tuple-element.48) | copy-start | bytes 393220
  138.7 11.0 %copy-start.21 = (bf16[64,1024]{1,0:T(8,128)(2,1)S(1)}, bf16[64,1024]{1,0:T(8,128)(2,1)}, u32[]{:S(2)}) copy-start(bf16[64,1024]{1,0:T(8,128)(2,1)} %get-tuple-element.49) | copy-start | bytes 393220
  138.7 14.4 %copy-start.20 = (bf16[64,1024]{1,0:T(8,128)(2,1)S(1)}, bf16[64,1024]{1,0:T(8,128)(2,1)}, u32[]{:S(2)}) copy-start(bf16[64,1024]{1,0:T(8,128)(2,1)} %get-tuple-element.50) | copy-start | bytes 393220
  138.7 27.9 %copy-start.1 = (bf16[64,1024]{1,0:T(8,128)(2,1)S(1)}, bf16[64,1024]{1,0:T(8,128)(2,1)}, u32[]{:S(2)}) copy-start(bf16[64,1024]{1,0:T(8,128)(2,1)} %get-tuple-element.47.refs_0_) | copy-start | bytes 393220
  138.7 31.6 %all-to-all-start.2 = ((bf16[32,8,2048]{2,1,0:T(8,128)(2,1)}), bf16[32,8,2048]{2,1,0:T(8,128)(2,1)S(1)}, u32[]{:S(2)}, u32[]{:S(2)}) async-start(bf16[32,8,2048]{2,1,0:T(8,128)(2,1)} %bitcast.18), calls=%async_computation.3 | async-start | bytes 2097152 | tf_op jit(solution)/shard_map/all_to_all | solution.py:304
  146.6 13.5 %collective-permute-start.8 = (bf16[64,1024]{1,0:T(8,128)(2,1)S(1)}, bf16[64,1024]{1,0:T(8,128)(2,1)S(1)}, u32[]{:S(2)}, u32[]{:S(2)}) collective-permute-start(bf16[64,1024]{1,0:T(8,128)(2,1)S(1)} %copy-done.22), channel_id=1, source_target_pairs={{0,16},{16,0},{32,48},{48,32},{64,80},{80,64},{96,112},{112,96},{1... | collective-permute-start | bytes 393224 | tf_op jit(solution)/shard_map/ppermute | solution.py:201
  149.7 15.8 %collective-permute-start.9 = (bf16[64,1024]{1,0:T(8,128)(2,1)S(1)}, bf16[64,1024]{1,0:T(8,128)(2,1)S(1)}, u32[]{:S(2)}, u32[]{:S(2)}) collective-permute-start(bf16[64,1024]{1,0:T(8,128)(2,1)S(1)} %copy-done.21), channel_id=1, source_target_pairs={{0,256},{16,272},{32,288},{48,304},{64,320},{80,336},{96,352},{112... | collective-permute-start | bytes 393224 | tf_op jit(solution)/shard_map/ppermute | solution.py:201
  153.1 13.4 %collective-permute-start.10 = (bf16[64,1024]{1,0:T(8,128)(2,1)S(1)}, bf16[64,1024]{1,0:T(8,128)(2,1)S(1)}, u32[]{:S(2)}, u32[]{:S(2)}) collective-permute-start(bf16[64,1024]{1,0:T(8,128)(2,1)S(1)} %copy-done.20), channel_id=1, source_target_pairs={{0,272},{16,256},{32,304},{48,288},{64,336},{80,320},{96,368},{112... | collective-permute-start | bytes 393224 | tf_op jit(solution)/shard_map/ppermute | solution.py:201
  170.4 8.5 %all-to-all-start.3 = ((bf16[4,64,256]{2,1,0:T(8,128)(2,1)}), bf16[4,64,256]{2,1,0:T(8,128)(2,1)S(1)}, u32[]{:S(2)}, u32[]{:S(2)}) async-start(bf16[4,64,256]{2,1,0:T(8,128)(2,1)} %bitcast.48), calls=%async_computation.4 | async-start | bytes 262144 | tf_op jit(solution)/shard_map/all_to_all | solution.py:339
  (8 other events, 30.4 us)
Sparse Core Ops, SparseCore 0:
  34.9 97.1 all-gather.2
Sparse Core Ops, SparseCore 1:
  107.6 62.7 reduce-scatter.1

commit v5 on v4

--- a/solution.py
+++ b/solution.py
@@ -71,31 +71,38 @@
         lane = lax.broadcasted_iota(jnp.int32, (1, LANES), 1)
         position = first + lane % BLOCK
         begin = jnp.zeros((1, LANES), jnp.int32)
-        low = jnp.int32(0)
+        low = high = jnp.int32(0)
         for start in starts:
             begin = jnp.where(position >= start, start, begin)
             low = jnp.where(first >= start, start, low)
+            high = jnp.where(first + BLOCK - 1 >= start, start, high)
         low_block = low // BLOCK
         count = query_block - low_block + 1
+        inner = jnp.minimum((high + BLOCK - 1) // BLOCK - low_block, count - 1)
 
         def tile(i):
             block = low_block + i
             return (ring - block) & (RING - 1), pl.multiple_of((block // RING) * BLOCK, BLOCK), block
 
-        def score_step(i, highest):
+        def score_step(masked, i, highest):
             slot, offset, block = tile(i)
             keys = kv_ref[slot, pl.ds(offset, BLOCK), 0:WIDTH]
             values = kv_ref[slot, pl.ds(offset, BLOCK), WIDTH : 2 * WIDTH]
             scores = lax.dot_general(keys, q_rows[...], NT, preferred_element_type=jnp.float32)
-            at = block * BLOCK + lax.broadcasted_iota(jnp.int32, (BLOCK, LANES), 0)
-            scores = jnp.where((at >= begin) & (at <= position), scores, -1e30)
+            if masked:
+                at = block * BLOCK + lax.broadcasted_iota(jnp.int32, (BLOCK, LANES), 0)
+                scores = jnp.where((at >= begin) & (at <= position), scores, -1e30)
             prob[i] = scores
             dprob[i] = lax.dot_general(
                 values, g_rows[...], NT, preferred_element_type=jnp.float32
             )
             return jnp.maximum(highest, jnp.max(scores, axis=0, keepdims=True))
 
-        highest = lax.fori_loop(0, count, score_step, jnp.full((1, LANES), -1e30, jnp.float32))
+        highest = jnp.full((1, LANES), -1e30, jnp.float32)
+        edge, whole = functools.partial(score_step, True), functools.partial(score_step, False)
+        highest = lax.fori_loop(0, inner, edge, highest)
+        highest = lax.fori_loop(inner, count - 1, whole, highest)
+        highest = edge(count - 1, highest)
 
         def sum_step(i, carry):
             total, weighted = carry

time: 187 us -> 186 us (level)
  Pallas kernels: 13.6 us -> 11 us
    all_gather x1, waiting for transfers between devices: 24.5 us -> 27.1 us  [local(): weights = lax.all_gather(pair, 'ctx', axis_index_groups=Z_LINES)]
    pallas_call x1, Pallas kernels: 7.93 us -> 5.34 us  [attention(): pl.pallas_call(attention_kernel, out_shape=(*[jax.ShapeDtypeStruct((PIECE...]
  transfers between devices with their start and end apart: 17 -> 17, of which waited for: 12 -> 11; matrix products, arithmetic and copies ran while one was open for 3% -> 3% of each run, Pallas kernels for 7% -> 6%
where the time goes in v5:
time: 186 us; the launch traced here: 184 us
  waiting for transfers between devices  76.4 us (41%)
  starting transfers between devices  68.7 us (37%)
  between operations  16 us (9%)
  Pallas kernels  11 us (6%)
  local copies, waits for them, and re-layouts  5.92 us (3%)
  other arithmetic  3.26 us (2%)
  matrix products  3.2 us (2%)
    all_gather x1, waiting for transfers between devices, local(): weights = lax.all_gather(pair, 'ctx', axis_index_groups=Z_LINES)  27.1 us
    ppermute x3, starting transfers between devices, local(): down = kv[RING - step] = lax.ppermute(down, 'ctx', z_shift(-2))  22.2 us
    all_to_all x2, starting transfers between devices, over_plane(): lax.all_to_all(array.reshape(2 * rounds, half, -1), ('ctx', 'exp'), 0, 0,...  14.9 us
    ppermute x3, waiting for transfers between devices, local(): down = kv[RING - step] = lax.ppermute(down, 'ctx', z_shift(-2))  14.6 us
    ppermute x1, waiting for transfers between devices, local(): other = lax.ppermute(shard, 'ctx', member_swap(2))  11.4 us
    ppermute x4, starting transfers between devices, local(): up = kv[step] = lax.ppermute(up, 'ctx', z_shift(2))  10.9 us
    ppermute x3, waiting for transfers between devices, swap(): lax.ppermute(pieces[step], 'ctx', member_swap(step))  10.2 us
    ppermute x3, starting transfers between devices, swap(): lax.ppermute(pieces[step], 'ctx', member_swap(step))  9.21 us
  transfers between devices with their start and end apart: 17, of which 11 were waited for; matrix products, arithmetic and copies ran while one was open for 3% of the time, Pallas kernels for 6%

profile of v5, /device:TPU:24, one launch (start us, length us, event | category | flops | bytes accessed | tf_op | source)
XLA Modules:
  0.0 184.5 jit_solution(15784368055335206849)
XLA Ops:
  10.4 1.1 pad_maximum_fusion
  11.6 4.2 %all-to-all-start = ((bf16[4,64,2304]{2,1,0:T(8,128)(2,1)}), bf16[4,64,2304]{2,1,0:T(8,128)(2,1)S(1)}, u32[]{:S(2)}, u32[]{:S(2)}) async-start(bf16[4,64,2304]{2,1,0:T(8,128)(2,1)} %pad_maximum_fusion), calls=%async_computation | async-start | bytes 2359296 | tf_op jit(solution)/shard_map/all_to_all | solution.py:291
  15.9 3.9 %collective-permute-start = (bf16[64,1152]{1,0:T(8,128)(2,1)S(1)}, bf16[64,1152]{1,0:T(8,128)(2,1)S(1)}, u32[]{:S(2)}, u32[]{:S(2)}) collective-permute-start(bf16[64,1152]{1,0:T(8,128)(2,1)S(1)} %get-tuple-element.61), channel_id=1, source_target_pairs={{0,256},{16,272},{32,288},{48,304},{64,320},{80,336},{96,352},{112... | collective-permute-start | bytes 442376 | tf_op jit(solution)/shard_map/ppermute | solution.py:283
  20.5 2.1 %convolution_convert_fusion = bf16[256,4096]{1,0:T(8,128)(2,1)} fusion(bf16[128,2048]{1,0:T(8,128)(2,1)S(1)} %multiply_convert_fusion, bf16[128,2048]{1,0:T(8,128)(2,1)S(1)} %copy-done.5, s32[128]{0:T(128)S(1)} %fusion.6), kind=kOutput, calls=%fused_computation | convolution fusion | flops 271613952 | bytes 3146240 | tf_op jit(solution)/shard_map/dot_general | solution.py:308
  22.5 11.4 %collective-permute-done = bf16[64,1152]{1,0:T(8,128)(2,1)S(1)} collective-permute-done((bf16[64,1152]{1,0:T(8,128)(2,1)S(1)}, bf16[64,1152]{1,0:T(8,128)(2,1)S(1)}, u32[]{:S(2)}, u32[]{:S(2)}) %collective-permute-start) | collective-permute-done | bytes 147488 | tf_op jit(solution)/shard_map/ppermute | solution.py:283
  34.7 7.0 %all-to-all-start.1 = ((bf16[32,8,4096]{2,1,0:T(8,128)(2,1)}), bf16[32,8,4096]{2,1,0:T(8,128)(2,1)S(1)}, u32[]{:S(2)}, u32[]{:S(2)}) async-start(bf16[32,8,4096]{2,1,0:T(8,128)(2,1)} %bitcast.37), calls=%async_computation.1 | async-start | bytes 4194304 | tf_op jit(solution)/shard_map/all_to_all | solution.py:311
  41.9 5.2 %collective-permute-start.1 = (bf16[256,256]{1,0:T(8,128)(2,1)S(1)}, bf16[256,256]{1,0:T(8,128)(2,1)S(1)}, u32[]{:S(2)}, u32[]{:S(2)}) collective-permute-start(bf16[256,256]{1,0:T(8,128)(2,1)S(1)} %slice.41), channel_id=1, source_target_pairs={{0,32},{16,48},{32,64},{48,80},{64,96},{80,112},{96,128},{112,144}... | collective-permute-start | bytes 393224 | tf_op jit(solution)/shard_map/ppermute | solution.py:328
  47.0 8.5 %collective-permute-start.5 = (bf16[256,256]{1,0:T(8,128)(2,1)S(1)}, bf16[256,256]{1,0:T(8,128)(2,1)S(1)}, u32[]{:S(2)}, u32[]{:S(2)}) collective-permute-start(bf16[256,256]{1,0:T(8,128)(2,1)S(1)} %slice.41), channel_id=1, source_target_pairs={{0,224},{16,240},{32,0},{48,16},{64,32},{80,48},{96,64},{112,80},{... | collective-permute-start | bytes 393224 | tf_op jit(solution)/shard_map/ppermute | solution.py:330
  55.6 2.0 %collective-permute-done.1.refs_0_ = bf16[256,256]{1,0:T(8,128)(2,1)S(1)} collective-permute-done((bf16[256,256]{1,0:T(8,128)(2,1)S(1)}, bf16[256,256]{1,0:T(8,128)(2,1)S(1)}, u32[]{:S(2)}, u32[]{:S(2)}) %collective-permute-start.1) | collective-permute-done | bytes 131104 | tf_op jit(solution)/shard_map/ppermute | solution.py:328
  57.6 1.9 %collective-permute-start.2 = (bf16[256,256]{1,0:T(8,128)(2,1)S(1)}, bf16[256,256]{1,0:T(8,128)(2,1)S(1)}, u32[]{:S(2)}, u32[]{:S(2)}) collective-permute-start(bf16[256,256]{1,0:T(8,128)(2,1)S(1)} %collective-permute-done.1.refs_0_), channel_id=1, source_target_pairs={{0,32},{16,48},{32,64},{48,80},{64,96},{80,112},{96,128},{112,144}... | collective-permute-start | bytes 393224 | tf_op jit(solution)/shard_map/ppermute | solution.py:328
  59.5 4.7 %collective-permute-done.5.refs_6_ = bf16[256,256]{1,0:T(8,128)(2,1)S(1)} collective-permute-done((bf16[256,256]{1,0:T(8,128)(2,1)S(1)}, bf16[256,256]{1,0:T(8,128)(2,1)S(1)}, u32[]{:S(2)}, u32[]{:S(2)}) %collective-permute-start.5) | collective-permute-done | bytes 131104 | tf_op jit(solution)/shard_map/ppermute | solution.py:330
  64.2 6.8 %collective-permute-start.6 = (bf16[256,256]{1,0:T(8,128)(2,1)S(1)}, bf16[256,256]{1,0:T(8,128)(2,1)S(1)}, u32[]{:S(2)}, u32[]{:S(2)}) collective-permute-start(bf16[256,256]{1,0:T(8,128)(2,1)S(1)} %collective-permute-done.5.refs_6_), channel_id=1, source_target_pairs={{0,224},{16,240},{32,0},{48,16},{64,32},{80,48},{96,64},{112,80},{... | collective-permute-start | bytes 393224 | tf_op jit(solution)/shard_map/ppermute | solution.py:330
  71.1 1.9 %collective-permute-start.3 = (bf16[256,256]{1,0:T(8,128)(2,1)S(1)}, bf16[256,256]{1,0:T(8,128)(2,1)S(1)}, u32[]{:S(2)}, u32[]{:S(2)}) collective-permute-start(bf16[256,256]{1,0:T(8,128)(2,1)S(1)} %collective-permute-done.2.refs_1_), channel_id=1, source_target_pairs={{0,32},{16,48},{32,64},{48,80},{64,96},{80,112},{96,128},{112,144}... | collective-permute-start | bytes 393224 | tf_op jit(solution)/shard_map/ppermute | solution.py:328
  73.0 5.8 %collective-permute-done.6.refs_5_ = bf16[256,256]{1,0:T(8,128)(2,1)S(1)} collective-permute-done((bf16[256,256]{1,0:T(8,128)(2,1)S(1)}, bf16[256,256]{1,0:T(8,128)(2,1)S(1)}, u32[]{:S(2)}, u32[]{:S(2)}) %collective-permute-start.6) | collective-permute-done | bytes 131104 | tf_op jit(solution)/shard_map/ppermute | solution.py:330
  78.8 6.8 %collective-permute-start.7 = (bf16[256,256]{1,0:T(8,128)(2,1)S(1)}, bf16[256,256]{1,0:T(8,128)(2,1)S(1)}, u32[]{:S(2)}, u32[]{:S(2)}) collective-permute-start(bf16[256,256]{1,0:T(8,128)(2,1)S(1)} %collective-permute-done.6.refs_5_), channel_id=1, source_target_pairs={{0,224},{16,240},{32,0},{48,16},{64,32},{80,48},{96,64},{112,80},{... | collective-permute-start | bytes 393224 | tf_op jit(solution)/shard_map/ppermute | solution.py:330
  85.6 1.9 %collective-permute-start.4 = (bf16[256,256]{1,0:T(8,128)(2,1)S(1)}, bf16[256,256]{1,0:T(8,128)(2,1)S(1)}, u32[]{:S(2)}, u32[]{:S(2)}) collective-permute-start(bf16[256,256]{1,0:T(8,128)(2,1)S(1)} %collective-permute-done.3.refs_2_), channel_id=1, source_target_pairs={{0,32},{16,48},{32,64},{48,80},{64,96},{80,112},{96,128},{112,144}... | collective-permute-start | bytes 393224 | tf_op jit(solution)/shard_map/ppermute | solution.py:328
  88.3 4.1 %collective-permute-done.7.refs_4_ = bf16[256,256]{1,0:T(8,128)(2,1)S(1)} collective-permute-done((bf16[256,256]{1,0:T(8,128)(2,1)S(1)}, bf16[256,256]{1,0:T(8,128)(2,1)S(1)}, u32[]{:S(2)}, u32[]{:S(2)}) %collective-permute-start.7) | collective-permute-done | bytes 131104 | tf_op jit(solution)/shard_map/ppermute | solution.py:330
  92.3 6.6 %collective-permute-done.4.refs_3_ = bf16[256,256]{1,0:T(8,128)(2,1)S(1)} collective-permute-done((bf16[256,256]{1,0:T(8,128)(2,1)S(1)}, bf16[256,256]{1,0:T(8,128)(2,1)S(1)}, u32[]{:S(2)}, u32[]{:S(2)}) %collective-permute-start.4) | collective-permute-done | bytes 131104 | tf_op jit(solution)/shard_map/ppermute | solution.py:328
  99.6 5.3 %shard_map.147 = (bf16[64,1024]{1,0:T(8,128)(2,1)}, bf16[64,1024]{1,0:T(8,128)(2,1)}, bf16[64,1024]{1,0:T(8,128)(2,1)}, bf16[64,1024]{1,0:T(8,128)(2,1)}, bf16[8,256,256]{2,1,0:T(8,128)(2,1)}) custom-call(s32[2,8]{1,0:T(2,128)} %lengths_ref.1, s32[3]{0:T(128)} %pad_add_fusion.place_ref, bf16[256,2304]{1,0:T(8,128)(2,1)} %bitcast.39, ...), custom_call_target="tpu_custom_call" | custom-call | flops 1000000 | bytes 10000 | tf_op jit(solution)/shard_map/pallas_call | solution.py:153
  104.9 27.1 %all-gather.3.cloned.1.call-done = bf16[32,64,1152]{2,1,0:T(8,128)(2,1)} async-done(((bf16[2,64,1152]{2,1,0:T(8,128)(2,1)}), bf16[32,64,1152]{2,1,0:T(8,128)(2,1)}) %all-gather.3.cloned.1.call-update) | async-done | bytes 4718608 | tf_op jit(solution)/shard_map/all_gather | solution.py:322
  132.1 2.3 %copy-done = bf16[32,64,1152]{2,1,0:T(8,128)(2,1)S(1)} copy-done((bf16[32,64,1152]{2,1,0:T(8,128)(2,1)S(1)}, bf16[32,64,1152]{2,1,0:T(8,128)(2,1)}, u32[]{:S(2)}) %copy-start) | copy-done | bytes 4718616
  134.4 4.3 %shard_map.149 = bf16[256,2048]{1,0:T(8,128)(2,1)} custom-call(s32[3]{0:T(128)S(1)} %copy-done.2, bf16[256,4096]{1,0:T(8,128)(2,1)S(1)} %bitcast.35, bf16[16,2,64,1152]{3,2,1,0:T(8,128)(2,1)S(1)} %bitcast.36), custom_call_target="tpu_custom_call" | custom-call | flops 2000000000 | bytes 8000000 | tf_op jit(solution)/shard_map/pallas_call | solution.py:250
  138.7 7.8 %all-to-all-start.2 = ((bf16[32,8,2048]{2,1,0:T(8,128)(2,1)}), bf16[32,8,2048]{2,1,0:T(8,128)(2,1)S(1)}, u32[]{:S(2)}, u32[]{:S(2)}) async-start(bf16[32,8,2048]{2,1,0:T(8,128)(2,1)} %bitcast.18), calls=%async_computation.3 | async-start | bytes 2097152 | tf_op jit(solution)/shard_map/all_to_all | solution.py:311
  146.6 3.1 %collective-permute-start.8 = (bf16[64,1024]{1,0:T(8,128)(2,1)S(1)}, bf16[64,1024]{1,0:T(8,128)(2,1)S(1)}, u32[]{:S(2)}, u32[]{:S(2)}) collective-permute-start(bf16[64,1024]{1,0:T(8,128)(2,1)S(1)} %copy-done.22), channel_id=1, source_target_pairs={{0,16},{16,0},{32,48},{48,32},{64,80},{80,64},{96,112},{112,96},{1... | collective-permute-start | bytes 393224 | tf_op jit(solution)/shard_map/ppermute | solution.py:208
  149.6 3.4 %collective-permute-start.9 = (bf16[64,1024]{1,0:T(8,128)(2,1)S(1)}, bf16[64,1024]{1,0:T(8,128)(2,1)S(1)}, u32[]{:S(2)}, u32[]{:S(2)}) collective-permute-start(bf16[64,1024]{1,0:T(8,128)(2,1)S(1)} %copy-done.21), channel_id=1, source_target_pairs={{0,256},{16,272},{32,288},{48,304},{64,320},{80,336},{96,352},{112... | collective-permute-start | bytes 393224 | tf_op jit(solution)/shard_map/ppermute | solution.py:208
  153.1 2.7 %collective-permute-start.10 = (bf16[64,1024]{1,0:T(8,128)(2,1)S(1)}, bf16[64,1024]{1,0:T(8,128)(2,1)S(1)}, u32[]{:S(2)}, u32[]{:S(2)}) collective-permute-start(bf16[64,1024]{1,0:T(8,128)(2,1)S(1)} %copy-done.20), channel_id=1, source_target_pairs={{0,272},{16,256},{32,304},{48,288},{64,336},{80,320},{96,368},{112... | collective-permute-start | bytes 393224 | tf_op jit(solution)/shard_map/ppermute | solution.py:208
  155.8 4.5 %collective-permute-done.8.refs_1_ = bf16[64,1024]{1,0:T(8,128)(2,1)S(1)} collective-permute-done((bf16[64,1024]{1,0:T(8,128)(2,1)S(1)}, bf16[64,1024]{1,0:T(8,128)(2,1)S(1)}, u32[]{:S(2)}, u32[]{:S(2)}) %collective-permute-start.8) | collective-permute-done | bytes 131104 | tf_op jit(solution)/shard_map/ppermute | solution.py:208
  160.3 5.7 %collective-permute-done.9.refs_2_ = bf16[64,1024]{1,0:T(8,128)(2,1)S(1)} collective-permute-done((bf16[64,1024]{1,0:T(8,128)(2,1)S(1)}, bf16[64,1024]{1,0:T(8,128)(2,1)S(1)}, u32[]{:S(2)}, u32[]{:S(2)}) %collective-permute-start.9) | collective-permute-done | bytes 131104 | tf_op jit(solution)/shard_map/ppermute | solution.py:208
  166.0 1.4 shard_map.148
  168.0 3.3 %all-to-all-start.3 = ((bf16[4,64,256]{2,1,0:T(8,128)(2,1)}), bf16[4,64,256]{2,1,0:T(8,128)(2,1)S(1)}, u32[]{:S(2)}, u32[]{:S(2)}) async-start(bf16[4,64,256]{2,1,0:T(8,128)(2,1)} %bitcast.48), calls=%async_computation.4 | async-start | bytes 262144 | tf_op jit(solution)/shard_map/all_to_all | solution.py:346
  171.3 1.1 convolution_convert_fusion.1
  172.5 3.8 %all-to-all-done.3 = bf16[4,64,256]{2,1,0:T(8,128)(2,1)S(1)} async-done(((bf16[4,64,256]{2,1,0:T(8,128)(2,1)}), bf16[4,64,256]{2,1,0:T(8,128)(2,1)S(1)}, u32[]{:S(2)}, u32[]{:S(2)}) %all-to-all-start.3) | async-done | bytes 131104 | tf_op jit(solution)/shard_map/all_to_all | solution.py:346
  (75 shorter events, 6.4 us)
Async XLA Ops:
  10.4 9.4 %copy-start.18 = (s32[128]{0:T(128)S(1)}, s32[128]{0:T(128)}, u32[]{:S(2)}) copy-start(s32[128]{0:T(128)} %param.19) | copy-start | bytes 1540
  11.6 8.7 %copy-start.4 = (bf16[128,2048]{1,0:T(8,128)(2,1)S(1)}, bf16[128,2048]{1,0:T(8,128)(2,1)}, u32[]{:S(2)}) copy-start(bf16[128,2048]{1,0:T(8,128)(2,1)} %param.18) | copy-start | bytes 1572868
  11.6 8.7 %copy-start.19 = (f32[128]{0:T(128)S(1)}, f32[128]{0:T(128)}, u32[]{:S(2)}) copy-start(f32[128]{0:T(128)} %param.20) | copy-start | bytes 1540
  11.6 8.9 %copy-start.5 = (bf16[128,2048]{1,0:T(8,128)(2,1)S(1)}, bf16[128,2048]{1,0:T(8,128)(2,1)}, u32[]{:S(2)}) copy-start(bf16[128,2048]{1,0:T(8,128)(2,1)} %param.17) | copy-start | bytes 1572868
  11.6 23.2 %all-to-all-start = ((bf16[4,64,2304]{2,1,0:T(8,128)(2,1)}), bf16[4,64,2304]{2,1,0:T(8,128)(2,1)S(1)}, u32[]{:S(2)}, u32[]{:S(2)}) async-start(bf16[4,64,2304]{2,1,0:T(8,128)(2,1)} %pad_maximum_fusion), calls=%async_computation | async-start | bytes 2359296 | tf_op jit(solution)/shard_map/all_to_all | solution.py:291
  15.8 116.3 %all-gather.3.cloned.1.call-start = ((), (), s32[]{:S(2)}) async-start(), calls=%async_computation.6 | async-start | bytes 5013504 | tf_op jit(solution)/shard_map/all_gather | solution.py:322
  15.9 18.1 %collective-permute-start = (bf16[64,1152]{1,0:T(8,128)(2,1)S(1)}, bf16[64,1152]{1,0:T(8,128)(2,1)S(1)}, u32[]{:S(2)}, u32[]{:S(2)}) collective-permute-start(bf16[64,1152]{1,0:T(8,128)(2,1)S(1)} %get-tuple-element.61), channel_id=1, source_target_pairs={{0,256},{16,272},{32,288},{48,304},{64,320},{80,336},{96,352},{112... | collective-permute-start | bytes 442376 | tf_op jit(solution)/shard_map/ppermute | solution.py:283
  34.7 7.1 %copy-start.3 = (bf16[4,64,2304]{2,1,0:T(8,128)(2,1)}, bf16[4,64,2304]{2,1,0:T(8,128)(2,1)S(1)}, u32[]{:S(2)}) copy-start(bf16[4,64,2304]{2,1,0:T(8,128)(2,1)S(1)} %all-to-all-done) | copy-start | bytes 3538948
  34.7 64.2 %all-to-all-start.1 = ((bf16[32,8,4096]{2,1,0:T(8,128)(2,1)}), bf16[32,8,4096]{2,1,0:T(8,128)(2,1)S(1)}, u32[]{:S(2)}, u32[]{:S(2)}) async-start(bf16[32,8,4096]{2,1,0:T(8,128)(2,1)} %bitcast.37), calls=%async_computation.1 | async-start | bytes 4194304 | tf_op jit(solution)/shard_map/all_to_all | solution.py:311
  41.8 126.2 %reduce-scatter.2.cloned.1.call-start = ((), (), s32[]{:S(2)}) async-start(), calls=%async_computation.5 | async-start | bytes 1179648 | tf_op jit(solution)/shard_map/reduce_scatter | solution.py:333
  41.9 15.7 %collective-permute-start.1 = (bf16[256,256]{1,0:T(8,128)(2,1)S(1)}, bf16[256,256]{1,0:T(8,128)(2,1)S(1)}, u32[]{:S(2)}, u32[]{:S(2)}) collective-permute-start(bf16[256,256]{1,0:T(8,128)(2,1)S(1)} %slice.41), channel_id=1, source_target_pairs={{0,32},{16,48},{32,64},{48,80},{64,96},{80,112},{96,128},{112,144}... | collective-permute-start | bytes 393224 | tf_op jit(solution)/shard_map/ppermute | solution.py:328
  47.0 17.2 %collective-permute-start.5 = (bf16[256,256]{1,0:T(8,128)(2,1)S(1)}, bf16[256,256]{1,0:T(8,128)(2,1)S(1)}, u32[]{:S(2)}, u32[]{:S(2)}) collective-permute-start(bf16[256,256]{1,0:T(8,128)(2,1)S(1)} %slice.41), channel_id=1, source_target_pairs={{0,224},{16,240},{32,0},{48,16},{64,32},{80,48},{96,64},{112,80},{... | collective-permute-start | bytes 393224 | tf_op jit(solution)/shard_map/ppermute | solution.py:330
  57.6 41.3 %copy-start.6 = (bf16[256,256]{1,0:T(8,128)(2,1)}, bf16[256,256]{1,0:T(8,128)(2,1)S(1)}, u32[]{:S(2)}) copy-start(bf16[256,256]{1,0:T(8,128)(2,1)S(1)} %collective-permute-done.1.refs_0_) | copy-start | bytes 393220
  57.6 13.5 %collective-permute-start.2 = (bf16[256,256]{1,0:T(8,128)(2,1)S(1)}, bf16[256,256]{1,0:T(8,128)(2,1)S(1)}, u32[]{:S(2)}, u32[]{:S(2)}) collective-permute-start(bf16[256,256]{1,0:T(8,128)(2,1)S(1)} %collective-permute-done.1.refs_0_), channel_id=1, source_target_pairs={{0,32},{16,48},{32,64},{48,80},{64,96},{80,112},{96,128},{112,144}... | collective-permute-start | bytes 393224 | tf_op jit(solution)/shard_map/ppermute | solution.py:328
  64.2 34.7 %copy-start.7 = (bf16[256,256]{1,0:T(8,128)(2,1)}, bf16[256,256]{1,0:T(8,128)(2,1)S(1)}, u32[]{:S(2)}) copy-start(bf16[256,256]{1,0:T(8,128)(2,1)S(1)} %collective-permute-done.5.refs_6_) | copy-start | bytes 393220
  64.2 14.5 %collective-permute-start.6 = (bf16[256,256]{1,0:T(8,128)(2,1)S(1)}, bf16[256,256]{1,0:T(8,128)(2,1)S(1)}, u32[]{:S(2)}, u32[]{:S(2)}) collective-permute-start(bf16[256,256]{1,0:T(8,128)(2,1)S(1)} %collective-permute-done.5.refs_6_), channel_id=1, source_target_pairs={{0,224},{16,240},{32,0},{48,16},{64,32},{80,48},{96,64},{112,80},{... | collective-permute-start | bytes 393224 | tf_op jit(solution)/shard_map/ppermute | solution.py:330
  71.1 27.9 %copy-start.8 = (bf16[256,256]{1,0:T(8,128)(2,1)}, bf16[256,256]{1,0:T(8,128)(2,1)S(1)}, u32[]{:S(2)}) copy-start(bf16[256,256]{1,0:T(8,128)(2,1)S(1)} %collective-permute-done.2.refs_1_) | copy-start | bytes 393220
  71.1 14.5 %collective-permute-start.3 = (bf16[256,256]{1,0:T(8,128)(2,1)S(1)}, bf16[256,256]{1,0:T(8,128)(2,1)S(1)}, u32[]{:S(2)}, u32[]{:S(2)}) collective-permute-start(bf16[256,256]{1,0:T(8,128)(2,1)S(1)} %collective-permute-done.2.refs_1_), channel_id=1, source_target_pairs={{0,32},{16,48},{32,64},{48,80},{64,96},{80,112},{96,128},{112,144}... | collective-permute-start | bytes 393224 | tf_op jit(solution)/shard_map/ppermute | solution.py:328
  78.8 20.2 %copy-start.9 = (bf16[256,256]{1,0:T(8,128)(2,1)}, bf16[256,256]{1,0:T(8,128)(2,1)S(1)}, u32[]{:S(2)}) copy-start(bf16[256,256]{1,0:T(8,128)(2,1)S(1)} %collective-permute-done.6.refs_5_) | copy-start | bytes 393220
  78.8 13.6 %collective-permute-start.7 = (bf16[256,256]{1,0:T(8,128)(2,1)S(1)}, bf16[256,256]{1,0:T(8,128)(2,1)S(1)}, u32[]{:S(2)}, u32[]{:S(2)}) collective-permute-start(bf16[256,256]{1,0:T(8,128)(2,1)S(1)} %collective-permute-done.6.refs_5_), channel_id=1, source_target_pairs={{0,224},{16,240},{32,0},{48,16},{64,32},{80,48},{96,64},{112,80},{... | collective-permute-start | bytes 393224 | tf_op jit(solution)/shard_map/ppermute | solution.py:330
  85.6 13.4 %copy-start.10 = (bf16[256,256]{1,0:T(8,128)(2,1)}, bf16[256,256]{1,0:T(8,128)(2,1)S(1)}, u32[]{:S(2)}) copy-start(bf16[256,256]{1,0:T(8,128)(2,1)S(1)} %collective-permute-done.3.refs_2_) | copy-start | bytes 393220
  85.6 13.3 %collective-permute-start.4 = (bf16[256,256]{1,0:T(8,128)(2,1)S(1)}, bf16[256,256]{1,0:T(8,128)(2,1)S(1)}, u32[]{:S(2)}, u32[]{:S(2)}) collective-permute-start(bf16[256,256]{1,0:T(8,128)(2,1)S(1)} %collective-permute-done.3.refs_2_), channel_id=1, source_target_pairs={{0,32},{16,48},{32,64},{48,80},{64,96},{80,112},{96,128},{112,144}... | collective-permute-start | bytes 393224 | tf_op jit(solution)/shard_map/ppermute | solution.py:328
  88.2 43.8 %copy-start.2 = (s32[3]{0:T(128)S(1)}, s32[3]{0:T(128)}, u32[]{:S(2)}) copy-start(s32[3]{0:T(128)} %pad_add_fusion.place_ref) | copy-start | bytes 40
  138.7 7.9 %copy-start.22 = (bf16[64,1024]{1,0:T(8,128)(2,1)S(1)}, bf16[64,1024]{1,0:T(8,128)(2,1)}, u32[]{:S(2)}) copy-start(bf16[64,1024]{1,0:T(8,128)(2,1)} %get-tuple-element.48) | copy-start | bytes 393220
  138.7 10.9 %copy-start.21 = (bf16[64,1024]{1,0:T(8,128)(2,1)S(1)}, bf16[64,1024]{1,0:T(8,128)(2,1)}, u32[]{:S(2)}) copy-start(bf16[64,1024]{1,0:T(8,128)(2,1)} %get-tuple-element.49) | copy-start | bytes 393220
  138.7 14.4 %copy-start.20 = (bf16[64,1024]{1,0:T(8,128)(2,1)S(1)}, bf16[64,1024]{1,0:T(8,128)(2,1)}, u32[]{:S(2)}) copy-start(bf16[64,1024]{1,0:T(8,128)(2,1)} %get-tuple-element.50) | copy-start | bytes 393220
  138.7 27.3 %copy-start.1 = (bf16[64,1024]{1,0:T(8,128)(2,1)S(1)}, bf16[64,1024]{1,0:T(8,128)(2,1)}, u32[]{:S(2)}) copy-start(bf16[64,1024]{1,0:T(8,128)(2,1)} %get-tuple-element.47.refs_0_) | copy-start | bytes 393220
  138.7 29.3 %all-to-all-start.2 = ((bf16[32,8,2048]{2,1,0:T(8,128)(2,1)}), bf16[32,8,2048]{2,1,0:T(8,128)(2,1)S(1)}, u32[]{:S(2)}, u32[]{:S(2)}) async-start(bf16[32,8,2048]{2,1,0:T(8,128)(2,1)} %bitcast.18), calls=%async_computation.3 | async-start | bytes 2097152 | tf_op jit(solution)/shard_map/all_to_all | solution.py:311
  146.6 13.7 %collective-permute-start.8 = (bf16[64,1024]{1,0:T(8,128)(2,1)S(1)}, bf16[64,1024]{1,0:T(8,128)(2,1)S(1)}, u32[]{:S(2)}, u32[]{:S(2)}) collective-permute-start(bf16[64,1024]{1,0:T(8,128)(2,1)S(1)} %copy-done.22), channel_id=1, source_target_pairs={{0,16},{16,0},{32,48},{48,32},{64,80},{80,64},{96,112},{112,96},{1... | collective-permute-start | bytes 393224 | tf_op jit(solution)/shard_map/ppermute | solution.py:208
  149.6 16.4 %collective-permute-start.9 = (bf16[64,1024]{1,0:T(8,128)(2,1)S(1)}, bf16[64,1024]{1,0:T(8,128)(2,1)S(1)}, u32[]{:S(2)}, u32[]{:S(2)}) collective-permute-start(bf16[64,1024]{1,0:T(8,128)(2,1)S(1)} %copy-done.21), channel_id=1, source_target_pairs={{0,256},{16,272},{32,288},{48,304},{64,320},{80,336},{96,352},{112... | collective-permute-start | bytes 393224 | tf_op jit(solution)/shard_map/ppermute | solution.py:208
  153.1 12.9 %collective-permute-start.10 = (bf16[64,1024]{1,0:T(8,128)(2,1)S(1)}, bf16[64,1024]{1,0:T(8,128)(2,1)S(1)}, u32[]{:S(2)}, u32[]{:S(2)}) collective-permute-start(bf16[64,1024]{1,0:T(8,128)(2,1)S(1)} %copy-done.20), channel_id=1, source_target_pairs={{0,272},{16,256},{32,304},{48,288},{64,336},{80,320},{96,368},{112... | collective-permute-start | bytes 393224 | tf_op jit(solution)/shard_map/ppermute | solution.py:208
  168.0 8.3 %all-to-all-start.3 = ((bf16[4,64,256]{2,1,0:T(8,128)(2,1)}), bf16[4,64,256]{2,1,0:T(8,128)(2,1)S(1)}, u32[]{:S(2)}, u32[]{:S(2)}) async-start(bf16[4,64,256]{2,1,0:T(8,128)(2,1)} %bitcast.48), calls=%async_computation.4 | async-start | bytes 262144 | tf_op jit(solution)/shard_map/all_to_all | solution.py:346
  (8 other events, 30.4 us)
Sparse Core Ops, SparseCore 0:
  34.9 97.1 all-gather.2
Sparse Core Ops, SparseCore 1:
  105.0 62.9 reduce-scatter.1
